TPU v7x, 256 devices: a whole 4x4x8 slice. The times are simulated.
256 devices in a mesh: gx: 32 (over z, x_hi, core), gz: 8 (over x_lo, y).
Axes of the slice: x: 4 (x_hi: 2, x_lo: 2; x = x_hi * 2 + x_lo), y: 4, z: 8, core: 2. Of those that a mesh axis runs over, the one named last changes fastest.
Arguments:
- residual: float32 [224, 112, 512], P('gx', 'gz'), may hold values from -3 to 3
- layer_heights: float32 [73], replicated, may hold values from 0.25 to 1
Outputs:
- correction: float32 [224, 112, 512], P('gx', 'gz')
All inputs are finite; a program needn't handle non-finite values.
Results may differ from a plain program's by a relative error of at most 0.0003.
Values sent between devices are 32-bit elements; how exact they have to be, the bound alone decides.
No kernel may reach another device: no remote copies, remote signals or barrier semaphores. Data moves between devices by JAX's collectives and lax.ppermute only.
A program may use at most 128 MiB of HBM per device.

v0:
```python
import jax
import jax.numpy as jnp
import numpy as np
from jax import lax
from jax.experimental import pallas as pl
from jax.experimental.pallas import tpu as pltpu
from jax.sharding import PartitionSpec as P


SMOOTH_STEPS = 3
COARSE_STEPS = 12
NX, NZ, NY = 32, 16, 73
DEVICES = 256
ROWS = 80
screen_shift = 0.02
smooth_floor = 0.1
coarse_floor = 0.01
HI = lax.Precision.HIGHEST
f32 = jnp.float32


def legendre_values(points, degree):
    columns = [np.ones(points.shape), points]
    for n in range(2, degree + 1):
        columns.append(((2 * n - 1) * points * columns[-1] - (n - 1) * columns[-2]) / n)
    return np.stack(columns[: degree + 1], axis=1)


def gll_tables(degree):
    nodes = -np.cos(np.pi * np.arange(degree + 1) / degree)
    for _ in range(100):
        values = legendre_values(nodes, degree)
        nodes = nodes - (nodes * values[:, degree] - values[:, degree - 1]) / (
            (degree + 1) * values[:, degree]
        )
    leading = legendre_values(nodes, degree)[:, degree]
    weights = 2.0 / (degree * (degree + 1) * leading**2)
    differ = np.zeros((degree + 1, degree + 1))
    for i in range(degree + 1):
        for j in range(degree + 1):
            if i != j:
                differ[i, j] = leading[i] / (leading[j] * (nodes[i] - nodes[j]))
    differ[0, 0] = -degree * (degree + 1) / 4.0
    differ[degree, degree] = degree * (degree + 1) / 4.0
    return nodes, weights, differ.T @ (weights[:, None] * differ)


def interp_table(fine_degree, coarse_degree):
    fine_nodes = gll_tables(fine_degree)[0]
    coarse_nodes = gll_tables(coarse_degree)[0]
    lagrange = np.ones((fine_degree + 1, coarse_degree + 1))
    for col in range(coarse_degree + 1):
        for other in range(coarse_degree + 1):
            if other != col:
                lagrange[:, col] *= (fine_nodes - coarse_nodes[other]) / (
                    coarse_nodes[col] - coarse_nodes[other]
                )
    return lagrange


def lanes_of(values):
    n = values.shape[0]
    out = np.zeros((8, 8))
    out[:n, :n] = values
    return out.reshape(64)


def square_of(matrix, n_out, n_in):
    out = np.zeros((8, 8, 8, 8))
    out[:n_out, :n_out, :n_in, :n_in] = matrix.reshape(n_out, n_out, n_in, n_in)
    return out.reshape(64, 64)


def quad(b00, b01, b10, b11):
    return np.block([[b00, b01], [b10, b11]])


class Level:
    def __init__(self, q):
        self.q = q
        _, w, s = gll_tables(q)
        self.w, self.s = w, s
        mass = 0.5 * w[:q].copy()
        mass[0] = 0.5 * (w[0] + w[q])
        diag = 2.0 * np.diag(s)[:q].copy()
        diag[0] = 2.0 * (s[0, 0] + s[q, q])
        self.mxz = np.outer(mass, mass)
        a = np.outer(diag, mass) + np.outer(mass, diag) + screen_shift * self.mxz
        self.ratio = lanes_of(a / self.mxz)
        spread = np.abs(s).sum(axis=1)
        self.bound = max(1.0, float(np.max(spread / np.diag(s))))
        base = 2.0 * s[:q, :q].copy()
        base[0, 0] += 2.0 * s[q, q]
        e1 = np.zeros((q, q))
        e1[:, 0] = 2.0 * s[:q, q]
        even, odd = e1 + e1.T, e1 - e1.T
        dm = np.diag(mass)
        zero = np.zeros((64, 64))
        scale = np.concatenate([lanes_of(1.0 / self.mxz)] * 2)[None, :]
        sq = lambda m: square_of(m, q, q)
        fixed = sq(np.kron(base, dm) + np.kron(dm, base) + screen_shift * np.kron(dm, dm))
        tables = [quad(fixed, zero, zero, fixed)]
        for c, n in (
            (np.kron(even, dm), np.kron(odd, dm)),
            (np.kron(dm, even), np.kron(dm, odd)),
        ):
            c, n = sq(c), sq(n)
            tables.append(quad(c, zero, zero, c))
            tables.append(quad(zero, -n, n, zero))
        self.tables = [t * scale for t in tables]
        self.mass_lanes = np.concatenate([lanes_of(self.mxz)] * 2)
        self.inv_mass_lanes = np.concatenate([lanes_of(1.0 / self.mxz)] * 2)
        self.ratio_lanes = np.concatenate([self.ratio] * 2)
        self.mask_lanes = (self.mass_lanes > 0).astype(np.float64)


def transfer_tables(fine, coarse):
    j = interp_table(fine, coarse)
    ja = j[:fine, :coarse]
    jb = np.zeros((fine, coarse))
    jb[:, 0] = j[:fine, coarse]
    zero = np.zeros((64, 64))
    sq = lambda m: square_of(m, fine, coarse)
    flat = sq(np.kron(ja, ja))
    tables = [quad(flat, zero, zero, flat)]
    for b in (np.kron(jb, ja), np.kron(ja, jb), np.kron(jb, jb)):
        b = sq(b)
        tables.append(quad(b, zero, zero, b))
        tables.append(quad(zero, -b, b, zero))
    return j, tables


def mode_list():
    special = [((0, 0), (16, 0)), ((0, 8), (16, 8))]
    seen = {k for pair in special for k in pair}
    modes = list(special)
    for kx in range(NX):
        for kz in range(NZ):
            if (kx, kz) not in seen:
                seen.add((kx, kz))
                seen.add(((-kx) % NX, (-kz) % NZ))
                modes.append(((kx, kz), None))
    assert len(modes) == DEVICES
    return modes


def fourier_tables():
    x, z = np.meshgrid(np.arange(NX), np.arange(NZ), indexing="ij")
    x, z = x.reshape(-1), z.reshape(-1)
    forward = np.zeros((2 * DEVICES, NX * NZ))
    backward = np.zeros((NX * NZ, 2 * DEVICES))
    scalars = np.zeros((DEVICES, 16))
    total = NX * NZ
    for m, (first, second) in enumerate(mode_list()):
        tx = 2 * np.pi * first[0] / NX
        tz = 2 * np.pi * first[1] / NZ
        phi = tx * x + tz * z
        forward[2 * m] = np.cos(phi)
        if second is None:
            forward[2 * m + 1] = -np.sin(phi)
            backward[:, 2 * m] = 2.0 / total * np.cos(phi)
            backward[:, 2 * m + 1] = -2.0 / total * np.sin(phi)
            for n, t in enumerate((tx, tz, tx + tz)):
                scalars[m, 3 * n : 3 * n + 3] = np.cos(t), np.cos(t), np.sin(t)
        else:
            ux = 2 * np.pi * second[0] / NX
            uz = 2 * np.pi * second[1] / NZ
            psi = ux * x + uz * z
            forward[2 * m + 1] = np.cos(psi)
            backward[:, 2 * m] = 1.0 / total * np.cos(phi)
            backward[:, 2 * m + 1] = 1.0 / total * np.cos(psi)
            for n, (t, u) in enumerate(((tx, ux), (tz, uz), (tx + tz, ux + uz))):
                scalars[m, 3 * n : 3 * n + 3] = np.cos(t), np.cos(u), 0.0
    return forward, backward, scalars


FINE, MID, LOW = Level(7), Level(3), Level(1)
J7, P7_TABLES = transfer_tables(7, 3)
J3, P3_TABLES = transfer_tables(3, 1)
FORWARD, BACKWARD, SCALARS = fourier_tables()
MATRICES = np.stack(FINE.tables + MID.tables + P7_TABLES + P3_TABLES).astype(np.float32)
G7_AT, G3_AT, P7_AT, P3_AT = 0, 5, 10, 17
LANES = np.zeros((16, 128))
for n, level in enumerate((FINE, MID)):
    LANES[4 * n] = level.mass_lanes
    LANES[4 * n + 1] = level.inv_mass_lanes
    LANES[4 * n + 2] = level.ratio_lanes
    LANES[4 * n + 3] = level.mask_lanes
LANES[8] = LOW.mask_lanes
LANES = LANES.astype(np.float32)


def cheb_steps(bound, sweeps, floor):
    centre = bound * (1.0 + floor) / 2.0
    half = bound * (1.0 - floor) / 2.0
    s = centre / half
    p = 1.0 / s
    steps = []
    for _ in range(sweeps - 1):
        p_next = 1.0 / (2.0 * s - p)
        steps.append((p_next * p, 2.0 * p_next / half))
        p = p_next
    return 1.0 / centre, steps


def pack_kernel(x_ref, o_ref, m_ref):
    m_ref[...] = jnp.zeros_like(m_ref)
    for e in range(2):
        for h in range(2):
            for a in range(7):
                r = e * 128 + h * 64 + a * 8
                m_ref[r : r + 7, :] = x_ref[a, e * 7 : e * 7 + 7, h * 256 : h * 256 + 256]
    for e in range(2):
        o_ref[pl.ds(e, 256, stride=2), :] = m_ref[e * 128 : e * 128 + 128, :].T


def unpack_kernel(x_ref, o_ref):
    for e in range(2):
        m = x_ref[pl.ds(e, 256, stride=2), :].T
        for h in range(2):
            for a in range(7):
                r = h * 64 + a * 8
                o_ref[a, e * 7 : e * 7 + 7, h * 256 : h * 256 + 256] = m[r : r + 7, :]


def dft_kernel(f_ref, x_ref, o_ref):
    o_ref[...] = jnp.dot(f_ref[...], x_ref[...], precision=HI, preferred_element_type=f32)


def roll_up(v):
    return pltpu.roll(v, ROWS - 1, axis=0)


def roll_down(v):
    return pltpu.roll(v, 1, axis=0)


def wall_apply(s, q, planes, g):
    parts = [g * p for p in planes] + [g * roll_up(planes[0])]
    n = q + 1
    half = n // 2
    even = [parts[l] + parts[q - l] for l in range(half)]
    odd = [parts[l] - parts[q - l] for l in range(half)]
    out = [None] * n
    for k in range(half):
        p = m = None
        for l in range(half):
            ce = 0.5 * (s[k, l] + s[k, q - l])
            co = 0.5 * (s[k, l] - s[k, q - l])
            te, to = float(ce) * even[l], float(co) * odd[l]
            p = te if p is None else p + te
            m = to if m is None else m + to
        out[k] = p + m
        out[q - k] = p - m
    out[0] = out[0] + roll_down(out[q])
    return out[:q]


def weighted_sum(coefs, planes):
    total = None
    for c, v in zip(coefs, planes):
        c = float(c)
        if c == 0.0:
            continue
        t = v if c == 1.0 else c * v
        total = t if total is None else total + t
    return total


def restrict_wall(j, fine, coarse, planes):
    out = [weighted_sum(j[:fine, c], planes) for c in range(coarse)]
    out[0] = out[0] + roll_down(weighted_sum(j[:fine, coarse], planes))
    return out


def prolong_wall(j, fine, coarse, planes):
    closed = list(planes) + [roll_up(planes[0])]
    return [weighted_sum(j[k], closed) for k in range(fine)]


def cycle_kernel(
    idx_ref, scal_ref, h_ref, lanes_ref, mats_ref, in_ref, out_ref,
    w_ref, hrow_ref, geo_ref,
    u7, r7, x7, d7, u3, r3, x3, d3,
    g7_ref, g3_ref, p7_ref, p3_ref,
):
    base = idx_ref[0] * 16
    sc = [scal_ref[base + n] for n in range(9)]
    lane = lax.broadcasted_iota(jnp.int32, (1, 128), 1)
    first = lane < 64

    cosines = [jnp.where(first, sc[3 * n], sc[3 * n + 1]) for n in range(3)]
    sines = [sc[3 * n + 2] for n in range(3)]
    for ref, at, phases in ((g7_ref, G7_AT, 2), (g3_ref, G3_AT, 2), (p7_ref, P7_AT, 3), (p3_ref, P3_AT, 3)):
        total = mats_ref[at]
        for n in range(phases):
            total = total + cosines[n] * mats_ref[at + 1 + 2 * n]
            total = total + sines[n] * mats_ref[at + 2 + 2 * n]
        ref[...] = total

    hrow_ref[...] = jnp.zeros_like(hrow_ref)
    hrow_ref[0:1, 0:NY] = h_ref[...]
    h = jnp.broadcast_to(hrow_ref[0:1, :], (128, 128)).T[:ROWS]
    row = lax.broadcasted_iota(jnp.int32, (ROWS, 128), 0)
    g = jnp.where(row < NY, 2.0 / jnp.where(row < NY, h, 1.0), 0.0)
    h_pair = h + roll_down(h)
    g_pair = g + roll_down(g)
    geo_ref[0] = h
    geo_ref[1] = g
    geo_ref[2] = h_pair

    def wall_mass(level, k):
        if k == 0:
            return (0.5 * float(level.w[0])) * geo_ref[2]
        return (0.5 * float(level.w[k])) * geo_ref[0]

    def inverse_diag(level, ratio, mask, k):
        s = level.s
        dy = float(s[0, 0]) * g_pair if k == 0 else float(s[k, k]) * g
        d = wall_mass(level, k) * ratio + dy
        return jnp.where(d > 0.0, mask / jnp.where(d > 0.0, d, 1.0), 0.0)

    mass7, inv7, ratio7, mask7 = (lanes_ref[n : n + 1, :] for n in range(4))
    mass3, inv3, ratio3, mask3 = (lanes_ref[n : n + 1, :] for n in range(4, 8))
    mask1 = lanes_ref[8:9, :]
    for k in range(7):
        d7[k] = inverse_diag(FINE, ratio7, mask7, k)
    for k in range(3):
        d3[k] = inverse_diag(MID, ratio3, mask3, k)
    d1_mix = (
        jnp.where(first, 2.0 - 2.0 * sc[0], 2.0 - 2.0 * sc[1])
        + jnp.where(first, 2.0 - 2.0 * sc[3], 2.0 - 2.0 * sc[4])
        + screen_shift
    ) * mask1
    d1 = inverse_diag(LOW, 4.0 + screen_shift, mask1, 0)

    re = in_ref[pl.ds(0, 256, stride=2), :]
    im = in_ref[pl.ds(1, 256, stride=2), :]
    w_ref[0:256, :] = jnp.where(first, re, pltpu.roll(im, 64, axis=1)) * inv7
    w_ref[256:512, :] = jnp.where(first, pltpu.roll(re, 64, axis=1), im) * inv7
    w_ref[512:, :] = jnp.zeros((w_ref.shape[0] - 512, 128), f32)
    for k in range(7):
        r7[k] = w_ref[pl.ds(k, ROWS, stride=7), :]

    def apply(level, u, table):
        q = level.q
        flat = u[...].reshape(q * ROWS, 128)
        m = jnp.dot(flat, table[...], precision=HI, preferred_element_type=f32)
        wall = wall_apply(level.s, q, [u[k] for k in range(q)], geo_ref[1])
        return [wall_mass(level, k) * m[k * ROWS : (k + 1) * ROWS] + wall[k] for k in range(q)]

    def smooth(level, u, r, x, d, table, fresh, keep_residual):
        q = level.q
        start, steps = cheb_steps(level.bound, SMOOTH_STEPS, smooth_floor)
        for k in range(q):
            t = start * (d[k] * r[k])
            u[k] = t
            x[k] = t if fresh else x[k] + t
        for alpha, beta in steps:
            au = apply(level, u, table)
            for k in range(q):
                t = r[k] - au[k]
                r[k] = t
                t = alpha * u[k] + beta * (d[k] * t)
                u[k] = t
                x[k] = x[k] + t
        if keep_residual:
            au = apply(level, u, table)
            for k in range(q):
                r[k] = r[k] - au[k]

    def restrict_lanes(planes, table, mass):
        flat = jnp.concatenate([p * mass for p in planes], axis=0)
        m = jnp.dot(flat, table[...], precision=HI, preferred_element_type=f32)
        return [m[k * ROWS : (k + 1) * ROWS] for k in range(len(planes))]

    def prolong_lanes(planes, table):
        flat = jnp.concatenate(planes, axis=0)
        m = lax.dot_general(
            flat, table[...], (((1,), (1,)), ((), ())), precision=HI, preferred_element_type=f32
        )
        return [m[k * ROWS : (k + 1) * ROWS] for k in range(len(planes))]

    smooth(FINE, u7, r7, x7, d7, g7_ref, True, True)
    down = restrict_wall(J7, 7, 3, [r7[k] for k in range(7)])
    down = restrict_lanes(down, p7_ref, mass7)
    for k in range(3):
        r3[k] = down[k] * inv3

    smooth(MID, u3, r3, x3, d3, g3_ref, True, True)
    down = restrict_wall(J3, 3, 1, [r3[k] for k in range(3)])
    r1 = restrict_lanes(down, p3_ref, mass3)[0]

    start, steps = cheb_steps(LOW.bound, COARSE_STEPS, coarse_floor)
    my1 = wall_mass(LOW, 0) * d1_mix
    u1 = start * (d1 * r1)
    x1 = u1
    for alpha, beta in steps:
        flow = (0.5 * g) * (u1 - roll_up(u1))
        r1 = r1 - (my1 * u1 + (flow - roll_down(flow)))
        u1 = alpha * u1 + beta * (d1 * r1)
        x1 = x1 + u1

    up = prolong_wall(J3, 3, 1, prolong_lanes([x1], p3_ref))
    for k in range(3):
        u3[k] = up[k]
        x3[k] = x3[k] + up[k]
    au = apply(MID, u3, g3_ref)
    for k in range(3):
        r3[k] = r3[k] - au[k]
    smooth(MID, u3, r3, x3, d3, g3_ref, False, False)

    up = prolong_wall(J7, 7, 3, prolong_lanes([x3[k] for k in range(3)], p7_ref))
    for k in range(7):
        u7[k] = up[k]
        x7[k] = x7[k] + up[k]
    au = apply(FINE, u7, g7_ref)
    for k in range(7):
        r7[k] = r7[k] - au[k]
    smooth(FINE, u7, r7, x7, d7, g7_ref, False, False)

    for k in range(7):
        w_ref[pl.ds(k, ROWS, stride=7), :] = x7[k]
    top = w_ref[0:256, :]
    low = w_ref[256:512, :]
    out_ref[pl.ds(0, 256, stride=2), :] = jnp.where(first, top, pltpu.roll(low, 64, axis=1))
    out_ref[pl.ds(1, 256, stride=2), :] = jnp.where(first, pltpu.roll(top, 64, axis=1), low)


VMEM = pl.BlockSpec(memory_space=pltpu.VMEM)
SMEM = pl.BlockSpec(memory_space=pltpu.SMEM)
PARAMS = pltpu.CompilerParams(vmem_limit_bytes=32 * 1024 * 1024)
FLAT = jax.ShapeDtypeStruct((512, 128), f32)


def exchange(block):
    moved = lax.all_to_all(block.reshape(DEVICES, 2, 128), ("gx", "gz"), 0, 0)
    return moved.reshape(512, 128)


def transform(table, block):
    return pl.pallas_call(
        dft_kernel, out_shape=FLAT, in_specs=[VMEM, VMEM], out_specs=VMEM, compiler_params=PARAMS
    )(jnp.asarray(table, f32), block)


def body(residual, layer_heights):
    packed = pl.pallas_call(
        pack_kernel, out_shape=FLAT, in_specs=[VMEM], out_specs=VMEM,
        scratch_shapes=[pltpu.VMEM((256, 256), f32)], compiler_params=PARAMS,
    )(residual)
    modes = exchange(transform(FORWARD, exchange(packed)))
    place = lax.axis_index("gx") * 8 + lax.axis_index("gz")
    fine = pltpu.VMEM((7, ROWS, 128), f32)
    mid = pltpu.VMEM((3, ROWS, 128), f32)
    square = pltpu.VMEM((128, 128), f32)
    solved = pl.pallas_call(
        cycle_kernel, out_shape=FLAT,
        in_specs=[SMEM, SMEM, VMEM, VMEM, VMEM, VMEM], out_specs=VMEM,
        scratch_shapes=[
            pltpu.VMEM((7 * ROWS, 128), f32), pltpu.VMEM((8, 128), f32),
            pltpu.VMEM((3, ROWS, 128), f32),
            fine, fine, fine, fine, mid, mid, mid, mid,
            square, square, square, square,
        ],
        compiler_params=PARAMS,
    )(
        place.astype(jnp.int32).reshape(1),
        jnp.asarray(SCALARS.reshape(-1), f32),
        layer_heights.reshape(1, NY),
        jnp.asarray(LANES),
        jnp.asarray(MATRICES),
        modes,
    )
    spread = exchange(transform(BACKWARD, exchange(solved)))
    return pl.pallas_call(
        unpack_kernel, out_shape=jax.ShapeDtypeStruct((7, 14, 512), f32),
        in_specs=[VMEM], out_specs=VMEM, compiler_params=PARAMS,
    )(spread)


def solution(mesh):
    return jax.shard_map(
        body,
        mesh=mesh,
        in_specs=(P("gx", "gz", None), P()),
        out_specs=P("gx", "gz", None),
        check_vma=False,
    )
```

profile of v0, /device:TPU:1, one launch (start us, length us, event | category | flops | bytes accessed | tf_op | source)
XLA Modules:
  0.0 106.2 jit_solution(5123708925434116008)
XLA Ops:
  0.0 0.0 copy-start
  0.0 0.0 copy-start.3
  0.0 1.1 copy-done.3
  1.1 0.1 shard_map.73
  1.2 30.3 %all_to_all.20 = f32[256,2,128]{2,1,0:T(2,128)S(1)} all-to-all(f32[256,2,128]{2,1,0:T(2,128)S(1)} %bitcast.11), channel_id=1, replica_groups=mesh['gx'=32,'gz'=8] {'gx','gz'}, dimensions={0} | all-to-all | bytes 524288 | tf_op jit(solution)/shard_map/all_to_all | solution.py:437
  31.5 0.0 copy-start.2
  31.5 1.2 %copy-done.2 = f32[512,512]{1,0:T(8,128)S(1)} copy-done((f32[512,512]{1,0:T(8,128)S(1)}, f32[512,512]{1,0:T(8,128)}, u32[]{:S(2)}) %copy-start.2) | copy-done | bytes 1048600
  32.8 0.0 copy-start.4
  32.8 0.0 copy-start.5
  32.8 0.0 copy-start.6
  32.8 1.7 %shard_map.74 = f32[512,128]{1,0:T(8,128)} custom-call(f32[512,512]{1,0:T(8,128)S(1)} %copy-done.2, f32[512,128]{1,0:T(8,128)S(1)} %bitcast.12), custom_call_target="tpu_custom_call" | custom-call | tf_op jit(solution)/shard_map/pallas_call | solution.py:442
  34.5 0.0 copy-start.1
  34.5 6.0 %all-to-all-start.1 = ((f32[256,2,128]{2,1,0:T(2,128)}), f32[256,2,128]{2,1,0:T(2,128)S(1)}, u32[]{:S(2)}, u32[]{:S(2)}) async-start(f32[256,2,128]{2,1,0:T(2,128)} %bitcast.4), calls=%async_computation.1 | async-start | bytes 524288 | tf_op jit(solution)/shard_map/all_to_all | solution.py:437
  40.5 14.9 %all-to-all-done.1 = f32[256,2,128]{2,1,0:T(2,128)S(1)} async-done(((f32[256,2,128]{2,1,0:T(2,128)}), f32[256,2,128]{2,1,0:T(2,128)S(1)}, u32[]{:S(2)}, u32[]{:S(2)}) %all-to-all-start.1) | async-done | bytes 262176 | tf_op jit(solution)/shard_map/all_to_all | solution.py:437
  55.4 0.0 copy-done
  55.4 0.0 copy-done.4
  55.4 0.0 copy-done.5
  55.4 0.0 copy-done.6
  55.4 7.8 %shard_map.75 = f32[512,128]{1,0:T(8,128)S(1)} custom-call(s32[1]{0:T(128)} %bitcast.idx_ref, f32[4096]{0:T(1024)S(1)} %copy-done.4, f32[1,73]{1,0:T(1,128)S(1)} %bitcast.17, f32[16,128]{1,0:T(8,128)S(1)} %copy-done.5, f32[24,128,128]{2,1,0:T(8,128)S(1)} %copy-done, f32[512,128]{1,0:T(8,128)S(1)} %bitcast.15), custom_call_target="tpu_custom_call" | custom-call | tf_op jit(solution)/shard_map/pallas_call | solution.py:457
  63.2 20.6 %all_to_all.21 = f32[256,2,128]{2,1,0:T(2,128)S(1)} all-to-all(f32[256,2,128]{2,1,0:T(2,128)S(1)} %bitcast.16), channel_id=1, replica_groups=mesh['gx'=32,'gz'=8] {'gx','gz'}, dimensions={0} | all-to-all | bytes 524288 | tf_op jit(solution)/shard_map/all_to_all | solution.py:437
  83.9 0.0 copy-done.1
  83.9 1.0 shard_map.76
  84.9 20.5 %all_to_all.22 = f32[256,2,128]{2,1,0:T(2,128)S(1)} all-to-all(f32[256,2,128]{2,1,0:T(2,128)S(1)} %bitcast.14), channel_id=1, replica_groups=mesh['gx'=32,'gz'=8] {'gx','gz'}, dimensions={0} | all-to-all | bytes 524288 | tf_op jit(solution)/shard_map/all_to_all | solution.py:437
  105.4 0.8 shard_map.77
Async XLA Ops:
  0.0 55.4 %copy-start = (f32[24,128,128]{2,1,0:T(8,128)S(1)}, f32[24,128,128]{2,1,0:T(8,128)}, u32[]{:S(2)}) copy-start(f32[24,128,128]{2,1,0:T(8,128)} %constant.24.clone.mats_ref) | copy-start | bytes 4718596
  0.0 1.1 copy-start.3
  31.5 1.2 %copy-start.2 = (f32[512,512]{1,0:T(8,128)S(1)}, f32[512,512]{1,0:T(8,128)}, u32[]{:S(2)}) copy-start(f32[512,512]{1,0:T(8,128)} %constant.21.clone.f_ref) | copy-start | bytes 3145732
  32.8 22.6 %copy-start.4 = (f32[4096]{0:T(1024)S(1)}, f32[4096]{0:T(1024)}, u32[]{:S(2)}) copy-start(f32[4096]{0:T(1024)} %constant.22.clone.scal_ref) | copy-start | bytes 49156
  32.8 22.6 %copy-start.5 = (f32[16,128]{1,0:T(8,128)S(1)}, f32[16,128]{1,0:T(8,128)}, u32[]{:S(2)}) copy-start(f32[16,128]{1,0:T(8,128)} %constant.23.clone.lanes_ref) | copy-start | bytes 24580
  32.8 22.6 %copy-start.6 = (f32[73]{0:T(128)S(1)}, f32[73]{0:T(128)}, u32[]{:S(2)}) copy-start(f32[73]{0:T(128)} %param.8) | copy-start | bytes 880
  34.5 49.4 %copy-start.1 = (f32[512,512]{1,0:T(8,128)S(1)}, f32[512,512]{1,0:T(8,128)}, u32[]{:S(2)}) copy-start(f32[512,512]{1,0:T(8,128)} %constant.25.clone.f_ref) | copy-start | bytes 3145732
  34.5 20.9 %all-to-all-start.1 = ((f32[256,2,128]{2,1,0:T(2,128)}), f32[256,2,128]{2,1,0:T(2,128)S(1)}, u32[]{:S(2)}, u32[]{:S(2)}) async-start(f32[256,2,128]{2,1,0:T(2,128)} %bitcast.4), calls=%async_computation.1 | async-start | bytes 524288 | tf_op jit(solution)/shard_map/all_to_all | solution.py:437
where the time goes:
time: 107 us; the launch traced here: 106 us
  blocking collectives  71.5 us (67%)
  waiting for transfers between devices  14.9 us (14%)
  Pallas kernels  11.5 us (11%)
  starting transfers between devices  5.97 us (6%)
  local copies, waits for them, and re-layouts  2.3 us (2%)
    all_to_all x3, blocking collectives, exchange(): moved = lax.all_to_all(block.reshape(DEVICES, 2, 128), ('gx', 'gz'), 0, 0)  71.5 us
    all_to_all x1, waiting for transfers between devices, exchange(): moved = lax.all_to_all(block.reshape(DEVICES, 2, 128), ('gx', 'gz'), 0, 0)  14.9 us
    pallas_call x1, Pallas kernels, body(): pl.pallas_call(cycle_kernel, out_shape=FLAT, in_specs=[SMEM, SMEM, VMEM,...  7.83 us
    all_to_all x1, starting transfers between devices, exchange(): moved = lax.all_to_all(block.reshape(DEVICES, 2, 128), ('gx', 'gz'), 0, 0)  5.97 us
    pallas_call x2, Pallas kernels, transform(): pl.pallas_call(dft_kernel, out_shape=FLAT, in_specs=[VMEM, VMEM], out_spe...  2.75 us
    unnamed x14, local copies, waits for them, and re-layouts  2.3 us
  transfers between devices with their start and end apart: 1, of which 1 were waited for; matrix products, arithmetic and copies ran while one was open for 0% of the time, Pallas kernels for 0%

commit v1 on v0

v1 whole, which is shorter than its diff:
```python
import jax
import jax.numpy as jnp
import ml_dtypes
import numpy as np
from jax import lax
from jax.experimental import pallas as pl
from jax.experimental.pallas import tpu as pltpu
from jax.sharding import PartitionSpec as P


SMOOTH_STEPS = 3
COARSE_STEPS = 12
NX, NZ, NY = 32, 16, 73
DEVICES = 256
ROWS = 80
screen_shift = 0.02
smooth_floor = 0.1
coarse_floor = 0.01
f32 = jnp.float32
bf16 = jnp.bfloat16


def legendre_values(points, degree):
    columns = [np.ones(points.shape), points]
    for n in range(2, degree + 1):
        columns.append(((2 * n - 1) * points * columns[-1] - (n - 1) * columns[-2]) / n)
    return np.stack(columns[: degree + 1], axis=1)


def gll_tables(degree):
    nodes = -np.cos(np.pi * np.arange(degree + 1) / degree)
    for _ in range(100):
        values = legendre_values(nodes, degree)
        nodes = nodes - (nodes * values[:, degree] - values[:, degree - 1]) / (
            (degree + 1) * values[:, degree]
        )
    leading = legendre_values(nodes, degree)[:, degree]
    weights = 2.0 / (degree * (degree + 1) * leading**2)
    differ = np.zeros((degree + 1, degree + 1))
    for i in range(degree + 1):
        for j in range(degree + 1):
            if i != j:
                differ[i, j] = leading[i] / (leading[j] * (nodes[i] - nodes[j]))
    differ[0, 0] = -degree * (degree + 1) / 4.0
    differ[degree, degree] = degree * (degree + 1) / 4.0
    return nodes, weights, differ.T @ (weights[:, None] * differ)


def interp_table(fine_degree, coarse_degree):
    fine_nodes = gll_tables(fine_degree)[0]
    coarse_nodes = gll_tables(coarse_degree)[0]
    lagrange = np.ones((fine_degree + 1, coarse_degree + 1))
    for col in range(coarse_degree + 1):
        for other in range(coarse_degree + 1):
            if other != col:
                lagrange[:, col] *= (fine_nodes - coarse_nodes[other]) / (
                    coarse_nodes[col] - coarse_nodes[other]
                )
    return lagrange


def lanes_of(values):
    n = values.shape[0]
    out = np.zeros((8, 8))
    out[:n, :n] = values
    return out.reshape(64)


def square_of(matrix, n_out, n_in):
    out = np.zeros((8, 8, 8, 8))
    out[:n_out, :n_out, :n_in, :n_in] = matrix.reshape(n_out, n_out, n_in, n_in)
    return out.reshape(64, 64)


class Level:
    def __init__(self, q):
        self.q = q
        _, w, s = gll_tables(q)
        self.w, self.s = w, s
        mass = 0.5 * w[:q].copy()
        mass[0] = 0.5 * (w[0] + w[q])
        diag = 2.0 * np.diag(s)[:q].copy()
        diag[0] = 2.0 * (s[0, 0] + s[q, q])
        self.mxz = np.outer(mass, mass)
        a = np.outer(diag, mass) + np.outer(mass, diag) + screen_shift * self.mxz
        self.ratio = lanes_of(a / self.mxz)
        spread = np.abs(s).sum(axis=1)
        self.bound = max(1.0, float(np.max(spread / np.diag(s))))
        base = 2.0 * s[:q, :q].copy()
        base[0, 0] += 2.0 * s[q, q]
        e1 = np.zeros((q, q))
        e1[:, 0] = 2.0 * s[:q, q]
        even, odd = e1 + e1.T, e1 - e1.T
        dm = np.diag(mass)
        scale = np.concatenate([lanes_of(1.0 / self.mxz)] * 2)[None, :]
        sq = lambda m: square_of(m, q, q)
        fixed = sq(np.kron(base, dm) + np.kron(dm, base) + screen_shift * np.kron(dm, dm))
        tables = [np.hstack([fixed, 0.0 * fixed])]
        for c, n in (
            (np.kron(even, dm), np.kron(odd, dm)),
            (np.kron(dm, even), np.kron(dm, odd)),
        ):
            tables.append(np.hstack([sq(c), -sq(n)]))
        self.tables = [(t * scale)[: 64 if q > 3 else 24] for t in tables]
        self.weight = 0.5 * w
        self.stiff = s / self.weight[:, None]
        self.mass_lanes = np.concatenate([lanes_of(self.mxz)] * 2)
        self.inv_mass_lanes = np.concatenate([lanes_of(1.0 / self.mxz)] * 2)
        self.ratio_lanes = np.concatenate([self.ratio] * 2)
        self.mask_lanes = (self.mass_lanes > 0).astype(np.float64)


def transfer_tables(fine, coarse):
    j = interp_table(fine, coarse)
    ja = j[:fine, :coarse]
    jb = np.zeros((fine, coarse))
    jb[:, 0] = j[:fine, coarse]
    tables = []
    for n, b in enumerate((np.kron(ja, ja), np.kron(jb, ja), np.kron(ja, jb), np.kron(jb, jb))):
        b = square_of(b, fine, coarse).T[: 24 if coarse > 1 else 8]
        tables.append(np.hstack([b, b if n else 0.0 * b]))
    return j, tables


def flow_tables():
    x = np.arange(NX)
    forward = np.zeros((2, 2 * NX, 2 * NX))
    backward = np.zeros((2, 2 * NX, 2 * NX))
    phases = np.zeros((152, 2, 64))
    re, im = slice(0, NX), slice(NX, 2 * NX)
    for n in range(NX):
        c, s = np.cos(2 * np.pi * n * x / NX), np.sin(2 * np.pi * n * x / NX)
        forward[1, 2 * n, re], forward[1, 2 * n, im] = c, s
        forward[1, 2 * n + 1, re], forward[1, 2 * n + 1, im] = -s, c
        backward[1, re, 2 * n], backward[1, re, 2 * n + 1] = c / NX, -s / NX
        backward[1, im, 2 * n], backward[1, im, 2 * n + 1] = s / NX, c / NX
        t = 2 * np.pi * n / NX
        phases[64 + 2 * n], phases[65 + 2 * n] = np.cos(t), np.sin(t)
    for half in range(2):
        part = slice(half * NX, half * NX + NX)
        for k in range(16):
            n = 16 * half + k
            if k:
                c, s = np.cos(2 * np.pi * k * x / NX), np.sin(2 * np.pi * k * x / NX)
                forward[0, 2 * n, part], forward[0, 2 * n + 1, part] = c, -s
                backward[0, part, 2 * n] = 2 * c / NX
                backward[0, part, 2 * n + 1] = -2 * s / NX
                t = 2 * np.pi * k / NX
                phases[2 * n], phases[2 * n + 1] = np.cos(t), np.sin(t)
            else:
                one, turn = np.ones(NX), np.cos(np.pi * x)
                forward[0, 2 * n, part], forward[0, 2 * n + 1, part] = one, turn
                backward[0, part, 2 * n], backward[0, part, 2 * n + 1] = one / NX, turn / NX
                phases[2 * n, 0], phases[2 * n, 1] = 1.0, -1.0
    for b in range(9):
        t = 2 * np.pi * b / NZ
        phases[128 + 2 * b], phases[129 + 2 * b] = np.cos(t), np.sin(t) if b % 8 else 0.0
    return forward, backward, phases.reshape(152, 128)


FINE, MID, LOW = Level(7), Level(3), Level(1)
J7, P7_TABLES = transfer_tables(7, 3)
J3, P3_TABLES = transfer_tables(3, 1)
FORWARD, BACKWARD, PHASES = flow_tables()
MATRICES = np.concatenate(FINE.tables + MID.tables + P7_TABLES + P3_TABLES).astype(np.float32)
R7 = FINE.weight[:, None] * J7 / MID.weight
R3 = MID.weight[:, None] * J3 / LOW.weight
G7_AT, G3_AT, P7_AT, P3_AT = 0, 192, 264, 360


def split_terms(tables):
    high = tables.astype(np.float32).astype(ml_dtypes.bfloat16)
    low = (tables - high.astype(np.float64)).astype(ml_dtypes.bfloat16)
    rows = np.concatenate([high, high, low], axis=2).reshape(4 * NX, 6 * NX)
    return np.concatenate([rows, np.zeros((4 * NX, 2 * NX), rows.dtype)], axis=1)


LANES = np.zeros((16, 128))
for n, level in enumerate((FINE, MID)):
    LANES[4 * n] = level.mass_lanes
    LANES[4 * n + 1] = level.inv_mass_lanes
    LANES[4 * n + 2] = level.ratio_lanes
    LANES[4 * n + 3] = level.mask_lanes
LANES[8] = LOW.mask_lanes
MATRICES = np.concatenate([MATRICES, LANES, PHASES]).astype(np.float32)
LANES_AT, PHASES_AT = 392, 408


def cheb_steps(bound, sweeps, floor):
    centre = bound * (1.0 + floor) / 2.0
    half = bound * (1.0 - floor) / 2.0
    s = centre / half
    p = 1.0 / s
    steps = []
    for _ in range(sweeps - 1):
        p_next = 1.0 / (2.0 * s - p)
        steps.append((p_next * p, 2.0 * p_next / half))
        p = p_next
    return 1.0 / centre, steps


def pack_kernel(x_ref, h_ref, o_ref, rows_ref, m_ref, line_ref):
    m_ref[...] = jnp.zeros_like(m_ref)
    for e in range(2):
        for h in range(2):
            for a in range(7):
                r = e * 128 + h * 64 + a * 8
                m_ref[r : r + 7, :] = x_ref[a, e * 7 : e * 7 + 7, h * 256 : h * 256 + 256]
    for e in range(2):
        o_ref[pl.ds(e, 256, stride=2), :] = m_ref[e * 128 : e * 128 + 128, :].T
    line_ref[...] = jnp.zeros_like(line_ref)
    line_ref[0:1, 0:NY] = h_ref[...]
    rows_ref[...] = jnp.broadcast_to(line_ref[0:1, :], (128, 128)).T[:ROWS]


def unpack_kernel(x_ref, o_ref):
    for e in range(2):
        m = x_ref[pl.ds(e, 256, stride=2), :].T
        for h in range(2):
            for a in range(7):
                r = h * 64 + a * 8
                o_ref[a, e * 7 : e * 7 + 7, h * 256 : h * 256 + 256] = m[r : r + 7, :]


def halves(v):
    high = v.astype(bf16)
    return high, (v - high.astype(f32)).astype(bf16)


def dot(a, b):
    return jnp.dot(a, b, preferred_element_type=f32)


def combine(pairs):
    total = None
    for c, v in pairs:
        c = float(c)
        if abs(c) < 1e-12:
            continue
        if abs(abs(c) - 1.0) < 1e-12:
            t = v
            if total is None:
                total = v if c > 0 else -v
            else:
                total = total + v if c > 0 else total - v
            continue
        t = c * v
        total = t if total is None else total + t
    return total


def flow_product(f_ref, which, rows):
    v = jnp.concatenate(rows, axis=1)
    high, low = halves(v)
    t = f_ref[which * 64 : which * 64 + 64, :][:, :192]
    return dot(t, jnp.concatenate([high, low, high], axis=0))


def forward_kernel(f_ref, x_ref, o_ref):
    v = [x_ref[pl.ds(z, NX, stride=NZ), :] for z in range(NZ)]
    ends = (v[0] + v[8], v[0] - v[8])
    even = [None] + [v[z] + v[16 - z] for z in range(1, 8)]
    odd = [None] + [v[z] - v[16 - z] for z in range(1, 8)]
    even2 = [[None] + [even[z] + even[8 - z] for z in (1, 2, 3)], [None] + [even[z] - even[8 - z] for z in (1, 2, 3)]]
    odd2 = [[None] + [odd[z] - odd[8 - z] for z in (1, 2, 3)], [None] + [odd[z] + odd[8 - z] for z in (1, 2, 3)]]
    re, im = [], []
    for k in range(9):
        a = 2 * np.pi * k / NZ
        p = k % 2
        pairs = [(1.0, ends[p])] + [(np.cos(a * z), even2[p][z]) for z in (1, 2, 3)]
        re.append(combine(pairs + [(np.cos(4 * a), even[4])]))
        pairs = [(-np.sin(a * z), odd2[p][z]) for z in (1, 2, 3)]
        im.append(combine(pairs + [(-np.sin(4 * a), odd[4])]) if 0 < k < 8 else None)
    im[0] = re[8]
    blocks = [jnp.concatenate([re[k], im[k]], axis=0) for k in range(8)]
    o_ref[0:64, :] = flow_product(f_ref, 0, blocks[:1])
    out = flow_product(f_ref, 1, blocks[1:])
    for k in range(7):
        o_ref[64 * k + 64 : 64 * k + 128, :] = out[:, 128 * k : 128 * k + 128]


def backward_kernel(f_ref, x_ref, o_ref):
    blocks = [x_ref[64 * k : 64 * k + 64, :] for k in range(8)]
    first = flow_product(f_ref, 0, blocks[:1])
    rest = flow_product(f_ref, 1, blocks[1:])
    parts = [first] + [rest[:, 128 * k : 128 * k + 128] for k in range(7)]
    re = [v[0:NX] for v in parts] + [first[NX:]]
    im = [v[NX:] for v in parts]
    for z in range(5):
        a = 2 * np.pi * z / NZ
        e0 = combine([(1 / 16, re[0]), (np.cos(8 * a) / 16, re[8])] + [(np.cos(a * k) / 8, re[k]) for k in (2, 4, 6)])
        e1 = combine([(np.cos(a * k) / 8, re[k]) for k in (1, 3, 5, 7)])
        o0 = combine([(np.sin(a * k) / 8, im[k]) for k in (2, 4, 6)])
        o1 = combine([(np.sin(a * k) / 8, im[k]) for k in (1, 3, 5, 7)])
        plus = lambda p, q: q if p is None else p if q is None else p + q
        minus = lambda p, q: p if q is None else -q if p is None else p - q
        places = [(z, plus(e0, e1), plus(o0, o1))]
        if z < 4:
            places.append((8 - z, minus(e0, e1), minus(o1, o0)))
        for place, e, o in places:
            o_ref[pl.ds(place, NX, stride=NZ), :] = minus(e, o)
            if 0 < place < 8:
                o_ref[pl.ds(16 - place, NX, stride=NZ), :] = plus(e, o)


def table_product(v, t_ref):
    both = dot(jnp.concatenate(halves(v), axis=1), t_ref[...])
    return both[:, :128] + both[:, 128:]


def store_table(t_ref, table):
    high, low = halves(table)
    t_ref[0:128, 0:128] = high
    t_ref[128:256, 0:128] = high
    t_ref[0:128, 128:256] = low
    t_ref[128:256, 128:256] = jnp.zeros((128, 128), bf16)


def roll_up(v):
    return pltpu.roll(v, ROWS - 1, axis=0)


def roll_down(v):
    return pltpu.roll(v, 1, axis=0)


def wall_apply(s, q, planes, g):
    parts = [g * p for p in planes] + [g * roll_up(planes[0])]
    n = q + 1
    half = n // 2
    even = [parts[l] + parts[q - l] for l in range(half)]
    odd = [parts[l] - parts[q - l] for l in range(half)]
    out = [None] * n
    for k in range(half):
        p = m = None
        for l in range(half):
            ce = 0.5 * (s[k, l] + s[k, q - l])
            co = 0.5 * (s[k, l] - s[k, q - l])
            te, to = float(ce) * even[l], float(co) * odd[l]
            p = te if p is None else p + te
            m = to if m is None else m + to
        out[k] = p + m
        out[q - k] = p - m
    out[0] = out[0] + roll_down(out[q])
    return out[:q]


def weighted_sum(coefs, planes):
    total = None
    for c, v in zip(coefs, planes):
        c = float(c)
        if c == 0.0:
            continue
        t = v if c == 1.0 else c * v
        total = t if total is None else total + t
    return total


def restrict_wall(j, fine, coarse, planes):
    out = [weighted_sum(j[:fine, c], planes) for c in range(coarse)]
    out[0] = out[0] + roll_down(weighted_sum(j[:fine, coarse], planes))
    return out


def prolong_wall(j, fine, coarse, planes):
    closed = list(planes) + [roll_up(planes[0])]
    return [weighted_sum(j[k], closed) for k in range(fine)]


def cycle_kernel(
    h_ref, mats_ref, in_ref, out_ref,
    w_ref, geo_ref,
    u7, r7, x7, d7, u3, r3, x3, d3,
    square, g7_ref, g3_ref, r7_ref, p7_ref, r3_ref, p3_ref,
):
    n = lax.axis_index("gx") % 4 * 8 + lax.axis_index("gz")
    b = lax.axis_index("gx") // 4
    at_x = PHASES_AT + 2 * n + jnp.where(b > 0, 64, 0)
    at_z = PHASES_AT + 128 + 2 * jnp.where(b > 0, b, n // 16 * 8)
    cx, sx = mats_ref[pl.ds(at_x, 1), :], mats_ref[pl.ds(at_x + 1, 1), :]
    cz, sz = mats_ref[pl.ds(at_z, 1), :], mats_ref[pl.ds(at_z + 1, 1), :]
    cosines = (cx, cz, cx * cz - sx * sz)
    sines = (sx, sz, sx * cz + cx * sz)
    lane = lax.broadcasted_iota(jnp.int32, (1, 128), 1)
    first = lane < 64
    mass7, inv7, ratio7, mask7 = (mats_ref[n : n + 1, :] for n in range(LANES_AT, LANES_AT + 4))
    mass3, inv3, ratio3, mask3 = (mats_ref[n : n + 1, :] for n in range(LANES_AT + 4, LANES_AT + 8))
    mask1 = mats_ref[LANES_AT + 8 : LANES_AT + 9, :]

    upper = [jnp.where(first, c, s) for c, s in zip(cosines, sines)]
    lower = [jnp.where(first, -s, c) for c, s in zip(cosines, sines)]

    def mode_table(at, rows, phases):
        top = mats_ref[at : at + rows]
        low = pltpu.roll(top, 64, axis=1)
        for n in range(phases):
            at += rows
            t = mats_ref[at : at + rows]
            top = top + upper[n] * t
            low = low + lower[n] * pltpu.roll(t, 64, axis=1)
        if rows == 64:
            return jnp.concatenate([top, low], axis=0)
        square[...] = jnp.zeros((128, 128), f32)
        square[0:rows] = top
        square[64 : 64 + rows] = low
        return square[...]

    store_table(g7_ref, mode_table(G7_AT, 64, 2))
    store_table(g3_ref, mode_table(G3_AT, 24, 2))
    table = mode_table(P7_AT, 24, 3)
    store_table(p7_ref, table)
    store_table(r7_ref, (table * mass7).T * inv3)
    table = mode_table(P3_AT, 8, 3)
    store_table(p3_ref, table)
    store_table(r3_ref, (table * mass3).T)

    re = in_ref[pl.ds(0, 256, stride=2), :]
    im = in_ref[pl.ds(1, 256, stride=2), :]
    w_ref[0:256, :] = jnp.where(first, re, pltpu.roll(im, 64, axis=1)) * inv7
    w_ref[256:512, :] = jnp.where(first, pltpu.roll(re, 64, axis=1), im) * inv7
    w_ref[512:, :] = jnp.zeros((w_ref.shape[0] - 512, 128), f32)
    for k in range(7):
        r7[k] = float(1.0 / FINE.weight[k]) * w_ref[pl.ds(k, ROWS, stride=7), :]

    h = h_ref[...]
    row = lax.broadcasted_iota(jnp.int32, (ROWS, 128), 0)
    g = jnp.where(row < NY, 2.0 / jnp.where(row < NY, h, 1.0), 0.0)
    h_pair = h + roll_down(h)
    g_pair = g + roll_down(g)
    geo_ref[0] = h
    geo_ref[1] = g
    geo_ref[2] = h_pair

    def height(k):
        return geo_ref[0 if k else 2]

    def inverse_diag(level, ratio, mask, k):
        d = height(k) * ratio + float(level.stiff[k, k]) * (g if k else g_pair)
        return jnp.where(d > 0.0, mask / jnp.where(d > 0.0, d, 1.0), 0.0)

    for k in range(7):
        d7[k] = inverse_diag(FINE, ratio7, mask7, k)
    for k in range(3):
        d3[k] = inverse_diag(MID, ratio3, mask3, k)
    d1_mix = ((4.0 + screen_shift) - 2.0 * cx - 2.0 * cz) * mask1
    d1 = inverse_diag(LOW, 4.0 + screen_shift, mask1, 0)

    def apply(level, u, table):
        q = level.q
        m = table_product(u[...].reshape(q * ROWS, 128), table)
        wall = wall_apply(level.stiff, q, [u[k] for k in range(q)], geo_ref[1])
        return [height(k) * m[k * ROWS : (k + 1) * ROWS] + wall[k] for k in range(q)]

    def smooth(level, u, r, x, d, table, fresh, keep_residual):
        q = level.q
        start, steps = cheb_steps(level.bound, SMOOTH_STEPS, smooth_floor)
        for k in range(q):
            t = start * (d[k] * r[k])
            u[k] = t
            x[k] = t if fresh else x[k] + t
        for alpha, beta in steps:
            au = apply(level, u, table)
            for k in range(q):
                t = r[k] - au[k]
                r[k] = t
                t = alpha * u[k] + beta * (d[k] * t)
                u[k] = t
                x[k] = x[k] + t
        if keep_residual:
            au = apply(level, u, table)
            for k in range(q):
                r[k] = r[k] - au[k]

    def product(planes, table):
        m = table_product(jnp.concatenate(planes, axis=0), table)
        return [m[k * ROWS : (k + 1) * ROWS] for k in range(len(planes))]

    smooth(FINE, u7, r7, x7, d7, g7_ref, True, True)
    down = product(restrict_wall(R7, 7, 3, [r7[k] for k in range(7)]), r7_ref)
    for k in range(3):
        r3[k] = down[k]

    smooth(MID, u3, r3, x3, d3, g3_ref, True, True)
    r1 = product(restrict_wall(R3, 3, 1, [r3[k] for k in range(3)]), r3_ref)[0]

    start, steps = cheb_steps(LOW.bound, COARSE_STEPS, coarse_floor)
    my1 = height(0) * d1_mix
    u1 = start * (d1 * r1)
    x1 = u1
    for alpha, beta in steps:
        flow = g * (u1 - roll_up(u1))
        r1 = r1 - (my1 * u1 + (flow - roll_down(flow)))
        u1 = alpha * u1 + beta * (d1 * r1)
        x1 = x1 + u1

    up = prolong_wall(J3, 3, 1, product([x1], p3_ref))
    for k in range(3):
        u3[k] = up[k]
        x3[k] = x3[k] + up[k]
    au = apply(MID, u3, g3_ref)
    for k in range(3):
        r3[k] = r3[k] - au[k]
    smooth(MID, u3, r3, x3, d3, g3_ref, False, False)

    up = prolong_wall(J7, 7, 3, product([x3[k] for k in range(3)], p7_ref))
    for k in range(7):
        u7[k] = up[k]
        x7[k] = x7[k] + up[k]
    au = apply(FINE, u7, g7_ref)
    for k in range(7):
        r7[k] = r7[k] - au[k]
    smooth(FINE, u7, r7, x7, d7, g7_ref, False, False)

    for k in range(7):
        w_ref[pl.ds(k, ROWS, stride=7), :] = x7[k]
    top = w_ref[0:256, :]
    low = w_ref[256:512, :]
    out_ref[pl.ds(0, 256, stride=2), :] = jnp.where(first, top, pltpu.roll(low, 64, axis=1))
    out_ref[pl.ds(1, 256, stride=2), :] = jnp.where(first, pltpu.roll(top, 64, axis=1), low)


VMEM = pl.BlockSpec(memory_space=pltpu.VMEM)
PARAMS = pltpu.CompilerParams(vmem_limit_bytes=32 * 1024 * 1024)
FLAT = jax.ShapeDtypeStruct((512, 128), f32)


def exchange(block):
    moved = lax.all_to_all(block.reshape(DEVICES, 2, 128), ("gx", "gz"), 0, 0)
    return moved.reshape(512, 128)


def cycle_call(heights, modes):
    fine = pltpu.VMEM((7, ROWS, 128), f32)
    mid = pltpu.VMEM((3, ROWS, 128), f32)
    table = pltpu.VMEM((256, 256), bf16)
    return pl.pallas_call(
        cycle_kernel, out_shape=FLAT,
        in_specs=[VMEM, VMEM, VMEM], out_specs=VMEM,
        scratch_shapes=[
            pltpu.VMEM((7 * ROWS, 128), f32), mid,
            fine, fine, fine, fine, mid, mid, mid, mid,
            pltpu.VMEM((128, 128), f32), table, table, table, table, table, table,
        ],
        compiler_params=PARAMS,
    )(
        heights, jnp.asarray(MATRICES), modes,
    )


def transform(kernel, table, block):
    return pl.pallas_call(
        kernel, out_shape=FLAT, in_specs=[VMEM, VMEM], out_specs=VMEM, compiler_params=PARAMS
    )(jnp.asarray(split_terms(table)), block)


def body(residual, layer_heights):
    packed, heights = pl.pallas_call(
        pack_kernel, out_shape=(FLAT, jax.ShapeDtypeStruct((ROWS, 128), f32)),
        in_specs=[VMEM, VMEM], out_specs=(VMEM, VMEM),
        scratch_shapes=[pltpu.VMEM((256, 256), f32), pltpu.VMEM((8, 128), f32)],
        compiler_params=PARAMS,
    )(residual, layer_heights.reshape(1, NY))
    modes = exchange(transform(forward_kernel, FORWARD, exchange(packed)))
    solved = cycle_call(heights, modes)
    spread = exchange(transform(backward_kernel, BACKWARD, exchange(solved)))
    return pl.pallas_call(
        unpack_kernel, out_shape=jax.ShapeDtypeStruct((7, 14, 512), f32),
        in_specs=[VMEM], out_specs=VMEM, compiler_params=PARAMS,
    )(spread)


def solution(mesh):
    return jax.shard_map(
        body,
        mesh=mesh,
        in_specs=(P("gx", "gz", None), P()),
        out_specs=P("gx", "gz", None),
        check_vma=False,
    )
```

time: 107 us -> 99.3 us (0.928)
  blocking collectives: 71.5 us -> 92.2 us
  waiting for transfers between devices: 14.9 us -> 0 us
  Pallas kernels: 11.5 us -> 5.18 us
  starting transfers between devices: 5.97 us -> 0 us
    all_to_all x3 -> x4, blocking collectives: 71.5 us -> 92.2 us  [exchange(): moved = lax.all_to_all(block.reshape(DEVICES, 2, 128), ('gx', 'gz'), 0, 0)]
    all_to_all x1 -> x0, waiting for transfers between devices: 14.9 us -> none  [exchange(): moved = lax.all_to_all(block.reshape(DEVICES, 2, 128), ('gx', 'gz'), 0, 0)]
    pallas_call x4, Pallas kernels: 10.7 us -> 4.36 us  [the longest x1 3.59 us: cycle_call(): pl.pallas_call(cycle_kernel, out_shape=FLAT, in_specs=[VMEM, VMEM, VMEM],...]
    all_to_all x1 -> x0, starting transfers between devices: 5.97 us -> none  [exchange(): moved = lax.all_to_all(block.reshape(DEVICES, 2, 128), ('gx', 'gz'), 0, 0)]
    unnamed x14 -> x10, local copies, waits for them, and re-layouts: 2.3 us -> 1.61 us
  transfers between devices with their start and end apart: 1 -> 0, of which waited for: 1 -> 0; matrix products, arithmetic and copies ran while one was open for 0% -> 0% of each run, Pallas kernels for 0% -> 0%
where the time goes in v1:
time: 99.3 us; the launch traced here: 99 us
  blocking collectives  92.2 us (93%)
  Pallas kernels  5.18 us (5%)
  local copies, waits for them, and re-layouts  1.61 us (2%)
    all_to_all x4, blocking collectives, exchange(): moved = lax.all_to_all(block.reshape(DEVICES, 2, 128), ('gx', 'gz'), 0, 0)  92.2 us
    pallas_call x1, Pallas kernels, cycle_call(): pl.pallas_call(cycle_kernel, out_shape=FLAT, in_specs=[VMEM, VMEM, VMEM],...  3.59 us

profile of v1, /device:TPU:1, one launch (start us, length us, event | category | flops | bytes accessed | tf_op | source)
XLA Modules:
  0.0 99.0 jit_solution(9649464679684768092)
XLA Ops:
  0.0 0.0 copy-start.4
  0.0 0.7 copy-done.4
  0.7 0.0 copy-start.1
  0.7 0.9 copy-done.1
  1.6 0.2 shard_map.55
  1.8 0.0 copy-start.3
  1.8 30.3 %all_to_all.20 = f32[256,2,128]{2,1,0:T(2,128)S(1)} all-to-all(f32[256,2,128]{2,1,0:T(2,128)S(1)} %bitcast.16), channel_id=1, replica_groups=mesh['gx'=32,'gz'=8] {'gx','gz'}, dimensions={0} | all-to-all | bytes 524288 | tf_op jit(solution)/shard_map/all_to_all | solution.py:528
  32.1 0.0 copy-done.3
  32.1 0.3 shard_map.56
  32.4 0.0 copy-start
  32.4 20.7 %all_to_all.21 = f32[256,2,128]{2,1,0:T(2,128)S(1)} all-to-all(f32[256,2,128]{2,1,0:T(2,128)S(1)} %bitcast.12), channel_id=1, replica_groups=mesh['gx'=32,'gz'=8] {'gx','gz'}, dimensions={0} | all-to-all | bytes 524288 | tf_op jit(solution)/shard_map/all_to_all | solution.py:528
  53.1 0.0 copy-done
  53.1 3.6 %shard_map.57 = f32[512,128]{1,0:T(8,128)S(1)} custom-call(f32[80,128]{1,0:T(8,128)S(1)} %get-tuple-element.7.h_ref, f32[560,128]{1,0:T(8,128)S(1)} %copy-done, f32[512,128]{1,0:T(8,128)S(1)} %bitcast.9), custom_call_target="tpu_custom_call" | custom-call | tf_op jit(solution)/shard_map/pallas_call | solution.py:536
  56.7 0.0 copy-start.2
  56.7 20.7 %all_to_all.22 = f32[256,2,128]{2,1,0:T(2,128)S(1)} all-to-all(f32[256,2,128]{2,1,0:T(2,128)S(1)} %bitcast.10), channel_id=1, replica_groups=mesh['gx'=32,'gz'=8] {'gx','gz'}, dimensions={0} | all-to-all | bytes 524288 | tf_op jit(solution)/shard_map/all_to_all | solution.py:528
  77.3 0.0 copy-done.2
  77.3 0.3 shard_map.58
  77.6 20.5 %all_to_all.23 = f32[256,2,128]{2,1,0:T(2,128)S(1)} all-to-all(f32[256,2,128]{2,1,0:T(2,128)S(1)} %bitcast.14), channel_id=1, replica_groups=mesh['gx'=32,'gz'=8] {'gx','gz'}, dimensions={0} | all-to-all | bytes 524288 | tf_op jit(solution)/shard_map/all_to_all | solution.py:528
  98.2 0.8 shard_map.59
Async XLA Ops:
  0.0 0.7 copy-start.4
  0.7 0.9 copy-start.1
  1.8 30.3 %copy-start.3 = (bf16[128,256]{1,0:T(8,128)(2,1)S(1)}, bf16[128,256]{1,0:T(8,128)(2,1)}, u32[]{:S(2)}) copy-start(bf16[128,256]{1,0:T(8,128)(2,1)} %constant.6.clone.f_ref) | copy-start | bytes 196612
  32.4 20.7 %copy-start = (f32[560,128]{1,0:T(8,128)S(1)}, f32[560,128]{1,0:T(8,128)}, u32[]{:S(2)}) copy-start(f32[560,128]{1,0:T(8,128)} %constant.7.clone.mats_ref) | copy-start | bytes 860164
  56.7 20.7 %copy-start.2 = (bf16[128,256]{1,0:T(8,128)(2,1)S(1)}, bf16[128,256]{1,0:T(8,128)(2,1)}, u32[]{:S(2)}) copy-start(bf16[128,256]{1,0:T(8,128)(2,1)} %constant.8.clone.f_ref) | copy-start | bytes 196612

commit v2 on v1

--- a/solution.py
+++ b/solution.py
@@ -5,6 +5,7 @@
 from jax import lax
 from jax.experimental import pallas as pl
 from jax.experimental.pallas import tpu as pltpu
+from jax.sharding import Mesh
 from jax.sharding import PartitionSpec as P
 
 
@@ -61,15 +62,15 @@
 
 def lanes_of(values):
     n = values.shape[0]
-    out = np.zeros((8, 8))
+    out = np.zeros((7, 7))
     out[:n, :n] = values
-    return out.reshape(64)
+    return np.pad(out.reshape(49), (0, 15))
 
 
 def square_of(matrix, n_out, n_in):
-    out = np.zeros((8, 8, 8, 8))
+    out = np.zeros((7, 7, 7, 7))
     out[:n_out, :n_out, :n_in, :n_in] = matrix.reshape(n_out, n_out, n_in, n_in)
-    return out.reshape(64, 64)
+    return np.pad(out.reshape(49, 49), ((0, 15), (0, 15)))
 
 
 class Level:
@@ -122,57 +123,30 @@
     return j, tables
 
 
-def flow_tables():
-    x = np.arange(NX)
-    forward = np.zeros((2, 2 * NX, 2 * NX))
-    backward = np.zeros((2, 2 * NX, 2 * NX))
-    phases = np.zeros((152, 2, 64))
-    re, im = slice(0, NX), slice(NX, 2 * NX)
+def phase_rows():
+    rows = np.zeros((152, 2, 64))
     for n in range(NX):
-        c, s = np.cos(2 * np.pi * n * x / NX), np.sin(2 * np.pi * n * x / NX)
-        forward[1, 2 * n, re], forward[1, 2 * n, im] = c, s
-        forward[1, 2 * n + 1, re], forward[1, 2 * n + 1, im] = -s, c
-        backward[1, re, 2 * n], backward[1, re, 2 * n + 1] = c / NX, -s / NX
-        backward[1, im, 2 * n], backward[1, im, 2 * n + 1] = s / NX, c / NX
         t = 2 * np.pi * n / NX
-        phases[64 + 2 * n], phases[65 + 2 * n] = np.cos(t), np.sin(t)
-    for half in range(2):
-        part = slice(half * NX, half * NX + NX)
-        for k in range(16):
-            n = 16 * half + k
-            if k:
-                c, s = np.cos(2 * np.pi * k * x / NX), np.sin(2 * np.pi * k * x / NX)
-                forward[0, 2 * n, part], forward[0, 2 * n + 1, part] = c, -s
-                backward[0, part, 2 * n] = 2 * c / NX
-                backward[0, part, 2 * n + 1] = -2 * s / NX
-                t = 2 * np.pi * k / NX
-                phases[2 * n], phases[2 * n + 1] = np.cos(t), np.sin(t)
-            else:
-                one, turn = np.ones(NX), np.cos(np.pi * x)
-                forward[0, 2 * n, part], forward[0, 2 * n + 1, part] = one, turn
-                backward[0, part, 2 * n], backward[0, part, 2 * n + 1] = one / NX, turn / NX
-                phases[2 * n, 0], phases[2 * n, 1] = 1.0, -1.0
-    for b in range(9):
-        t = 2 * np.pi * b / NZ
-        phases[128 + 2 * b], phases[129 + 2 * b] = np.cos(t), np.sin(t) if b % 8 else 0.0
-    return forward, backward, phases.reshape(152, 128)
+        rows[64 + 2 * n], rows[65 + 2 * n] = np.cos(t), np.sin(t)
+        k = n % 16
+        t = 2 * np.pi * k / NX
+        if k:
+            rows[2 * n], rows[2 * n + 1] = np.cos(t), np.sin(t)
+        else:
+            rows[2 * n, 0], rows[2 * n, 1] = 1.0, -1.0
+    for k in range(9):
+        t = 2 * np.pi * k / NZ
+        rows[128 + 2 * k], rows[129 + 2 * k] = np.cos(t), np.sin(t) if k % 8 else 0.0
+    return rows.reshape(152, 128)
 
 
 FINE, MID, LOW = Level(7), Level(3), Level(1)
 J7, P7_TABLES = transfer_tables(7, 3)
 J3, P3_TABLES = transfer_tables(3, 1)
-FORWARD, BACKWARD, PHASES = flow_tables()
 MATRICES = np.concatenate(FINE.tables + MID.tables + P7_TABLES + P3_TABLES).astype(np.float32)
 R7 = FINE.weight[:, None] * J7 / MID.weight
 R3 = MID.weight[:, None] * J3 / LOW.weight
 G7_AT, G3_AT, P7_AT, P3_AT = 0, 192, 264, 360
-
-
-def split_terms(tables):
-    high = tables.astype(np.float32).astype(ml_dtypes.bfloat16)
-    low = (tables - high.astype(np.float64)).astype(ml_dtypes.bfloat16)
-    rows = np.concatenate([high, high, low], axis=2).reshape(4 * NX, 6 * NX)
-    return np.concatenate([rows, np.zeros((4 * NX, 2 * NX), rows.dtype)], axis=1)
 
 
 LANES = np.zeros((16, 128))
@@ -182,7 +156,7 @@
     LANES[4 * n + 2] = level.ratio_lanes
     LANES[4 * n + 3] = level.mask_lanes
 LANES[8] = LOW.mask_lanes
-MATRICES = np.concatenate([MATRICES, LANES, PHASES]).astype(np.float32)
+MATRICES = np.concatenate([MATRICES, LANES, phase_rows()]).astype(np.float32)
 LANES_AT, PHASES_AT = 392, 408
 
 
@@ -199,27 +173,43 @@
     return 1.0 / centre, steps
 
 
-def pack_kernel(x_ref, h_ref, o_ref, rows_ref, m_ref, line_ref):
-    m_ref[...] = jnp.zeros_like(m_ref)
-    for e in range(2):
-        for h in range(2):
-            for a in range(7):
-                r = e * 128 + h * 64 + a * 8
-                m_ref[r : r + 7, :] = x_ref[a, e * 7 : e * 7 + 7, h * 256 : h * 256 + 256]
-    for e in range(2):
-        o_ref[pl.ds(e, 256, stride=2), :] = m_ref[e * 128 : e * 128 + 128, :].T
+SLAB = 13
+FIELD = 32 * SLAB
+USED = 8 * 49
+
+
+def swap(v):
+    return pltpu.roll(v, 64, axis=1)
+
+
+def mix(first, v, w):
+    return jnp.where(first, v, swap(w)), jnp.where(first, swap(v), w)
+
+
+def pack_kernel(x_ref, h_ref, o_ref, rows_ref, line_ref):
+    first, _ = lane_tools()
+    o_ref[USED:, :] = jnp.zeros((FIELD - USED, 128), f32)
+    for a in range(7):
+        for t in range(4):
+            part = slice(128 * t, 128 * t + 128)
+            low, high = mix(first, x_ref[a, 0:7, part], x_ref[a, 7:14, part])
+            r = 98 * t + 7 * a
+            o_ref[r : r + 7, :] = low
+            o_ref[r + 49 : r + 56, :] = high
     line_ref[...] = jnp.zeros_like(line_ref)
     line_ref[0:1, 0:NY] = h_ref[...]
     rows_ref[...] = jnp.broadcast_to(line_ref[0:1, :], (128, 128)).T[:ROWS]
 
 
 def unpack_kernel(x_ref, o_ref):
-    for e in range(2):
-        m = x_ref[pl.ds(e, 256, stride=2), :].T
-        for h in range(2):
-            for a in range(7):
-                r = h * 64 + a * 8
-                o_ref[a, e * 7 : e * 7 + 7, h * 256 : h * 256 + 256] = m[r : r + 7, :]
+    first, _ = lane_tools()
+    for a in range(7):
+        for t in range(4):
+            part = slice(128 * t, 128 * t + 128)
+            r = 98 * t + 7 * a
+            low, high = mix(first, x_ref[r : r + 7, :], x_ref[r + 49 : r + 56, :])
+            o_ref[a, 0:7, part] = low
+            o_ref[a, 7:14, part] = high
 
 
 def halves(v):
@@ -231,76 +221,126 @@
     return jnp.dot(a, b, preferred_element_type=f32)
 
 
-def combine(pairs):
-    total = None
-    for c, v in pairs:
-        c = float(c)
-        if abs(c) < 1e-12:
-            continue
-        if abs(abs(c) - 1.0) < 1e-12:
-            t = v
-            if total is None:
-                total = v if c > 0 else -v
-            else:
-                total = total + v if c > 0 else total - v
-            continue
-        t = c * v
-        total = t if total is None else total + t
-    return total
-
-
-def flow_product(f_ref, which, rows):
-    v = jnp.concatenate(rows, axis=1)
-    high, low = halves(v)
-    t = f_ref[which * 64 : which * 64 + 64, :][:, :192]
-    return dot(t, jnp.concatenate([high, low, high], axis=0))
-
-
-def forward_kernel(f_ref, x_ref, o_ref):
-    v = [x_ref[pl.ds(z, NX, stride=NZ), :] for z in range(NZ)]
-    ends = (v[0] + v[8], v[0] - v[8])
-    even = [None] + [v[z] + v[16 - z] for z in range(1, 8)]
-    odd = [None] + [v[z] - v[16 - z] for z in range(1, 8)]
-    even2 = [[None] + [even[z] + even[8 - z] for z in (1, 2, 3)], [None] + [even[z] - even[8 - z] for z in (1, 2, 3)]]
-    odd2 = [[None] + [odd[z] - odd[8 - z] for z in (1, 2, 3)], [None] + [odd[z] + odd[8 - z] for z in (1, 2, 3)]]
-    re, im = [], []
-    for k in range(9):
-        a = 2 * np.pi * k / NZ
-        p = k % 2
-        pairs = [(1.0, ends[p])] + [(np.cos(a * z), even2[p][z]) for z in (1, 2, 3)]
-        re.append(combine(pairs + [(np.cos(4 * a), even[4])]))
-        pairs = [(-np.sin(a * z), odd2[p][z]) for z in (1, 2, 3)]
-        im.append(combine(pairs + [(-np.sin(4 * a), odd[4])]) if 0 < k < 8 else None)
-    im[0] = re[8]
-    blocks = [jnp.concatenate([re[k], im[k]], axis=0) for k in range(8)]
-    o_ref[0:64, :] = flow_product(f_ref, 0, blocks[:1])
-    out = flow_product(f_ref, 1, blocks[1:])
-    for k in range(7):
-        o_ref[64 * k + 64 : 64 * k + 128, :] = out[:, 128 * k : 128 * k + 128]
-
-
-def backward_kernel(f_ref, x_ref, o_ref):
-    blocks = [x_ref[64 * k : 64 * k + 64, :] for k in range(8)]
-    first = flow_product(f_ref, 0, blocks[:1])
-    rest = flow_product(f_ref, 1, blocks[1:])
-    parts = [first] + [rest[:, 128 * k : 128 * k + 128] for k in range(7)]
-    re = [v[0:NX] for v in parts] + [first[NX:]]
-    im = [v[NX:] for v in parts]
-    for z in range(5):
-        a = 2 * np.pi * z / NZ
-        e0 = combine([(1 / 16, re[0]), (np.cos(8 * a) / 16, re[8])] + [(np.cos(a * k) / 8, re[k]) for k in (2, 4, 6)])
-        e1 = combine([(np.cos(a * k) / 8, re[k]) for k in (1, 3, 5, 7)])
-        o0 = combine([(np.sin(a * k) / 8, im[k]) for k in (2, 4, 6)])
-        o1 = combine([(np.sin(a * k) / 8, im[k]) for k in (1, 3, 5, 7)])
-        plus = lambda p, q: q if p is None else p if q is None else p + q
-        minus = lambda p, q: p if q is None else -q if p is None else p - q
-        places = [(z, plus(e0, e1), plus(o0, o1))]
-        if z < 4:
-            places.append((8 - z, minus(e0, e1), minus(o1, o0)))
-        for place, e, o in places:
-            o_ref[pl.ds(place, NX, stride=NZ), :] = minus(e, o)
-            if 0 < place < 8:
-                o_ref[pl.ds(16 - place, NX, stride=NZ), :] = plus(e, o)
+HALF = float(np.sqrt(0.5))
+
+
+def lane_tools():
+    first = lax.broadcasted_iota(jnp.int32, (1, 128), 1) < 64
+    return first, jnp.where(first, 1.0, -1.0).astype(f32)
+
+
+def plane(ref, n):
+    return ref[n * SLAB : n * SLAB + SLAB, :]
+
+
+def put(ref, n, v):
+    ref[n * SLAB : n * SLAB + SLAB, :] = v
+
+
+def span_forward_kernel(x_ref, o_ref):
+    first, sign = lane_tools()
+    for r in range(4):
+        x = [plane(x_ref, 8 * r + j) for j in range(8)]
+        s = [None] + [x[j] + x[8 - j] for j in (1, 2, 3)]
+        d = [None] + [x[j] - x[8 - j] for j in (1, 2, 3)]
+        up, down = x[0] + x[4], x[0] - x[4]
+        odd, turn = s[1] + s[3], HALF * (s[1] - s[3])
+        slope = HALF * (d[1] + d[3])
+        re = [up + s[2] + odd, down + turn, up - s[2], down - turn, up + s[2] - odd]
+        im = [None, -slope - d[2], d[3] - d[1], d[2] - slope]
+        flip = swap(re[0])
+        put(o_ref, r, jnp.where(first, re[0] + flip, flip - re[0]))
+        put(o_ref, 16 + r, sign * re[4])
+        for f in (1, 2, 3):
+            c, t = float(np.cos(np.pi * f / 8)), float(np.sin(np.pi * f / 8))
+            re_swap, im_swap = swap(re[f]), swap(im[f])
+            base = jnp.where(first, re[f], im_swap)
+            extra = c * jnp.where(first, re_swap, im[f]) + t * jnp.where(first, im_swap, -re[f])
+            put(o_ref, 4 * f + r, base + extra)
+            put(o_ref, 4 * (8 - f) + r, sign * (base - extra))
+
+
+def span_backward_kernel(x_ref, o_ref):
+    first, sign = lane_tools()
+    for r in range(4):
+        v = [plane(x_ref, 4 * k + r) for k in range(8)]
+        flip = swap(v[0])
+        re = [jnp.where(first, v[0] + flip, flip - v[0])]
+        im = [None]
+        for f in (1, 2, 3):
+            c, t = float(np.cos(np.pi * f / 8)), float(np.sin(np.pi * f / 8))
+            total, other = v[f] + v[8 - f], swap(v[f] - v[8 - f])
+            re.append(2.0 * jnp.where(first, total, c * other - t * total))
+            im.append(2.0 * jnp.where(first, other, t * other + c * total))
+        re.append((2.0 * sign) * v[4])
+        up, down = re[0] + re[4], re[0] - re[4]
+        odd, turn = re[1] + re[3], HALF * (re[1] - re[3])
+        slope = HALF * (im[1] + im[3])
+        c = [up + re[2] + odd, down + turn, up - re[2], down - turn, up + re[2] - odd]
+        s = [None, slope + im[2], im[1] - im[3], slope - im[2]]
+        put(o_ref, 8 * r, c[0])
+        put(o_ref, 8 * r + 4, c[4])
+        for j in (1, 2, 3):
+            put(o_ref, 8 * r + j, c[j] - s[j])
+            put(o_ref, 8 * r + 8 - j, c[j] + s[j])
+
+
+def complex_transform(x, sign, direction):
+    n = len(x)
+    if n == 1:
+        return x
+    even = complex_transform(x[0::2], sign, direction)
+    odd = complex_transform(x[1::2], sign, direction)
+    low, high = [], []
+    for k in range(n // 2):
+        c = float(np.cos(2 * np.pi * k / n))
+        s = direction * float(np.sin(2 * np.pi * k / n))
+        if k == 0:
+            t = odd[k]
+        elif 4 * k == n:
+            t = (s * sign) * swap(odd[k])
+        else:
+            t = c * odd[k] + (s * sign) * swap(odd[k])
+        low.append(even[k] + t)
+        high.append(even[k] - t)
+    return low + high
+
+
+def flow_forward_kernel(x_ref, o_ref):
+    first, sign = lane_tools()
+    for n, v in enumerate(complex_transform([plane(x_ref, n) for n in range(NX)], sign, 1.0)):
+        put(o_ref, n, v)
+
+    @pl.when(lax.axis_index("z") == 0)
+    def _():
+        w = [plane(o_ref, n) for n in range(NX)]
+        put(o_ref, 0, jnp.where(first, w[0], swap(w[16])))
+        put(o_ref, 16, jnp.where(first, swap(w[0]), w[16]))
+        for n in range(1, 16):
+            total, differ = w[n] + w[NX - n], w[n] - w[NX - n]
+            put(o_ref, n, 0.5 * jnp.where(first, total, differ))
+            put(o_ref, 16 + n, 0.5 * swap(jnp.where(first, -differ, total)))
+
+
+def flow_backward_kernel(x_ref, o_ref, w_ref):
+    first, sign = lane_tools()
+
+    @pl.when(lax.axis_index("z") == 0)
+    def _():
+        v = [plane(x_ref, n) for n in range(NX)]
+        put(w_ref, 0, jnp.where(first, v[0], swap(v[16])))
+        put(w_ref, 16, jnp.where(first, swap(v[0]), v[16]))
+        for n in range(1, 16):
+            other = swap(v[16 + n])
+            put(w_ref, n, v[n] - sign * other)
+            put(w_ref, NX - n, sign * v[n] + other)
+
+    @pl.when(lax.axis_index("z") > 0)
+    def _():
+        w_ref[...] = x_ref[...]
+
+    for n, v in enumerate(complex_transform([plane(w_ref, n) for n in range(NX)], sign, -1.0)):
+        put(o_ref, n, v)
 
 
 def table_product(v, t_ref):
@@ -373,8 +413,8 @@
     u7, r7, x7, d7, u3, r3, x3, d3,
     square, g7_ref, g3_ref, r7_ref, p7_ref, r3_ref, p3_ref,
 ):
-    n = lax.axis_index("gx") % 4 * 8 + lax.axis_index("gz")
-    b = lax.axis_index("gx") // 4
+    n = lax.axis_index("r") * 8 + lax.axis_index("gz")
+    b = lax.axis_index("z")
     at_x = PHASES_AT + 2 * n + jnp.where(b > 0, 64, 0)
     at_z = PHASES_AT + 128 + 2 * jnp.where(b > 0, b, n // 16 * 8)
     cx, sx = mats_ref[pl.ds(at_x, 1), :], mats_ref[pl.ds(at_x + 1, 1), :]
@@ -414,10 +454,13 @@
     store_table(p3_ref, table)
     store_table(r3_ref, (table * mass3).T)
 
-    re = in_ref[pl.ds(0, 256, stride=2), :]
-    im = in_ref[pl.ds(1, 256, stride=2), :]
-    w_ref[0:256, :] = jnp.where(first, re, pltpu.roll(im, 64, axis=1)) * inv7
-    w_ref[256:512, :] = jnp.where(first, pltpu.roll(re, 64, axis=1), im) * inv7
+    scale = inv7 * (1.0 / (NX * NZ))
+    for t in range(4):
+        r = 98 * t
+        both = jnp.concatenate([in_ref[r : r + 64, :], in_ref[r + 49 : r + 113, :]], axis=0).T
+        low, high = mix(first, both[:64], both[64:])
+        w_ref[128 * t : 128 * t + 64, :] = low * scale
+        w_ref[128 * t + 64 : 128 * t + 128, :] = high * scale
     w_ref[512:, :] = jnp.zeros((w_ref.shape[0] - 512, 128), f32)
     for k in range(7):
         r7[k] = float(1.0 / FINE.weight[k]) * w_ref[pl.ds(k, ROWS, stride=7), :]
@@ -513,20 +556,29 @@
 
     for k in range(7):
         w_ref[pl.ds(k, ROWS, stride=7), :] = x7[k]
-    top = w_ref[0:256, :]
-    low = w_ref[256:512, :]
-    out_ref[pl.ds(0, 256, stride=2), :] = jnp.where(first, top, pltpu.roll(low, 64, axis=1))
-    out_ref[pl.ds(1, 256, stride=2), :] = jnp.where(first, pltpu.roll(top, 64, axis=1), low)
+    for t in range(4):
+        r = 98 * t
+        both = jnp.concatenate(
+            mix(first, w_ref[128 * t : 128 * t + 64, :], w_ref[128 * t + 64 : 128 * t + 128, :]), axis=0
+        ).T
+        out_ref[r : r + 49, :] = both[0:49]
+        out_ref[r + 49 : r + 98, :] = both[64:113]
+    out_ref[USED:, :] = jnp.zeros((FIELD - USED, 128), f32)
 
 
 VMEM = pl.BlockSpec(memory_space=pltpu.VMEM)
 PARAMS = pltpu.CompilerParams(vmem_limit_bytes=32 * 1024 * 1024)
-FLAT = jax.ShapeDtypeStruct((512, 128), f32)
-
-
-def exchange(block):
-    moved = lax.all_to_all(block.reshape(DEVICES, 2, 128), ("gx", "gz"), 0, 0)
-    return moved.reshape(512, 128)
+FLAT = jax.ShapeDtypeStruct((FIELD, 128), f32)
+
+
+def in_plane(block):
+    block = block.reshape(32, SLAB, 1, 128)
+    return lax.all_to_all(block, ("r", "gz"), 0, 0).reshape(FIELD, 128)
+
+
+def along_z(block):
+    block = block.reshape(8, 4 * SLAB, 1, 128)
+    return lax.all_to_all(block, "z", 0, 0).reshape(FIELD, 128)
 
 
 def cycle_call(heights, modes):
@@ -547,22 +599,25 @@
     )
 
 
-def transform(kernel, table, block):
+def transform(kernel, block, scratch=()):
     return pl.pallas_call(
-        kernel, out_shape=FLAT, in_specs=[VMEM, VMEM], out_specs=VMEM, compiler_params=PARAMS
-    )(jnp.asarray(split_terms(table)), block)
+        kernel, out_shape=FLAT, in_specs=[VMEM], out_specs=VMEM,
+        scratch_shapes=scratch, compiler_params=PARAMS,
+    )(block)
 
 
 def body(residual, layer_heights):
     packed, heights = pl.pallas_call(
         pack_kernel, out_shape=(FLAT, jax.ShapeDtypeStruct((ROWS, 128), f32)),
         in_specs=[VMEM, VMEM], out_specs=(VMEM, VMEM),
-        scratch_shapes=[pltpu.VMEM((256, 256), f32), pltpu.VMEM((8, 128), f32)],
+        scratch_shapes=[pltpu.VMEM((8, 128), f32)],
         compiler_params=PARAMS,
     )(residual, layer_heights.reshape(1, NY))
-    modes = exchange(transform(forward_kernel, FORWARD, exchange(packed)))
+    spans = transform(span_forward_kernel, in_plane(packed))
+    modes = in_plane(transform(flow_forward_kernel, along_z(spans)))
     solved = cycle_call(heights, modes)
-    spread = exchange(transform(backward_kernel, BACKWARD, exchange(solved)))
+    flows = transform(flow_backward_kernel, in_plane(solved), [pltpu.VMEM((FIELD, 128), f32)])
+    spread = in_plane(transform(span_backward_kernel, along_z(flows)))
     return pl.pallas_call(
         unpack_kernel, out_shape=jax.ShapeDtypeStruct((7, 14, 512), f32),
         in_specs=[VMEM], out_specs=VMEM, compiler_params=PARAMS,
@@ -570,10 +625,8 @@
 
 
 def solution(mesh):
+    split = Mesh(mesh.devices.reshape(8, 4, 8), ("z", "r", "gz"))
+    spec = P(("z", "r"), "gz", None)
     return jax.shard_map(
-        body,
-        mesh=mesh,
-        in_specs=(P("gx", "gz", None), P()),
-        out_specs=P("gx", "gz", None),
-        check_vma=False,
+        body, mesh=split, in_specs=(spec, P()), out_specs=spec, check_vma=False
     )

time: 99.3 us -> 94.2 us (0.949)
  blocking collectives: 92.2 us -> 86.4 us
    all_to_all x4 -> x6, blocking collectives: 92.2 us -> 86.4 us  [the longest x4 55.4 us: in_plane(): return lax.all_to_all(block, ('r', 'gz'), 0, 0).reshape(FIELD, 128)]
where the time goes in v2:
time: 94.2 us; the launch traced here: 93.9 us
  blocking collectives  86.4 us (92%)
  Pallas kernels  5.82 us (6%)
  local copies, waits for them, and re-layouts  1.6 us (2%)
    all_to_all x4, blocking collectives, in_plane(): return lax.all_to_all(block, ('r', 'gz'), 0, 0).reshape(FIELD, 128)  55.4 us
    all_to_all x2, blocking collectives, along_z(): return lax.all_to_all(block, 'z', 0, 0).reshape(FIELD, 128)  31 us
    pallas_call x1, Pallas kernels, cycle_call(): pl.pallas_call(cycle_kernel, out_shape=FLAT, in_specs=[VMEM, VMEM, VMEM],...  3.77 us

profile of v2, /device:TPU:1, one launch (start us, length us, event | category | flops | bytes accessed | tf_op | source)
XLA Modules:
  0.0 93.9 jit_solution(1617949310109098124)
XLA Ops:
  0.0 0.0 copy-start.2
  0.0 0.7 copy-done.2
  0.7 0.0 copy-start.1
  0.7 0.9 copy-done.1
  1.6 0.2 shard_map.37
  1.8 16.8 %all_to_all.30 = f32[32,13,1,128]{3,2,1,0:T(1,128)S(1)} all-to-all(f32[32,13,1,128]{3,2,1,0:T(1,128)S(1)} %bitcast.24), channel_id=1, replica_groups=mesh['z'=8,'r'=4,'gz'=8] {'r','gz'}, dimensions={0} | all-to-all | bytes 425984 | tf_op jit(solution)/shard_map/all_to_all | solution.py:576
  18.6 0.1 shard_map.38
  18.7 17.7 %all_to_all.31 = f32[8,52,1,128]{3,2,1,0:T(1,128)S(1)} all-to-all(f32[8,52,1,128]{3,2,1,0:T(1,128)S(1)} %bitcast.17), channel_id=1, replica_groups=mesh['z'=8,'r'=4,'gz'=8] {'z'}, dimensions={0} | all-to-all | bytes 425984 | tf_op jit(solution)/shard_map/all_to_all | solution.py:581
  36.5 0.4 shard_map.39
  36.9 0.0 copy-start
  36.9 13.9 %all_to_all.32 = f32[32,13,1,128]{3,2,1,0:T(1,128)S(1)} all-to-all(f32[32,13,1,128]{3,2,1,0:T(1,128)S(1)} %bitcast.19), channel_id=1, replica_groups=mesh['z'=8,'r'=4,'gz'=8] {'r','gz'}, dimensions={0} | all-to-all | bytes 425984 | tf_op jit(solution)/shard_map/all_to_all | solution.py:576
  50.7 0.0 copy-done
  50.7 3.8 %shard_map.40 = f32[416,128]{1,0:T(8,128)S(1)} custom-call(f32[80,128]{1,0:T(8,128)S(1)} %get-tuple-element.7.h_ref, f32[560,128]{1,0:T(8,128)S(1)} %copy-done, f32[416,128]{1,0:T(8,128)S(1)} %bitcast.14), custom_call_target="tpu_custom_call" | custom-call | tf_op jit(solution)/shard_map/pallas_call | solution.py:588
  54.5 12.1 %all_to_all.33 = f32[32,13,1,128]{3,2,1,0:T(1,128)S(1)} all-to-all(f32[32,13,1,128]{3,2,1,0:T(1,128)S(1)} %bitcast.15), channel_id=1, replica_groups=mesh['z'=8,'r'=4,'gz'=8] {'r','gz'}, dimensions={0} | all-to-all | bytes 425984 | tf_op jit(solution)/shard_map/all_to_all | solution.py:576
  66.6 0.4 shard_map.41
  67.0 13.2 %all_to_all.34 = f32[8,52,1,128]{3,2,1,0:T(1,128)S(1)} all-to-all(f32[8,52,1,128]{3,2,1,0:T(1,128)S(1)} %bitcast.21), channel_id=1, replica_groups=mesh['z'=8,'r'=4,'gz'=8] {'z'}, dimensions={0} | all-to-all | bytes 425984 | tf_op jit(solution)/shard_map/all_to_all | solution.py:581
  80.3 0.1 shard_map.42
  80.4 12.6 %all_to_all.35 = f32[32,13,1,128]{3,2,1,0:T(1,128)S(1)} all-to-all(f32[32,13,1,128]{3,2,1,0:T(1,128)S(1)} %bitcast.23), channel_id=1, replica_groups=mesh['z'=8,'r'=4,'gz'=8] {'r','gz'}, dimensions={0} | all-to-all | bytes 425984 | tf_op jit(solution)/shard_map/all_to_all | solution.py:576
  93.1 0.8 shard_map.43
Async XLA Ops:
  0.0 0.7 copy-start.2
  0.7 0.9 copy-start.1
  36.9 13.9 %copy-start = (f32[560,128]{1,0:T(8,128)S(1)}, f32[560,128]{1,0:T(8,128)}, u32[]{:S(2)}) copy-start(f32[560,128]{1,0:T(8,128)} %constant.2.clone.mats_ref) | copy-start | bytes 860164

commit v3 on v2

--- a/solution.py
+++ b/solution.py
@@ -173,6 +173,8 @@
     return 1.0 / centre, steps
 
 
+FLOW, SPAN = ("zh", "z0", "xh", "core"), ("xl", "y")
+LAST = ("xl", "y", "z0", "core")
 SLAB = 13
 FIELD = 32 * SLAB
 USED = 8 * 49
@@ -237,10 +239,15 @@
     ref[n * SLAB : n * SLAB + SLAB, :] = v
 
 
+def span_mode():
+    return lax.axis_index("zh") * 2 + lax.axis_index("xh")
+
+
 def span_forward_kernel(x_ref, o_ref):
     first, sign = lane_tools()
-    for r in range(4):
-        x = [plane(x_ref, 8 * r + j) for j in range(8)]
+    for z0, core in ((0, 0), (0, 1), (1, 0), (1, 1)):
+        x = [plane(x_ref, 4 * j + 2 * z0 + core) for j in range(8)]
+        at = [4 * (k // 2 * 2 + z0) + 2 * (k % 2) + core for k in range(8)]
         s = [None] + [x[j] + x[8 - j] for j in (1, 2, 3)]
         d = [None] + [x[j] - x[8 - j] for j in (1, 2, 3)]
         up, down = x[0] + x[4], x[0] - x[4]
@@ -249,21 +256,21 @@
         re = [up + s[2] + odd, down + turn, up - s[2], down - turn, up + s[2] - odd]
         im = [None, -slope - d[2], d[3] - d[1], d[2] - slope]
         flip = swap(re[0])
-        put(o_ref, r, jnp.where(first, re[0] + flip, flip - re[0]))
-        put(o_ref, 16 + r, sign * re[4])
+        put(o_ref, at[0], jnp.where(first, re[0] + flip, flip - re[0]))
+        put(o_ref, at[4], sign * re[4])
         for f in (1, 2, 3):
             c, t = float(np.cos(np.pi * f / 8)), float(np.sin(np.pi * f / 8))
             re_swap, im_swap = swap(re[f]), swap(im[f])
             base = jnp.where(first, re[f], im_swap)
             extra = c * jnp.where(first, re_swap, im[f]) + t * jnp.where(first, im_swap, -re[f])
-            put(o_ref, 4 * f + r, base + extra)
-            put(o_ref, 4 * (8 - f) + r, sign * (base - extra))
+            put(o_ref, at[f], base + extra)
+            put(o_ref, at[8 - f], sign * (base - extra))
 
 
 def span_backward_kernel(x_ref, o_ref):
     first, sign = lane_tools()
-    for r in range(4):
-        v = [plane(x_ref, 4 * k + r) for k in range(8)]
+    for z0, core in ((0, 0), (0, 1), (1, 0), (1, 1)):
+        v = [plane(x_ref, 4 * (k // 2 * 2 + z0) + 2 * (k % 2) + core) for k in range(8)]
         flip = swap(v[0])
         re = [jnp.where(first, v[0] + flip, flip - v[0])]
         im = [None]
@@ -278,11 +285,12 @@
         slope = HALF * (im[1] + im[3])
         c = [up + re[2] + odd, down + turn, up - re[2], down - turn, up + re[2] - odd]
         s = [None, slope + im[2], im[1] - im[3], slope - im[2]]
-        put(o_ref, 8 * r, c[0])
-        put(o_ref, 8 * r + 4, c[4])
+        at = [4 * j + 2 * z0 + core for j in range(8)]
+        put(o_ref, at[0], c[0])
+        put(o_ref, at[4], c[4])
         for j in (1, 2, 3):
-            put(o_ref, 8 * r + j, c[j] - s[j])
-            put(o_ref, 8 * r + 8 - j, c[j] + s[j])
+            put(o_ref, at[j], c[j] - s[j])
+            put(o_ref, at[8 - j], c[j] + s[j])
 
 
 def complex_transform(x, sign, direction):
@@ -311,7 +319,7 @@
     for n, v in enumerate(complex_transform([plane(x_ref, n) for n in range(NX)], sign, 1.0)):
         put(o_ref, n, v)
 
-    @pl.when(lax.axis_index("z") == 0)
+    @pl.when(span_mode() == 0)
     def _():
         w = [plane(o_ref, n) for n in range(NX)]
         put(o_ref, 0, jnp.where(first, w[0], swap(w[16])))
@@ -325,7 +333,7 @@
 def flow_backward_kernel(x_ref, o_ref, w_ref):
     first, sign = lane_tools()
 
-    @pl.when(lax.axis_index("z") == 0)
+    @pl.when(span_mode() == 0)
     def _():
         v = [plane(x_ref, n) for n in range(NX)]
         put(w_ref, 0, jnp.where(first, v[0], swap(v[16])))
@@ -335,7 +343,7 @@
             put(w_ref, n, v[n] - sign * other)
             put(w_ref, NX - n, sign * v[n] + other)
 
-    @pl.when(lax.axis_index("z") > 0)
+    @pl.when(span_mode() > 0)
     def _():
         w_ref[...] = x_ref[...]
 
@@ -413,8 +421,8 @@
     u7, r7, x7, d7, u3, r3, x3, d3,
     square, g7_ref, g3_ref, r7_ref, p7_ref, r3_ref, p3_ref,
 ):
-    n = lax.axis_index("r") * 8 + lax.axis_index("gz")
-    b = lax.axis_index("z")
+    n = lax.axis_index(LAST)
+    b = span_mode()
     at_x = PHASES_AT + 2 * n + jnp.where(b > 0, 64, 0)
     at_z = PHASES_AT + 128 + 2 * jnp.where(b > 0, b, n // 16 * 8)
     cx, sx = mats_ref[pl.ds(at_x, 1), :], mats_ref[pl.ds(at_x + 1, 1), :]
@@ -571,14 +579,10 @@
 FLAT = jax.ShapeDtypeStruct((FIELD, 128), f32)
 
 
-def in_plane(block):
-    block = block.reshape(32, SLAB, 1, 128)
-    return lax.all_to_all(block, ("r", "gz"), 0, 0).reshape(FIELD, 128)
-
-
-def along_z(block):
-    block = block.reshape(8, 4 * SLAB, 1, 128)
-    return lax.all_to_all(block, "z", 0, 0).reshape(FIELD, 128)
+def exchange(block, axes):
+    n = lax.axis_size(axes)
+    block = block.reshape(n, FIELD // n, 1, 128)
+    return lax.all_to_all(block, axes, 0, 0).reshape(FIELD, 128)
 
 
 def cycle_call(heights, modes):
@@ -613,11 +617,11 @@
         scratch_shapes=[pltpu.VMEM((8, 128), f32)],
         compiler_params=PARAMS,
     )(residual, layer_heights.reshape(1, NY))
-    spans = transform(span_forward_kernel, in_plane(packed))
-    modes = in_plane(transform(flow_forward_kernel, along_z(spans)))
-    solved = cycle_call(heights, modes)
-    flows = transform(flow_backward_kernel, in_plane(solved), [pltpu.VMEM((FIELD, 128), f32)])
-    spread = in_plane(transform(span_backward_kernel, along_z(flows)))
+    spans = transform(span_forward_kernel, exchange(packed, SPAN))
+    modes = exchange(transform(flow_forward_kernel, exchange(spans, FLOW)), LAST)
+    solved = exchange(cycle_call(heights, modes), LAST)
+    flows = transform(flow_backward_kernel, solved, [pltpu.VMEM((FIELD, 128), f32)])
+    spread = exchange(transform(span_backward_kernel, exchange(flows, FLOW)), SPAN)
     return pl.pallas_call(
         unpack_kernel, out_shape=jax.ShapeDtypeStruct((7, 14, 512), f32),
         in_specs=[VMEM], out_specs=VMEM, compiler_params=PARAMS,
@@ -625,8 +629,8 @@
 
 
 def solution(mesh):
-    split = Mesh(mesh.devices.reshape(8, 4, 8), ("z", "r", "gz"))
-    spec = P(("z", "r"), "gz", None)
+    split = Mesh(mesh.devices.reshape(4, 2, 2, 2, 2, 4), FLOW + SPAN)
+    spec = P(FLOW, SPAN, None)
     return jax.shard_map(
         body, mesh=split, in_specs=(spec, P()), out_specs=spec, check_vma=False
     )

time: 94.2 us -> 91 us (0.966)
  blocking collectives: 86.4 us -> 83.2 us
    all_to_all x6, blocking collectives: 86.4 us -> 83.2 us  [exchange(): return lax.all_to_all(block, axes, 0, 0).reshape(FIELD, 128)]
where the time goes in v3:
time: 91 us; the launch traced here: 90.7 us
  blocking collectives  83.2 us (91%)
  Pallas kernels  5.82 us (6%)
  local copies, waits for them, and re-layouts  1.6 us (2%)
    all_to_all x6, blocking collectives, exchange(): return lax.all_to_all(block, axes, 0, 0).reshape(FIELD, 128)  83.2 us
    pallas_call x1, Pallas kernels, cycle_call(): pl.pallas_call(cycle_kernel, out_shape=FLAT, in_specs=[VMEM, VMEM, VMEM],...  3.77 us

profile of v3, /device:TPU:1, one launch (start us, length us, event | category | flops | bytes accessed | tf_op | source)
XLA Modules:
  0.0 90.7 jit_solution(13842204321665971116)
XLA Ops:
  0.0 0.0 copy-start.2
  0.0 0.7 copy-done.2
  0.7 0.0 copy-start.1
  0.7 0.9 %copy-done.1 = f32[7,14,512]{2,1,0:T(8,128)S(1)} copy-done((f32[7,14,512]{2,1,0:T(8,128)S(1)}, f32[7,14,512]{2,1,0:T(8,128)}, u32[]{:S(2)}) %copy-start.1) | copy-done | bytes 200728
  1.6 0.2 shard_map.37
  1.8 11.7 %all_to_all.30 = f32[8,52,1,128]{3,2,1,0:T(1,128)S(1)} all-to-all(f32[8,52,1,128]{3,2,1,0:T(1,128)S(1)} %bitcast.24), channel_id=1, replica_groups=mesh['zh'=4,'z0'=2,'xh'=2,'core'=2,'xl'=2,'y'=4] {'xl','y'}, dimensions={0} | all-to-all | bytes 425984 | tf_op jit(solution)/shard_map/all_to_all | solution.py:585
  13.5 0.1 shard_map.38
  13.6 24.7 %all_to_all.31 = f32[32,13,1,128]{3,2,1,0:T(1,128)S(1)} all-to-all(f32[32,13,1,128]{3,2,1,0:T(1,128)S(1)} %bitcast.17), channel_id=1, replica_groups=mesh['zh'=4,'z0'=2,'xh'=2,'core'=2,'xl'=2,'y'=4] {'zh','z0','xh','core'}, dimensions={0} | all-to-all | bytes 425984 | tf_op jit(solution)/shard_map/all_to_all | solution.py:585
  38.3 0.4 shard_map.39
  38.7 0.0 copy-start
  38.7 11.4 %all_to_all.32 = f32[32,13,1,128]{3,2,1,0:T(1,128)S(1)} all-to-all(f32[32,13,1,128]{3,2,1,0:T(1,128)S(1)} %bitcast.19), channel_id=1, replica_groups=mesh['zh'=4,'z0'=2,'xh'=2,'core'=2,'xl'=2,'y'=4] {'xl','y','z0','core'}, dimensions={0} | all-to-all | bytes 425984 | tf_op jit(solution)/shard_map/all_to_all | solution.py:585
  50.2 0.0 copy-done
  50.2 3.8 %shard_map.40 = f32[416,128]{1,0:T(8,128)S(1)} custom-call(f32[80,128]{1,0:T(8,128)S(1)} %get-tuple-element.7.h_ref, f32[560,128]{1,0:T(8,128)S(1)} %copy-done, f32[416,128]{1,0:T(8,128)S(1)} %bitcast.14), custom_call_target="tpu_custom_call" | custom-call | tf_op jit(solution)/shard_map/pallas_call | solution.py:592
  54.0 11.1 %all_to_all.33 = f32[32,13,1,128]{3,2,1,0:T(1,128)S(1)} all-to-all(f32[32,13,1,128]{3,2,1,0:T(1,128)S(1)} %bitcast.15), channel_id=1, replica_groups=mesh['zh'=4,'z0'=2,'xh'=2,'core'=2,'xl'=2,'y'=4] {'xl','y','z0','core'}, dimensions={0} | all-to-all | bytes 425984 | tf_op jit(solution)/shard_map/all_to_all | solution.py:585
  65.1 0.4 shard_map.41
  65.5 15.8 %all_to_all.34 = f32[32,13,1,128]{3,2,1,0:T(1,128)S(1)} all-to-all(f32[32,13,1,128]{3,2,1,0:T(1,128)S(1)} %bitcast.21), channel_id=1, replica_groups=mesh['zh'=4,'z0'=2,'xh'=2,'core'=2,'xl'=2,'y'=4] {'zh','z0','xh','core'}, dimensions={0} | all-to-all | bytes 425984 | tf_op jit(solution)/shard_map/all_to_all | solution.py:585
  81.3 0.1 shard_map.42
  81.5 8.4 %all_to_all.35 = f32[8,52,1,128]{3,2,1,0:T(1,128)S(1)} all-to-all(f32[8,52,1,128]{3,2,1,0:T(1,128)S(1)} %bitcast.23), channel_id=1, replica_groups=mesh['zh'=4,'z0'=2,'xh'=2,'core'=2,'xl'=2,'y'=4] {'xl','y'}, dimensions={0} | all-to-all | bytes 425984 | tf_op jit(solution)/shard_map/all_to_all | solution.py:585
  89.9 0.8 shard_map.43
Async XLA Ops:
  0.0 0.7 copy-start.2
  0.7 0.9 %copy-start.1 = (f32[7,14,512]{2,1,0:T(8,128)S(1)}, f32[7,14,512]{2,1,0:T(8,128)}, u32[]{:S(2)}) copy-start(f32[7,14,512]{2,1,0:T(8,128)} %x_ref.1) | copy-start | bytes 602116
  38.7 11.5 %copy-start = (f32[560,128]{1,0:T(8,128)S(1)}, f32[560,128]{1,0:T(8,128)}, u32[]{:S(2)}) copy-start(f32[560,128]{1,0:T(8,128)} %constant.2.clone.mats_ref) | copy-start | bytes 860164

commit v4 on v3

--- a/solution.py
+++ b/solution.py
@@ -175,6 +175,7 @@
 
 FLOW, SPAN = ("zh", "z0", "xh", "core"), ("xl", "y")
 LAST = ("xl", "y", "z0", "core")
+ORDER = ("zh", "z0", "xh", "core")
 SLAB = 13
 FIELD = 32 * SLAB
 USED = 8 * 49
@@ -188,9 +189,18 @@
     return jnp.where(first, v, swap(w)), jnp.where(first, swap(v), w)
 
 
-def pack_kernel(x_ref, h_ref, o_ref, rows_ref, line_ref):
+def pack_kernel(x_hbm, h_hbm, o_ref, rows_ref, x_ref, h_ref, line_ref, sems):
+    line = pltpu.make_async_copy(h_hbm, h_ref, sems.at[0])
+    line.start()
+    field = pltpu.make_async_copy(x_hbm, x_ref, sems.at[1])
+    field.start()
     first, _ = lane_tools()
     o_ref[USED:, :] = jnp.zeros((FIELD - USED, 128), f32)
+    line_ref[...] = jnp.zeros_like(line_ref)
+    line.wait()
+    line_ref[0:1, 0:NY] = h_ref[...]
+    rows_ref[...] = jnp.broadcast_to(line_ref[0:1, :], (128, 128)).T[:ROWS]
+    field.wait()
     for a in range(7):
         for t in range(4):
             part = slice(128 * t, 128 * t + 128)
@@ -198,9 +208,6 @@
             r = 98 * t + 7 * a
             o_ref[r : r + 7, :] = low
             o_ref[r + 49 : r + 56, :] = high
-    line_ref[...] = jnp.zeros_like(line_ref)
-    line_ref[0:1, 0:NY] = h_ref[...]
-    rows_ref[...] = jnp.broadcast_to(line_ref[0:1, :], (128, 128)).T[:ROWS]
 
 
 def unpack_kernel(x_ref, o_ref):
@@ -239,6 +246,14 @@
     ref[n * SLAB : n * SLAB + SLAB, :] = v
 
 
+def flow_place(n):
+    bits = {"zh": n // 8, "z0": n // 4 % 2, "xh": n // 2 % 2, "core": n % 2}
+    place = 0
+    for name in ORDER:
+        place = place * (4 if name == "zh" else 2) + bits[name]
+    return place
+
+
 def span_mode():
     return lax.axis_index("zh") * 2 + lax.axis_index("xh")
 
@@ -247,7 +262,7 @@
     first, sign = lane_tools()
     for z0, core in ((0, 0), (0, 1), (1, 0), (1, 1)):
         x = [plane(x_ref, 4 * j + 2 * z0 + core) for j in range(8)]
-        at = [4 * (k // 2 * 2 + z0) + 2 * (k % 2) + core for k in range(8)]
+        at = [flow_place(4 * (k // 2 * 2 + z0) + 2 * (k % 2) + core) for k in range(8)]
         s = [None] + [x[j] + x[8 - j] for j in (1, 2, 3)]
         d = [None] + [x[j] - x[8 - j] for j in (1, 2, 3)]
         up, down = x[0] + x[4], x[0] - x[4]
@@ -270,7 +285,7 @@
 def span_backward_kernel(x_ref, o_ref):
     first, sign = lane_tools()
     for z0, core in ((0, 0), (0, 1), (1, 0), (1, 1)):
-        v = [plane(x_ref, 4 * (k // 2 * 2 + z0) + 2 * (k % 2) + core) for k in range(8)]
+        v = [plane(x_ref, flow_place(4 * (k // 2 * 2 + z0) + 2 * (k % 2) + core)) for k in range(8)]
         flip = swap(v[0])
         re = [jnp.where(first, v[0] + flip, flip - v[0])]
         im = [None]
@@ -316,7 +331,7 @@
 
 def flow_forward_kernel(x_ref, o_ref):
     first, sign = lane_tools()
-    for n, v in enumerate(complex_transform([plane(x_ref, n) for n in range(NX)], sign, 1.0)):
+    for n, v in enumerate(complex_transform([plane(x_ref, flow_place(n)) for n in range(NX)], sign, 1.0)):
         put(o_ref, n, v)
 
     @pl.when(span_mode() == 0)
@@ -348,7 +363,7 @@
         w_ref[...] = x_ref[...]
 
     for n, v in enumerate(complex_transform([plane(w_ref, n) for n in range(NX)], sign, -1.0)):
-        put(o_ref, n, v)
+        put(o_ref, flow_place(n), v)
 
 
 def table_product(v, t_ref):
@@ -575,6 +590,7 @@
 
 
 VMEM = pl.BlockSpec(memory_space=pltpu.VMEM)
+HBM = pl.BlockSpec(memory_space=pltpu.HBM)
 PARAMS = pltpu.CompilerParams(vmem_limit_bytes=32 * 1024 * 1024)
 FLAT = jax.ShapeDtypeStruct((FIELD, 128), f32)
 
@@ -611,17 +627,21 @@
 
 
 def body(residual, layer_heights):
+    stay = lambda v: pltpu.with_memory_space_constraint(v, pltpu.HBM)
     packed, heights = pl.pallas_call(
         pack_kernel, out_shape=(FLAT, jax.ShapeDtypeStruct((ROWS, 128), f32)),
-        in_specs=[VMEM, VMEM], out_specs=(VMEM, VMEM),
-        scratch_shapes=[pltpu.VMEM((8, 128), f32)],
+        in_specs=[HBM, HBM], out_specs=(VMEM, VMEM),
+        scratch_shapes=[
+            pltpu.VMEM((7, 14, 512), f32), pltpu.VMEM((1, NY), f32), pltpu.VMEM((8, 128), f32),
+            pltpu.SemaphoreType.DMA((2,)),
+        ],
         compiler_params=PARAMS,
-    )(residual, layer_heights.reshape(1, NY))
+    )(stay(residual), stay(layer_heights.reshape(1, NY)))
     spans = transform(span_forward_kernel, exchange(packed, SPAN))
-    modes = exchange(transform(flow_forward_kernel, exchange(spans, FLOW)), LAST)
+    modes = exchange(transform(flow_forward_kernel, exchange(spans, ORDER)), LAST)
     solved = exchange(cycle_call(heights, modes), LAST)
     flows = transform(flow_backward_kernel, solved, [pltpu.VMEM((FIELD, 128), f32)])
-    spread = exchange(transform(span_backward_kernel, exchange(flows, FLOW)), SPAN)
+    spread = exchange(transform(span_backward_kernel, exchange(flows, ORDER)), SPAN)
     return pl.pallas_call(
         unpack_kernel, out_shape=jax.ShapeDtypeStruct((7, 14, 512), f32),
         in_specs=[VMEM], out_specs=VMEM, compiler_params=PARAMS,

time: 91 us -> 90.4 us (level)
  local copies, waits for them, and re-layouts: 1.6 us -> 0.01 us
  Pallas kernels: 5.82 us -> 6.76 us
    unnamed x6 -> x2, local copies, waits for them, and re-layouts: 1.6 us -> 0.01 us
    pallas_call x1, Pallas kernels: 0.16 us -> 1.1 us  [body(): pl.pallas_call(pack_kernel, out_shape=(FLAT, jax.ShapeDtypeStruct((ROWS,...]
where the time goes in v4:
time: 90.4 us; the launch traced here: 90.1 us
  blocking collectives  83.2 us (92%)
  Pallas kernels  6.76 us (7%)
    all_to_all x6, blocking collectives, exchange(): return lax.all_to_all(block, axes, 0, 0).reshape(FIELD, 128)  83.2 us
    pallas_call x1, Pallas kernels, cycle_call(): pl.pallas_call(cycle_kernel, out_shape=FLAT, in_specs=[VMEM, VMEM, VMEM],...  3.77 us

profile of v4, /device:TPU:1, one launch (start us, length us, event | category | flops | bytes accessed | tf_op | source)
XLA Modules:
  0.0 90.1 jit_solution(9699933908647053722)
XLA Ops:
  0.0 1.1 %shard_map.37 = (f32[416,128]{1,0:T(8,128)S(1)}, f32[80,128]{1,0:T(8,128)S(1)}) custom-call(f32[7,14,512]{2,1,0:T(8,128)} %x_hbm.1, f32[1,73]{1,0:T(1,128)} %bitcast.25), custom_call_target="tpu_custom_call" | custom-call | tf_op jit(solution)/shard_map/pallas_call | solution.py:631
  1.1 11.7 %all_to_all.30 = f32[8,52,1,128]{3,2,1,0:T(1,128)S(1)} all-to-all(f32[8,52,1,128]{3,2,1,0:T(1,128)S(1)} %bitcast.24), channel_id=1, replica_groups=mesh['zh'=4,'z0'=2,'xh'=2,'core'=2,'xl'=2,'y'=4] {'xl','y'}, dimensions={0} | all-to-all | bytes 425984 | tf_op jit(solution)/shard_map/all_to_all | solution.py:601
  12.8 0.1 shard_map.38
  13.0 24.7 %all_to_all.31 = f32[32,13,1,128]{3,2,1,0:T(1,128)S(1)} all-to-all(f32[32,13,1,128]{3,2,1,0:T(1,128)S(1)} %bitcast.17), channel_id=1, replica_groups=mesh['zh'=4,'z0'=2,'xh'=2,'core'=2,'xl'=2,'y'=4] {'zh','z0','xh','core'}, dimensions={0} | all-to-all | bytes 425984 | tf_op jit(solution)/shard_map/all_to_all | solution.py:601
  37.7 0.4 shard_map.39
  38.1 0.0 copy-start
  38.1 11.4 %all_to_all.32 = f32[32,13,1,128]{3,2,1,0:T(1,128)S(1)} all-to-all(f32[32,13,1,128]{3,2,1,0:T(1,128)S(1)} %bitcast.19), channel_id=1, replica_groups=mesh['zh'=4,'z0'=2,'xh'=2,'core'=2,'xl'=2,'y'=4] {'xl','y','z0','core'}, dimensions={0} | all-to-all | bytes 425984 | tf_op jit(solution)/shard_map/all_to_all | solution.py:601
  49.5 0.0 copy-done
  49.6 3.8 %shard_map.40 = f32[416,128]{1,0:T(8,128)S(1)} custom-call(f32[80,128]{1,0:T(8,128)S(1)} %get-tuple-element.7.h_ref, f32[560,128]{1,0:T(8,128)S(1)} %copy-done, f32[416,128]{1,0:T(8,128)S(1)} %bitcast.14), custom_call_target="tpu_custom_call" | custom-call | tf_op jit(solution)/shard_map/pallas_call | solution.py:608
  53.3 11.1 %all_to_all.33 = f32[32,13,1,128]{3,2,1,0:T(1,128)S(1)} all-to-all(f32[32,13,1,128]{3,2,1,0:T(1,128)S(1)} %bitcast.15), channel_id=1, replica_groups=mesh['zh'=4,'z0'=2,'xh'=2,'core'=2,'xl'=2,'y'=4] {'xl','y','z0','core'}, dimensions={0} | all-to-all | bytes 425984 | tf_op jit(solution)/shard_map/all_to_all | solution.py:601
  64.5 0.4 shard_map.41
  64.9 15.8 %all_to_all.34 = f32[32,13,1,128]{3,2,1,0:T(1,128)S(1)} all-to-all(f32[32,13,1,128]{3,2,1,0:T(1,128)S(1)} %bitcast.21), channel_id=1, replica_groups=mesh['zh'=4,'z0'=2,'xh'=2,'core'=2,'xl'=2,'y'=4] {'zh','z0','xh','core'}, dimensions={0} | all-to-all | bytes 425984 | tf_op jit(solution)/shard_map/all_to_all | solution.py:601
  80.7 0.1 shard_map.42
  80.8 8.4 %all_to_all.35 = f32[8,52,1,128]{3,2,1,0:T(1,128)S(1)} all-to-all(f32[8,52,1,128]{3,2,1,0:T(1,128)S(1)} %bitcast.23), channel_id=1, replica_groups=mesh['zh'=4,'z0'=2,'xh'=2,'core'=2,'xl'=2,'y'=4] {'xl','y'}, dimensions={0} | all-to-all | bytes 425984 | tf_op jit(solution)/shard_map/all_to_all | solution.py:601
  89.2 0.8 shard_map.43
Async XLA Ops:
  38.1 11.5 %copy-start = (f32[560,128]{1,0:T(8,128)S(1)}, f32[560,128]{1,0:T(8,128)}, u32[]{:S(2)}) copy-start(f32[560,128]{1,0:T(8,128)} %constant.2.clone.mats_ref) | copy-start | bytes 860164

commit v5 on v4

--- a/solution.py
+++ b/solution.py
@@ -60,17 +60,52 @@
     return lagrange
 
 
+def lane_at(a, b):
+    n = 7 * b + a
+    return n if n < 25 else n + 7
+
+
 def lanes_of(values):
     n = values.shape[0]
-    out = np.zeros((7, 7))
-    out[:n, :n] = values
-    return np.pad(out.reshape(49), (0, 15))
+    out = np.zeros(64)
+    for a in range(n):
+        for b in range(n):
+            out[lane_at(a, b)] = values[a, b]
+    return out
 
 
 def square_of(matrix, n_out, n_in):
-    out = np.zeros((7, 7, 7, 7))
-    out[:n_out, :n_out, :n_in, :n_in] = matrix.reshape(n_out, n_out, n_in, n_in)
-    return np.pad(out.reshape(49, 49), ((0, 15), (0, 15)))
+    rows = [lane_at(a, b) for a in range(n_out) for b in range(n_out)]
+    columns = [lane_at(a, b) for a in range(n_in) for b in range(n_in)]
+    out = np.zeros((64, 64))
+    out[np.ix_(rows, columns)] = matrix
+    return out
+
+
+def line_basis(q, t):
+    u = np.zeros((q, q), complex)
+    u[0, 0] = 1.0
+    turn = np.exp(-0.5j * t) / np.sqrt(2.0)
+    for a in range(1, (q + 1) // 2):
+        u[a, a] = u[a, q - a] = turn
+        u[q - a, a], u[q - a, q - a] = -1j * turn, 1j * turn
+    return u
+
+
+def closing(q, t):
+    out = np.eye(q + 1, q, dtype=complex)
+    out[q, 0] = np.exp(1j * t)
+    return out
+
+
+def real_parts(matrix_of, count):
+    angles = 0.3 + 0.7 * np.arange(8)
+    terms = np.stack([np.ones(8), np.cos(angles / 2), np.sin(angles / 2), np.cos(angles)], 1)[:, :count]
+    values = np.stack([matrix_of(t) for t in angles])
+    flat = values.reshape(8, -1)
+    parts = np.linalg.lstsq(terms, flat.real, rcond=None)[0]
+    assert np.abs(terms @ parts - flat).max() < 1e-11 * np.abs(flat).max()
+    return parts.reshape((count,) + values.shape[1:])
 
 
 class Level:
@@ -95,13 +130,15 @@
         dm = np.diag(mass)
         scale = np.concatenate([lanes_of(1.0 / self.mxz)] * 2)[None, :]
         sq = lambda m: square_of(m, q, q)
-        fixed = sq(np.kron(base, dm) + np.kron(dm, base) + screen_shift * np.kron(dm, dm))
+        span = real_parts(
+            lambda t: line_basis(q, t) @ closing(q, t).conj().T @ (2.0 * s) @ closing(q, t) @ line_basis(q, t).conj().T, 4
+        )
+        fixed = sq(np.kron(base, dm) + np.kron(dm, span[0]) + screen_shift * np.kron(dm, dm))
         tables = [np.hstack([fixed, 0.0 * fixed])]
-        for c, n in (
-            (np.kron(even, dm), np.kron(odd, dm)),
-            (np.kron(dm, even), np.kron(dm, odd)),
-        ):
-            tables.append(np.hstack([sq(c), -sq(n)]))
+        tables.append(np.hstack([sq(np.kron(even, dm)), -sq(np.kron(odd, dm))]))
+        for part in span[1:]:
+            part = sq(np.kron(dm, part))
+            tables.append(np.hstack([part, 0.0 * part]))
         self.tables = [(t * scale)[: 64 if q > 3 else 24] for t in tables]
         self.weight = 0.5 * w
         self.stiff = s / self.weight[:, None]
@@ -116,28 +153,31 @@
     ja = j[:fine, :coarse]
     jb = np.zeros((fine, coarse))
     jb[:, 0] = j[:fine, coarse]
+    span = real_parts(
+        lambda t: line_basis(fine, t) @ j[:fine] @ closing(coarse, t) @ line_basis(coarse, t).conj().T, 3
+    )
     tables = []
-    for n, b in enumerate((np.kron(ja, ja), np.kron(jb, ja), np.kron(ja, jb), np.kron(jb, jb))):
-        b = square_of(b, fine, coarse).T[: 24 if coarse > 1 else 8]
-        tables.append(np.hstack([b, b if n else 0.0 * b]))
+    for part in span:
+        for flow in (ja, jb):
+            b = square_of(np.kron(flow, part), fine, coarse).T[: 24 if coarse > 1 else 8]
+            tables.append(np.hstack([b, b if flow is jb else 0.0 * b]))
     return j, tables
 
 
 def phase_rows():
-    rows = np.zeros((152, 2, 64))
-    for n in range(NX):
+    rows = np.zeros((80, 2, 64))
+    for n in range(16):
         t = 2 * np.pi * n / NX
-        rows[64 + 2 * n], rows[65 + 2 * n] = np.cos(t), np.sin(t)
-        k = n % 16
-        t = 2 * np.pi * k / NX
-        if k:
+        if n:
             rows[2 * n], rows[2 * n + 1] = np.cos(t), np.sin(t)
         else:
-            rows[2 * n, 0], rows[2 * n, 1] = 1.0, -1.0
-    for k in range(9):
-        t = 2 * np.pi * k / NZ
-        rows[128 + 2 * k], rows[129 + 2 * k] = np.cos(t), np.sin(t) if k % 8 else 0.0
-    return rows.reshape(152, 128)
+            rows[0, 0], rows[0, 1] = 1.0, -1.0
+    for k in range(8):
+        for part in range(2):
+            t = 2 * np.pi * k / NZ if k else np.pi * part
+            at = 32 + 3 * (2 * k + part)
+            rows[at], rows[at + 1], rows[at + 2] = np.cos(t / 2), np.sin(t / 2), np.cos(t)
+    return rows.reshape(80, 128)
 
 
 FINE, MID, LOW = Level(7), Level(3), Level(1)
@@ -146,7 +186,7 @@
 MATRICES = np.concatenate(FINE.tables + MID.tables + P7_TABLES + P3_TABLES).astype(np.float32)
 R7 = FINE.weight[:, None] * J7 / MID.weight
 R3 = MID.weight[:, None] * J3 / LOW.weight
-G7_AT, G3_AT, P7_AT, P3_AT = 0, 192, 264, 360
+G7_AT, G3_AT, P7_AT, P3_AT = 0, 320, 440, 584
 
 
 LANES = np.zeros((16, 128))
@@ -157,7 +197,7 @@
     LANES[4 * n + 3] = level.mask_lanes
 LANES[8] = LOW.mask_lanes
 MATRICES = np.concatenate([MATRICES, LANES, phase_rows()]).astype(np.float32)
-LANES_AT, PHASES_AT = 392, 408
+LANES_AT, PHASES_AT = 632, 648
 
 
 def cheb_steps(bound, sweeps, floor):
@@ -174,11 +214,10 @@
 
 
 FLOW, SPAN = ("zh", "z0", "xh", "core"), ("xl", "y")
-LAST = ("xl", "y", "z0", "core")
-ORDER = ("zh", "z0", "xh", "core")
+LAST = ("xl", "y", "core")
+USED = 8 * 49
 SLAB = 13
 FIELD = 32 * SLAB
-USED = 8 * 49
 
 
 def swap(v):
@@ -195,7 +234,6 @@
     field = pltpu.make_async_copy(x_hbm, x_ref, sems.at[1])
     field.start()
     first, _ = lane_tools()
-    o_ref[USED:, :] = jnp.zeros((FIELD - USED, 128), f32)
     line_ref[...] = jnp.zeros_like(line_ref)
     line.wait()
     line_ref[0:1, 0:NY] = h_ref[...]
@@ -205,9 +243,8 @@
         for t in range(4):
             part = slice(128 * t, 128 * t + 128)
             low, high = mix(first, x_ref[a, 0:7, part], x_ref[a, 7:14, part])
-            r = 98 * t + 7 * a
-            o_ref[r : r + 7, :] = low
-            o_ref[r + 49 : r + 56, :] = high
+            o_ref[pl.ds(98 * t + a, 7, stride=7), :] = low
+            o_ref[pl.ds(98 * t + 49 + a, 7, stride=7), :] = high
 
 
 def unpack_kernel(x_ref, o_ref):
@@ -215,8 +252,11 @@
     for a in range(7):
         for t in range(4):
             part = slice(128 * t, 128 * t + 128)
-            r = 98 * t + 7 * a
-            low, high = mix(first, x_ref[r : r + 7, :], x_ref[r + 49 : r + 56, :])
+            low, high = mix(
+                first,
+                x_ref[pl.ds(98 * t + a, 7, stride=7), :],
+                x_ref[pl.ds(98 * t + 49 + a, 7, stride=7), :],
+            )
             o_ref[a, 0:7, part] = low
             o_ref[a, 7:14, part] = high
 
@@ -238,132 +278,159 @@
     return first, jnp.where(first, 1.0, -1.0).astype(f32)
 
 
-def plane(ref, n):
-    return ref[n * SLAB : n * SLAB + SLAB, :]
-
-
-def put(ref, n, v):
-    ref[n * SLAB : n * SLAB + SLAB, :] = v
-
-
-def flow_place(n):
-    bits = {"zh": n // 8, "z0": n // 4 % 2, "xh": n // 2 % 2, "core": n % 2}
-    place = 0
-    for name in ORDER:
-        place = place * (4 if name == "zh" else 2) + bits[name]
-    return place
-
-
-def span_mode():
-    return lax.axis_index("zh") * 2 + lax.axis_index("xh")
-
-
-def span_forward_kernel(x_ref, o_ref):
+def turned(v, sign, angle, size):
+    c, s = float(size * np.cos(angle)), float(size * np.sin(angle))
+    return c * v + (s * sign) * swap(v)
+
+
+def span_modes(x, first, sign):
+    s = [None] + [x[j] + x[8 - j] for j in (1, 2, 3)]
+    d = [None] + [x[j] - x[8 - j] for j in (1, 2, 3)]
+    up, down = x[0] + x[4], x[0] - x[4]
+    odd, turn = s[1] + s[3], HALF * (s[1] - s[3])
+    slope = HALF * (d[1] + d[3])
+    re = [up + s[2] + odd, down + turn, up - s[2], down - turn, up + s[2] - odd]
+    im = [None, -slope - d[2], d[3] - d[1], d[2] - slope]
+    flip = swap(re[0])
+    out = [None] * 8
+    out[0] = jnp.where(first, re[0] + flip, flip - re[0])
+    out[4] = sign * re[4]
+    for f in (1, 2, 3):
+        c, t = float(np.cos(np.pi * f / 8)), float(np.sin(np.pi * f / 8))
+        re_swap, im_swap = swap(re[f]), swap(im[f])
+        base = jnp.where(first, re[f], im_swap)
+        extra = c * jnp.where(first, re_swap, im[f]) + t * jnp.where(first, im_swap, -re[f])
+        out[f] = base + extra
+        out[8 - f] = sign * (base - extra)
+    return out
+
+
+def span_elements(v, first, sign):
+    flip = swap(v[0])
+    re = [jnp.where(first, v[0] + flip, flip - v[0])]
+    im = [None]
+    for f in (1, 2, 3):
+        c, t = float(np.cos(np.pi * f / 8)), float(np.sin(np.pi * f / 8))
+        total, other = v[f] + v[8 - f], swap(v[f] - v[8 - f])
+        re.append(2.0 * jnp.where(first, total, c * other - t * total))
+        im.append(2.0 * jnp.where(first, other, t * other + c * total))
+    re.append((2.0 * sign) * v[4])
+    up, down = re[0] + re[4], re[0] - re[4]
+    odd, turn = re[1] + re[3], HALF * (re[1] - re[3])
+    slope = HALF * (im[1] + im[3])
+    c = [up + re[2] + odd, down + turn, up - re[2], down - turn, up + re[2] - odd]
+    s = [None, slope + im[2], im[1] - im[3], slope - im[2]]
+    return [c[0]] + [c[j] - s[j] for j in (1, 2, 3)] + [c[4]] + [c[j] + s[j] for j in (3, 2, 1)]
+
+
+def mode_rows(k, part):
+    return 26 * (4 * (k // 2) + 2 * part + k % 2)
+
+
+def span_forward_kernel(x_ref, o_ref, v_ref):
     first, sign = lane_tools()
-    for z0, core in ((0, 0), (0, 1), (1, 0), (1, 1)):
-        x = [plane(x_ref, 4 * j + 2 * z0 + core) for j in range(8)]
-        at = [flow_place(4 * (k // 2 * 2 + z0) + 2 * (k % 2) + core) for k in range(8)]
-        s = [None] + [x[j] + x[8 - j] for j in (1, 2, 3)]
-        d = [None] + [x[j] - x[8 - j] for j in (1, 2, 3)]
-        up, down = x[0] + x[4], x[0] - x[4]
-        odd, turn = s[1] + s[3], HALF * (s[1] - s[3])
-        slope = HALF * (d[1] + d[3])
-        re = [up + s[2] + odd, down + turn, up - s[2], down - turn, up + s[2] - odd]
-        im = [None, -slope - d[2], d[3] - d[1], d[2] - slope]
-        flip = swap(re[0])
-        put(o_ref, at[0], jnp.where(first, re[0] + flip, flip - re[0]))
-        put(o_ref, at[4], sign * re[4])
-        for f in (1, 2, 3):
-            c, t = float(np.cos(np.pi * f / 8)), float(np.sin(np.pi * f / 8))
-            re_swap, im_swap = swap(re[f]), swap(im[f])
-            base = jnp.where(first, re[f], im_swap)
-            extra = c * jnp.where(first, re_swap, im[f]) + t * jnp.where(first, im_swap, -re[f])
-            put(o_ref, at[f], base + extra)
-            put(o_ref, at[8 - f], sign * (base - extra))
-
-
-def span_backward_kernel(x_ref, o_ref):
+    for k in range(8):
+        v_ref[k, 48:56] = jnp.zeros((8, 128), f32)
+    nodes = lambda b: [x_ref[49 * j + 7 * b : 49 * j + 7 * b + 7, :] for j in range(8)]
+    for k, v in enumerate(span_modes(nodes(0), first, sign)):
+        v_ref[k, 0:7] = v
+    for b in (1, 2, 3):
+        near, far = nodes(b), nodes(7 - b)
+        total = span_modes([p + q for p, q in zip(near, far)], first, sign)
+        differ = span_modes([p - q for p, q in zip(near, far)], first, sign)
+        for k in range(8):
+            t = np.pi * k / NZ
+            at, end = 7 * b, 7 * (7 - b)
+            v_ref[k, at : at + 7] = turned(total[k], sign, t, HALF) if k else HALF * total[k]
+            v_ref[k, end : end + 7] = turned(differ[k], sign, t + np.pi / 2, HALF) if k else -HALF * differ[k]
+    for k in range(8):
+        re, im = mix(first, v_ref[k, 0:26], v_ref[k, 25:51])
+        o_ref[mode_rows(k, 0) : mode_rows(k, 0) + 26, :] = re
+        o_ref[mode_rows(k, 1) : mode_rows(k, 1) + 26, :] = im
+
+
+def span_backward_kernel(x_ref, o_ref, v_ref):
     first, sign = lane_tools()
-    for z0, core in ((0, 0), (0, 1), (1, 0), (1, 1)):
-        v = [plane(x_ref, flow_place(4 * (k // 2 * 2 + z0) + 2 * (k % 2) + core)) for k in range(8)]
-        flip = swap(v[0])
-        re = [jnp.where(first, v[0] + flip, flip - v[0])]
-        im = [None]
-        for f in (1, 2, 3):
-            c, t = float(np.cos(np.pi * f / 8)), float(np.sin(np.pi * f / 8))
-            total, other = v[f] + v[8 - f], swap(v[f] - v[8 - f])
-            re.append(2.0 * jnp.where(first, total, c * other - t * total))
-            im.append(2.0 * jnp.where(first, other, t * other + c * total))
-        re.append((2.0 * sign) * v[4])
-        up, down = re[0] + re[4], re[0] - re[4]
-        odd, turn = re[1] + re[3], HALF * (re[1] - re[3])
-        slope = HALF * (im[1] + im[3])
-        c = [up + re[2] + odd, down + turn, up - re[2], down - turn, up + re[2] - odd]
-        s = [None, slope + im[2], im[1] - im[3], slope - im[2]]
-        at = [4 * j + 2 * z0 + core for j in range(8)]
-        put(o_ref, at[0], c[0])
-        put(o_ref, at[4], c[4])
-        for j in (1, 2, 3):
-            put(o_ref, at[j], c[j] - s[j])
-            put(o_ref, at[8 - j], c[j] + s[j])
-
-
-def complex_transform(x, sign, direction):
+    for k in range(8):
+        near, far = mix(
+            first,
+            x_ref[mode_rows(k, 0) : mode_rows(k, 0) + 26, :],
+            x_ref[mode_rows(k, 1) : mode_rows(k, 1) + 26, :],
+        )
+        v_ref[k, 0:25] = near[0:25]
+        v_ref[k, 25:49] = far[0:24]
+
+    def store(b, planes):
+        for j, v in enumerate(planes):
+            o_ref[49 * j + 7 * b : 49 * j + 7 * b + 7, :] = v
+
+    store(0, span_elements([v_ref[k, 0:7] for k in range(8)], first, sign))
+    for b in (1, 2, 3):
+        total, differ = [], []
+        for k in range(8):
+            t = np.pi * k / NZ
+            at, end = 7 * b, 7 * (7 - b)
+            v, w = v_ref[k, at : at + 7], v_ref[k, end : end + 7]
+            total.append(turned(v, sign, -t, HALF) if k else HALF * v)
+            differ.append(turned(w, sign, -t - np.pi / 2, HALF) if k else -HALF * w)
+        total, differ = span_elements(total, first, sign), span_elements(differ, first, sign)
+        store(b, [p + q for p, q in zip(total, differ)])
+        store(7 - b, [p - q for p, q in zip(total, differ)])
+
+
+def line_modes(x):
     n = len(x)
     if n == 1:
-        return x
-    even = complex_transform(x[0::2], sign, direction)
-    odd = complex_transform(x[1::2], sign, direction)
-    low, high = [], []
-    for k in range(n // 2):
-        c = float(np.cos(2 * np.pi * k / n))
-        s = direction * float(np.sin(2 * np.pi * k / n))
-        if k == 0:
-            t = odd[k]
-        elif 4 * k == n:
-            t = (s * sign) * swap(odd[k])
-        else:
-            t = c * odd[k] + (s * sign) * swap(odd[k])
-        low.append(even[k] + t)
-        high.append(even[k] - t)
-    return low + high
+        return [(x[0], None)]
+    even, odd = line_modes(x[0::2]), line_modes(x[1::2])
+    out = [None] * (n // 2 + 1)
+    out[0], out[n // 2] = (even[0][0] + odd[0][0], None), (even[0][0] - odd[0][0], None)
+    for k in range(1, n // 4 + 1):
+        (p, q), (v, w) = even[k], odd[k]
+        if 4 * k == n:
+            out[k] = (p, -v)
+            continue
+        c, s = float(np.cos(2 * np.pi * k / n)), float(np.sin(2 * np.pi * k / n))
+        re, im = c * v + s * w, c * w - s * v
+        out[k], out[n // 2 - k] = (p + re, q + im), (p - re, im - q)
+    return out
+
+
+def line_elements(modes, n):
+    if n == 1:
+        return [modes[0][0]]
+    even, odd = [None] * (n // 4 + 1), [None] * (n // 4 + 1)
+    low, high = modes[0][0], modes[n // 2][0]
+    even[0], odd[0] = (low + high, None), (low - high, None)
+    for k in range(1, n // 4 + 1):
+        (p, q), (v, w) = modes[k], modes[n // 2 - k]
+        if 4 * k == n:
+            even[k], odd[k] = (2.0 * p, None), (-2.0 * q, None)
+            continue
+        c, s = float(np.cos(2 * np.pi * k / n)), float(np.sin(2 * np.pi * k / n))
+        re, im = p - v, q + w
+        even[k], odd[k] = (p + v, q - w), (c * re - s * im, c * im + s * re)
+    x, y = line_elements(even, n // 2), line_elements(odd, n // 2)
+    return [v for pair in zip(x, y) for v in pair]
+
+
+def slab(ref, n):
+    return ref[n * SLAB : n * SLAB + SLAB, :]
 
 
 def flow_forward_kernel(x_ref, o_ref):
-    first, sign = lane_tools()
-    for n, v in enumerate(complex_transform([plane(x_ref, flow_place(n)) for n in range(NX)], sign, 1.0)):
-        put(o_ref, n, v)
-
-    @pl.when(span_mode() == 0)
-    def _():
-        w = [plane(o_ref, n) for n in range(NX)]
-        put(o_ref, 0, jnp.where(first, w[0], swap(w[16])))
-        put(o_ref, 16, jnp.where(first, swap(w[0]), w[16]))
-        for n in range(1, 16):
-            total, differ = w[n] + w[NX - n], w[n] - w[NX - n]
-            put(o_ref, n, 0.5 * jnp.where(first, total, differ))
-            put(o_ref, 16 + n, 0.5 * swap(jnp.where(first, -differ, total)))
-
-
-def flow_backward_kernel(x_ref, o_ref, w_ref):
-    first, sign = lane_tools()
-
-    @pl.when(span_mode() == 0)
-    def _():
-        v = [plane(x_ref, n) for n in range(NX)]
-        put(w_ref, 0, jnp.where(first, v[0], swap(v[16])))
-        put(w_ref, 16, jnp.where(first, swap(v[0]), v[16]))
-        for n in range(1, 16):
-            other = swap(v[16 + n])
-            put(w_ref, n, v[n] - sign * other)
-            put(w_ref, NX - n, sign * v[n] + other)
-
-    @pl.when(span_mode() > 0)
-    def _():
-        w_ref[...] = x_ref[...]
-
-    for n, v in enumerate(complex_transform([plane(w_ref, n) for n in range(NX)], sign, -1.0)):
-        put(o_ref, flow_place(n), v)
+    modes = line_modes([slab(x_ref, n) for n in range(NX)])
+    for n in range(16):
+        re, im = modes[n][0], modes[n][1] if n else modes[16][0]
+        o_ref[26 * n : 26 * n + 13, :] = re
+        o_ref[26 * n + 13 : 26 * n + 26, :] = im
+
+
+def flow_backward_kernel(x_ref, o_ref):
+    modes = [(slab(x_ref, 2 * n), slab(x_ref, 2 * n + 1)) for n in range(16)]
+    modes = [(modes[0][0], None)] + modes[1:] + [(modes[0][1], None)]
+    for n, v in enumerate(line_elements(modes, NX)):
+        o_ref[n * SLAB : n * SLAB + SLAB, :] = v
 
 
 def table_product(v, t_ref):
@@ -430,37 +497,38 @@
     return [weighted_sum(j[k], closed) for k in range(fine)]
 
 
+PIECES = [(y, half, part) for y in range(2) for half in range(2) for part in range(2)]
+
+
 def cycle_kernel(
     h_ref, mats_ref, in_ref, out_ref,
     w_ref, geo_ref,
     u7, r7, x7, d7, u3, r3, x3, d3,
     square, g7_ref, g3_ref, r7_ref, p7_ref, r3_ref, p3_ref,
 ):
-    n = lax.axis_index(LAST)
-    b = span_mode()
-    at_x = PHASES_AT + 2 * n + jnp.where(b > 0, 64, 0)
-    at_z = PHASES_AT + 128 + 2 * jnp.where(b > 0, b, n // 16 * 8)
+    at_x = PHASES_AT + 2 * lax.axis_index(LAST)
+    at_z = PHASES_AT + 32 + 3 * lax.axis_index(("zh", "xh", "z0"))
     cx, sx = mats_ref[pl.ds(at_x, 1), :], mats_ref[pl.ds(at_x + 1, 1), :]
-    cz, sz = mats_ref[pl.ds(at_z, 1), :], mats_ref[pl.ds(at_z + 1, 1), :]
-    cosines = (cx, cz, cx * cz - sx * sz)
-    sines = (sx, sz, sx * cz + cx * sz)
+    ch, sh, cz = (mats_ref[pl.ds(at_z + n, 1), :] for n in range(3))
     lane = lax.broadcasted_iota(jnp.int32, (1, 128), 1)
     first = lane < 64
     mass7, inv7, ratio7, mask7 = (mats_ref[n : n + 1, :] for n in range(LANES_AT, LANES_AT + 4))
     mass3, inv3, ratio3, mask3 = (mats_ref[n : n + 1, :] for n in range(LANES_AT + 4, LANES_AT + 8))
     mask1 = mats_ref[LANES_AT + 8 : LANES_AT + 9, :]
 
-    upper = [jnp.where(first, c, s) for c, s in zip(cosines, sines)]
-    lower = [jnp.where(first, -s, c) for c, s in zip(cosines, sines)]
+    both = (cx, sx)
+    alone = lambda c: (c, jnp.zeros_like(c))
+    operator = [both, alone(ch), alone(sh), alone(cz)]
+    transfer = [both, alone(ch), (cx * ch, sx * ch), alone(sh), (cx * sh, sx * sh)]
 
     def mode_table(at, rows, phases):
         top = mats_ref[at : at + rows]
         low = pltpu.roll(top, 64, axis=1)
-        for n in range(phases):
+        for c, s in phases:
             at += rows
             t = mats_ref[at : at + rows]
-            top = top + upper[n] * t
-            low = low + lower[n] * pltpu.roll(t, 64, axis=1)
+            top = top + jnp.where(first, c, s) * t
+            low = low + jnp.where(first, -s, c) * pltpu.roll(t, 64, axis=1)
         if rows == 64:
             return jnp.concatenate([top, low], axis=0)
         square[...] = jnp.zeros((128, 128), f32)
@@ -468,22 +536,26 @@
         square[64 : 64 + rows] = low
         return square[...]
 
-    store_table(g7_ref, mode_table(G7_AT, 64, 2))
-    store_table(g3_ref, mode_table(G3_AT, 24, 2))
-    table = mode_table(P7_AT, 24, 3)
+    store_table(g7_ref, mode_table(G7_AT, 64, operator))
+    store_table(g3_ref, mode_table(G3_AT, 24, operator))
+    table = mode_table(P7_AT, 24, transfer)
     store_table(p7_ref, table)
     store_table(r7_ref, (table * mass7).T * inv3)
-    table = mode_table(P3_AT, 8, 3)
+    table = mode_table(P3_AT, 8, transfer)
     store_table(p3_ref, table)
     store_table(r3_ref, (table * mass3).T)
 
     scale = inv7 * (1.0 / (NX * NZ))
+    outer = lane % 64 < 32
+    square[...] = jnp.zeros((128, 128), f32)
     for t in range(4):
-        r = 98 * t
-        both = jnp.concatenate([in_ref[r : r + 64, :], in_ref[r + 49 : r + 113, :]], axis=0).T
-        low, high = mix(first, both[:64], both[64:])
-        w_ref[128 * t : 128 * t + 64, :] = low * scale
-        w_ref[128 * t + 64 : 128 * t + 128, :] = high * scale
+        for y, half, part in PIECES:
+            r, v = 64 * part + 32 * y + 13 * half, 52 * (2 * t + y) + 26 * half + 13 * part
+            square[r : r + 13, :] = in_ref[v : v + 13, :]
+        both = square[...].T
+        low, high = both[:64], both[64:]
+        w_ref[128 * t : 128 * t + 64, :] = jnp.where(outer, low, pltpu.roll(high, 32, axis=1)) * scale
+        w_ref[128 * t + 64 : 128 * t + 128, :] = jnp.where(outer, pltpu.roll(low, 96, axis=1), high) * scale
     w_ref[512:, :] = jnp.zeros((w_ref.shape[0] - 512, 128), f32)
     for k in range(7):
         r7[k] = float(1.0 / FINE.weight[k]) * w_ref[pl.ds(k, ROWS, stride=7), :]
@@ -580,25 +652,31 @@
     for k in range(7):
         w_ref[pl.ds(k, ROWS, stride=7), :] = x7[k]
     for t in range(4):
-        r = 98 * t
-        both = jnp.concatenate(
-            mix(first, w_ref[128 * t : 128 * t + 64, :], w_ref[128 * t + 64 : 128 * t + 128, :]), axis=0
+        low, high = w_ref[128 * t : 128 * t + 64, :], w_ref[128 * t + 64 : 128 * t + 128, :]
+        square[...] = jnp.concatenate(
+            [
+                jnp.where(outer, low, pltpu.roll(high, 32, axis=1)),
+                jnp.where(outer, pltpu.roll(low, 96, axis=1), high),
+            ],
+            axis=0,
         ).T
-        out_ref[r : r + 49, :] = both[0:49]
-        out_ref[r + 49 : r + 98, :] = both[64:113]
-    out_ref[USED:, :] = jnp.zeros((FIELD - USED, 128), f32)
+        for y, half, part in PIECES:
+            r, v = 64 * part + 32 * y + 13 * half, 52 * (2 * t + y) + 26 * half + 13 * part
+            out_ref[v : v + 13, :] = square[r : r + 13, :]
 
 
 VMEM = pl.BlockSpec(memory_space=pltpu.VMEM)
 HBM = pl.BlockSpec(memory_space=pltpu.HBM)
 PARAMS = pltpu.CompilerParams(vmem_limit_bytes=32 * 1024 * 1024)
 FLAT = jax.ShapeDtypeStruct((FIELD, 128), f32)
+TIGHT = jax.ShapeDtypeStruct((USED, 128), f32)
+LINES = [pltpu.VMEM((8, 56, 128), f32)]
 
 
 def exchange(block, axes):
-    n = lax.axis_size(axes)
-    block = block.reshape(n, FIELD // n, 1, 128)
-    return lax.all_to_all(block, axes, 0, 0).reshape(FIELD, 128)
+    n, rows = lax.axis_size(axes), block.shape[0]
+    block = block.reshape(n, rows // n, 1, 128)
+    return lax.all_to_all(block, axes, 0, 0).reshape(rows, 128)
 
 
 def cycle_call(heights, modes):
@@ -619,9 +697,9 @@
     )
 
 
-def transform(kernel, block, scratch=()):
+def transform(kernel, block, out_shape=FLAT, scratch=()):
     return pl.pallas_call(
-        kernel, out_shape=FLAT, in_specs=[VMEM], out_specs=VMEM,
+        kernel, out_shape=out_shape, in_specs=[VMEM], out_specs=VMEM,
         scratch_shapes=scratch, compiler_params=PARAMS,
     )(block)
 
@@ -629,7 +707,7 @@
 def body(residual, layer_heights):
     stay = lambda v: pltpu.with_memory_space_constraint(v, pltpu.HBM)
     packed, heights = pl.pallas_call(
-        pack_kernel, out_shape=(FLAT, jax.ShapeDtypeStruct((ROWS, 128), f32)),
+        pack_kernel, out_shape=(TIGHT, jax.ShapeDtypeStruct((ROWS, 128), f32)),
         in_specs=[HBM, HBM], out_specs=(VMEM, VMEM),
         scratch_shapes=[
             pltpu.VMEM((7, 14, 512), f32), pltpu.VMEM((1, NY), f32), pltpu.VMEM((8, 128), f32),
@@ -637,11 +715,11 @@
         ],
         compiler_params=PARAMS,
     )(stay(residual), stay(layer_heights.reshape(1, NY)))
-    spans = transform(span_forward_kernel, exchange(packed, SPAN))
-    modes = exchange(transform(flow_forward_kernel, exchange(spans, ORDER)), LAST)
+    spans = transform(span_forward_kernel, exchange(packed, SPAN), scratch=LINES)
+    modes = exchange(transform(flow_forward_kernel, exchange(spans, FLOW)), LAST)
     solved = exchange(cycle_call(heights, modes), LAST)
-    flows = transform(flow_backward_kernel, solved, [pltpu.VMEM((FIELD, 128), f32)])
-    spread = exchange(transform(span_backward_kernel, exchange(flows, ORDER)), SPAN)
+    flows = exchange(transform(flow_backward_kernel, solved), FLOW)
+    spread = exchange(transform(span_backward_kernel, flows, TIGHT, LINES), SPAN)
     return pl.pallas_call(
         unpack_kernel, out_shape=jax.ShapeDtypeStruct((7, 14, 512), f32),
         in_specs=[VMEM], out_specs=VMEM, compiler_params=PARAMS,

time: 90.4 us -> 87.8 us (0.971)
  blocking collectives: 83.2 us -> 80.8 us
    all_to_all x6, blocking collectives: 83.2 us -> 80.8 us  [exchange(): return lax.all_to_all(block, axes, 0, 0).reshape(rows, 128)]
where the time goes in v5:
time: 87.8 us; the launch traced here: 87.5 us
  blocking collectives  80.8 us (92%)
  Pallas kernels  6.6 us (8%)
    all_to_all x6, blocking collectives, exchange(): return lax.all_to_all(block, axes, 0, 0).reshape(rows, 128)  80.8 us
    pallas_call x1, Pallas kernels, cycle_call(): pl.pallas_call(cycle_kernel, out_shape=FLAT, in_specs=[VMEM, VMEM, VMEM],...  3.88 us

profile of v5, /device:TPU:1, one launch (start us, length us, event | category | flops | bytes accessed | tf_op | source)
XLA Modules:
  0.0 87.5 jit_solution(15759581032058580841)
XLA Ops:
  0.0 1.1 %shard_map.37 = (f32[392,128]{1,0:T(8,128)S(1)}, f32[80,128]{1,0:T(8,128)S(1)}) custom-call(f32[7,14,512]{2,1,0:T(8,128)} %x_hbm.1, f32[1,73]{1,0:T(1,128)} %bitcast.25), custom_call_target="tpu_custom_call" | custom-call | tf_op jit(solution)/shard_map/pallas_call | solution.py:709
  1.1 11.6 %all_to_all.30 = f32[8,49,1,128]{3,2,1,0:T(1,128)S(1)} all-to-all(f32[8,49,1,128]{3,2,1,0:T(1,128)S(1)} %bitcast.24), channel_id=1, replica_groups=mesh['zh'=4,'z0'=2,'xh'=2,'core'=2,'xl'=2,'y'=4] {'xl','y'}, dimensions={0} | all-to-all | bytes 401408 | tf_op jit(solution)/shard_map/all_to_all | solution.py:679
  12.8 0.3 shard_map.38
  13.1 24.7 %all_to_all.31 = f32[32,13,1,128]{3,2,1,0:T(1,128)S(1)} all-to-all(f32[32,13,1,128]{3,2,1,0:T(1,128)S(1)} %bitcast.13), channel_id=1, replica_groups=mesh['zh'=4,'z0'=2,'xh'=2,'core'=2,'xl'=2,'y'=4] {'zh','z0','xh','core'}, dimensions={0} | all-to-all | bytes 425984 | tf_op jit(solution)/shard_map/all_to_all | solution.py:679
  37.8 0.0 copy-start
  37.8 0.1 shard_map.39
  37.9 9.8 %all_to_all.32 = f32[16,26,1,128]{3,2,1,0:T(1,128)S(1)} all-to-all(f32[16,26,1,128]{3,2,1,0:T(1,128)S(1)} %bitcast.18), channel_id=1, replica_groups=mesh['zh'=4,'z0'=2,'xh'=2,'core'=2,'xl'=2,'y'=4] {'xl','y','core'}, dimensions={0} | all-to-all | bytes 425984 | tf_op jit(solution)/shard_map/all_to_all | solution.py:679
  47.7 0.0 copy-done
  47.7 3.9 %shard_map.40 = f32[416,128]{1,0:T(8,128)S(1)} custom-call(f32[80,128]{1,0:T(8,128)S(1)} %get-tuple-element.7.h_ref, f32[728,128]{1,0:T(8,128)S(1)} %copy-done, f32[416,128]{1,0:T(8,128)S(1)} %bitcast.15), custom_call_target="tpu_custom_call" | custom-call | tf_op jit(solution)/shard_map/pallas_call | solution.py:686
  51.6 10.1 %all_to_all.33 = f32[16,26,1,128]{3,2,1,0:T(1,128)S(1)} all-to-all(f32[16,26,1,128]{3,2,1,0:T(1,128)S(1)} %bitcast.16), channel_id=1, replica_groups=mesh['zh'=4,'z0'=2,'xh'=2,'core'=2,'xl'=2,'y'=4] {'xl','y','core'}, dimensions={0} | all-to-all | bytes 425984 | tf_op jit(solution)/shard_map/all_to_all | solution.py:679
  61.7 0.1 shard_map.41
  61.8 16.3 %all_to_all.34 = f32[32,13,1,128]{3,2,1,0:T(1,128)S(1)} all-to-all(f32[32,13,1,128]{3,2,1,0:T(1,128)S(1)} %bitcast.20), channel_id=1, replica_groups=mesh['zh'=4,'z0'=2,'xh'=2,'core'=2,'xl'=2,'y'=4] {'zh','z0','xh','core'}, dimensions={0} | all-to-all | bytes 425984 | tf_op jit(solution)/shard_map/all_to_all | solution.py:679
  78.1 0.3 shard_map.42
  78.4 8.2 %all_to_all.35 = f32[8,49,1,128]{3,2,1,0:T(1,128)S(1)} all-to-all(f32[8,49,1,128]{3,2,1,0:T(1,128)S(1)} %bitcast.22), channel_id=1, replica_groups=mesh['zh'=4,'z0'=2,'xh'=2,'core'=2,'xl'=2,'y'=4] {'xl','y'}, dimensions={0} | all-to-all | bytes 401408 | tf_op jit(solution)/shard_map/all_to_all | solution.py:679
  86.6 0.8 shard_map.43
Async XLA Ops:
  37.8 9.9 %copy-start = (f32[728,128]{1,0:T(8,128)S(1)}, f32[728,128]{1,0:T(8,128)}, u32[]{:S(2)}) copy-start(f32[728,128]{1,0:T(8,128)} %constant.2.clone.mats_ref) | copy-start | bytes 1118212

commit v6 on v5

--- a/solution.py
+++ b/solution.py
@@ -278,12 +278,7 @@
     return first, jnp.where(first, 1.0, -1.0).astype(f32)
 
 
-def turned(v, sign, angle, size):
-    c, s = float(size * np.cos(angle)), float(size * np.sin(angle))
-    return c * v + (s * sign) * swap(v)
-
-
-def span_modes(x, first, sign):
+def span_modes(x, first, sign, offset, size):
     s = [None] + [x[j] + x[8 - j] for j in (1, 2, 3)]
     d = [None] + [x[j] - x[8 - j] for j in (1, 2, 3)]
     up, down = x[0] + x[4], x[0] - x[4]
@@ -291,30 +286,51 @@
     slope = HALF * (d[1] + d[3])
     re = [up + s[2] + odd, down + turn, up - s[2], down - turn, up + s[2] - odd]
     im = [None, -slope - d[2], d[3] - d[1], d[2] - slope]
+
+    def phases(k):
+        t = np.pi * k / 8
+        p = 0.0 if offset is None else t / 2 + offset
+        return [float(size * v) for v in (np.cos(p), np.sin(p), np.cos(p + t), np.sin(p + t))]
+
     flip = swap(re[0])
     out = [None] * 8
     out[0] = jnp.where(first, re[0] + flip, flip - re[0])
-    out[4] = sign * re[4]
+    c, s, v, w = phases(4)
+    out[4] = jnp.where(first, c, -w) * re[4] + jnp.where(first, v, -s) * swap(re[4])
     for f in (1, 2, 3):
-        c, t = float(np.cos(np.pi * f / 8)), float(np.sin(np.pi * f / 8))
         re_swap, im_swap = swap(re[f]), swap(im[f])
-        base = jnp.where(first, re[f], im_swap)
-        extra = c * jnp.where(first, re_swap, im[f]) + t * jnp.where(first, im_swap, -re[f])
-        out[f] = base + extra
-        out[8 - f] = sign * (base - extra)
+        a = jnp.where(first, re[f], im_swap)
+        b = jnp.where(first, im[f], -re_swap)
+        p = jnp.where(first, re_swap, im[f])
+        q = jnp.where(first, im_swap, -re[f])
+        c, s, v, w = phases(f)
+        out[f] = (c * a + v * p) + (s * b + w * q)
+        c, s, v, w = phases(8 - f)
+        out[8 - f] = sign * ((c * a + v * p) - (s * b + w * q))
     return out
 
 
-def span_elements(v, first, sign):
-    flip = swap(v[0])
-    re = [jnp.where(first, v[0] + flip, flip - v[0])]
+def span_elements(x, first, sign, offset, size):
+    def phases(k):
+        t = np.pi * k / 8
+        p = 0.0 if offset is None else t / 2 + offset
+        return [float(size * v) for v in (np.cos(p), np.sin(p), np.cos(p + t), np.sin(p + t))]
+
+    pick = lambda p, q: jnp.where(first, p, q)
+    flip = swap(x[0])
+    re = [jnp.where(first, x[0] + flip, flip - x[0])]
     im = [None]
     for f in (1, 2, 3):
-        c, t = float(np.cos(np.pi * f / 8)), float(np.sin(np.pi * f / 8))
-        total, other = v[f] + v[8 - f], swap(v[f] - v[8 - f])
-        re.append(2.0 * jnp.where(first, total, c * other - t * total))
-        im.append(2.0 * jnp.where(first, other, t * other + c * total))
-    re.append((2.0 * sign) * v[4])
+        c, s, v, w = [2.0 * n for n in phases(f)]
+        near, near_swap = x[f], swap(x[f])
+        one = pick(c, -w) * near + pick(-s, v) * near_swap
+        two = pick(s, v) * near + pick(c, w) * near_swap
+        c, s, v, w = [2.0 * n for n in phases(8 - f)]
+        far, far_swap = x[8 - f], swap(x[8 - f])
+        re.append(one + (pick(c, -w) * far + pick(-s, v) * far_swap))
+        im.append(two - (pick(s, v) * far + pick(c, w) * far_swap))
+    c, s, v, w = [2.0 * n for n in phases(4)]
+    re.append(pick(c, -w) * x[4] + pick(-s, v) * swap(x[4]))
     up, down = re[0] + re[4], re[0] - re[4]
     odd, turn = re[1] + re[3], HALF * (re[1] - re[3])
     slope = HALF * (im[1] + im[3])
@@ -332,17 +348,16 @@
     for k in range(8):
         v_ref[k, 48:56] = jnp.zeros((8, 128), f32)
     nodes = lambda b: [x_ref[49 * j + 7 * b : 49 * j + 7 * b + 7, :] for j in range(8)]
-    for k, v in enumerate(span_modes(nodes(0), first, sign)):
+    for k, v in enumerate(span_modes(nodes(0), first, sign, None, 1.0)):
         v_ref[k, 0:7] = v
     for b in (1, 2, 3):
         near, far = nodes(b), nodes(7 - b)
-        total = span_modes([p + q for p, q in zip(near, far)], first, sign)
-        differ = span_modes([p - q for p, q in zip(near, far)], first, sign)
+        total = span_modes([p + q for p, q in zip(near, far)], first, sign, 0.0, HALF)
+        differ = span_modes([p - q for p, q in zip(near, far)], first, sign, np.pi / 2, HALF)
+        total[0], differ[0] = HALF * total[0], -HALF * differ[0]
         for k in range(8):
-            t = np.pi * k / NZ
-            at, end = 7 * b, 7 * (7 - b)
-            v_ref[k, at : at + 7] = turned(total[k], sign, t, HALF) if k else HALF * total[k]
-            v_ref[k, end : end + 7] = turned(differ[k], sign, t + np.pi / 2, HALF) if k else -HALF * differ[k]
+            v_ref[k, 7 * b : 7 * b + 7] = total[k]
+            v_ref[k, 7 * (7 - b) : 7 * (7 - b) + 7] = differ[k]
     for k in range(8):
         re, im = mix(first, v_ref[k, 0:26], v_ref[k, 25:51])
         o_ref[mode_rows(k, 0) : mode_rows(k, 0) + 26, :] = re
@@ -364,16 +379,13 @@
         for j, v in enumerate(planes):
             o_ref[49 * j + 7 * b : 49 * j + 7 * b + 7, :] = v
 
-    store(0, span_elements([v_ref[k, 0:7] for k in range(8)], first, sign))
+    store(0, span_elements([v_ref[k, 0:7] for k in range(8)], first, sign, None, 1.0))
     for b in (1, 2, 3):
-        total, differ = [], []
-        for k in range(8):
-            t = np.pi * k / NZ
-            at, end = 7 * b, 7 * (7 - b)
-            v, w = v_ref[k, at : at + 7], v_ref[k, end : end + 7]
-            total.append(turned(v, sign, -t, HALF) if k else HALF * v)
-            differ.append(turned(w, sign, -t - np.pi / 2, HALF) if k else -HALF * w)
-        total, differ = span_elements(total, first, sign), span_elements(differ, first, sign)
+        total = [v_ref[k, 7 * b : 7 * b + 7] for k in range(8)]
+        differ = [v_ref[k, 7 * (7 - b) : 7 * (7 - b) + 7] for k in range(8)]
+        total[0], differ[0] = HALF * total[0], -HALF * differ[0]
+        total = span_elements(total, first, sign, 0.0, HALF)
+        differ = span_elements(differ, first, sign, np.pi / 2, HALF)
         store(b, [p + q for p, q in zip(total, differ)])
         store(7 - b, [p - q for p, q in zip(total, differ)])
 
@@ -622,13 +634,14 @@
     r1 = product(restrict_wall(R3, 3, 1, [r3[k] for k in range(3)]), r3_ref)[0]
 
     start, steps = cheb_steps(LOW.bound, COARSE_STEPS, coarse_floor)
-    my1 = height(0) * d1_mix
-    u1 = start * (d1 * r1)
+    middle = d1 * (height(0) * d1_mix + g_pair)
+    after, before = d1 * g, d1 * roll_down(g)
+    r1 = d1 * r1
+    u1 = start * r1
     x1 = u1
     for alpha, beta in steps:
-        flow = g * (u1 - roll_up(u1))
-        r1 = r1 - (my1 * u1 + (flow - roll_down(flow)))
-        u1 = alpha * u1 + beta * (d1 * r1)
+        r1 = (r1 - middle * u1) + (after * roll_up(u1) + before * roll_down(u1))
+        u1 = alpha * u1 + beta * r1
         x1 = x1 + u1
 
     up = prolong_wall(J3, 3, 1, product([x1], p3_ref))

time: 87.8 us -> 87.6 us (level)
  no operation moved by 1% of the time
where the time goes in v6:
time: 87.6 us; the launch traced here: 87.3 us
  blocking collectives  80.8 us (92%)
  Pallas kernels  6.45 us (7%)
    all_to_all x6, blocking collectives, exchange(): return lax.all_to_all(block, axes, 0, 0).reshape(rows, 128)  80.8 us
    pallas_call x1, Pallas kernels, cycle_call(): pl.pallas_call(cycle_kernel, out_shape=FLAT, in_specs=[VMEM, VMEM, VMEM],...  3.84 us

profile of v6, /device:TPU:1, one launch (start us, length us, event | category | flops | bytes accessed | tf_op | source)
XLA Modules:
  0.0 87.3 jit_solution(16355520593889591465)
XLA Ops:
  0.0 1.1 %shard_map.37 = (f32[392,128]{1,0:T(8,128)S(1)}, f32[80,128]{1,0:T(8,128)S(1)}) custom-call(f32[7,14,512]{2,1,0:T(8,128)} %x_hbm.1, f32[1,73]{1,0:T(1,128)} %bitcast.25), custom_call_target="tpu_custom_call" | custom-call | tf_op jit(solution)/shard_map/pallas_call | solution.py:722
  1.1 11.6 %all_to_all.30 = f32[8,49,1,128]{3,2,1,0:T(1,128)S(1)} all-to-all(f32[8,49,1,128]{3,2,1,0:T(1,128)S(1)} %bitcast.24), channel_id=1, replica_groups=mesh['zh'=4,'z0'=2,'xh'=2,'core'=2,'xl'=2,'y'=4] {'xl','y'}, dimensions={0} | all-to-all | bytes 401408 | tf_op jit(solution)/shard_map/all_to_all | solution.py:692
  12.8 0.3 shard_map.38
  13.0 24.7 %all_to_all.31 = f32[32,13,1,128]{3,2,1,0:T(1,128)S(1)} all-to-all(f32[32,13,1,128]{3,2,1,0:T(1,128)S(1)} %bitcast.13), channel_id=1, replica_groups=mesh['zh'=4,'z0'=2,'xh'=2,'core'=2,'xl'=2,'y'=4] {'zh','z0','xh','core'}, dimensions={0} | all-to-all | bytes 425984 | tf_op jit(solution)/shard_map/all_to_all | solution.py:692
  37.7 0.0 copy-start
  37.7 0.1 shard_map.39
  37.8 9.8 %all_to_all.32 = f32[16,26,1,128]{3,2,1,0:T(1,128)S(1)} all-to-all(f32[16,26,1,128]{3,2,1,0:T(1,128)S(1)} %bitcast.18), channel_id=1, replica_groups=mesh['zh'=4,'z0'=2,'xh'=2,'core'=2,'xl'=2,'y'=4] {'xl','y','core'}, dimensions={0} | all-to-all | bytes 425984 | tf_op jit(solution)/shard_map/all_to_all | solution.py:692
  47.6 0.0 copy-done
  47.6 3.8 %shard_map.40 = f32[416,128]{1,0:T(8,128)S(1)} custom-call(f32[80,128]{1,0:T(8,128)S(1)} %get-tuple-element.7.h_ref, f32[728,128]{1,0:T(8,128)S(1)} %copy-done, f32[416,128]{1,0:T(8,128)S(1)} %bitcast.15), custom_call_target="tpu_custom_call" | custom-call | tf_op jit(solution)/shard_map/pallas_call | solution.py:699
  51.5 10.1 %all_to_all.33 = f32[16,26,1,128]{3,2,1,0:T(1,128)S(1)} all-to-all(f32[16,26,1,128]{3,2,1,0:T(1,128)S(1)} %bitcast.16), channel_id=1, replica_groups=mesh['zh'=4,'z0'=2,'xh'=2,'core'=2,'xl'=2,'y'=4] {'xl','y','core'}, dimensions={0} | all-to-all | bytes 425984 | tf_op jit(solution)/shard_map/all_to_all | solution.py:692
  61.6 0.1 shard_map.41
  61.7 16.3 %all_to_all.34 = f32[32,13,1,128]{3,2,1,0:T(1,128)S(1)} all-to-all(f32[32,13,1,128]{3,2,1,0:T(1,128)S(1)} %bitcast.20), channel_id=1, replica_groups=mesh['zh'=4,'z0'=2,'xh'=2,'core'=2,'xl'=2,'y'=4] {'zh','z0','xh','core'}, dimensions={0} | all-to-all | bytes 425984 | tf_op jit(solution)/shard_map/all_to_all | solution.py:692
  78.0 0.3 shard_map.42
  78.3 8.2 %all_to_all.35 = f32[8,49,1,128]{3,2,1,0:T(1,128)S(1)} all-to-all(f32[8,49,1,128]{3,2,1,0:T(1,128)S(1)} %bitcast.22), channel_id=1, replica_groups=mesh['zh'=4,'z0'=2,'xh'=2,'core'=2,'xl'=2,'y'=4] {'xl','y'}, dimensions={0} | all-to-all | bytes 401408 | tf_op jit(solution)/shard_map/all_to_all | solution.py:692
  86.5 0.8 shard_map.43
Async XLA Ops:
  37.7 9.9 %copy-start = (f32[728,128]{1,0:T(8,128)S(1)}, f32[728,128]{1,0:T(8,128)}, u32[]{:S(2)}) copy-start(f32[728,128]{1,0:T(8,128)} %constant.2.clone.mats_ref) | copy-start | bytes 1118212

commit v7 on v6

--- a/solution.py
+++ b/solution.py
@@ -214,7 +214,7 @@
 
 
 FLOW, SPAN = ("zh", "z0", "xh", "core"), ("xl", "y")
-LAST = ("xl", "y", "core")
+LAST = ("core", "xl", "y")
 USED = 8 * 49
 SLAB = 13
 FIELD = 32 * SLAB
@@ -562,7 +562,7 @@
     square[...] = jnp.zeros((128, 128), f32)
     for t in range(4):
         for y, half, part in PIECES:
-            r, v = 64 * part + 32 * y + 13 * half, 52 * (2 * t + y) + 26 * half + 13 * part
+            r, v = 64 * part + 32 * y + 13 * half, 208 * half + 26 * (2 * t + y) + 13 * part
             square[r : r + 13, :] = in_ref[v : v + 13, :]
         both = square[...].T
         low, high = both[:64], both[64:]
@@ -674,7 +674,7 @@
             axis=0,
         ).T
         for y, half, part in PIECES:
-            r, v = 64 * part + 32 * y + 13 * half, 52 * (2 * t + y) + 26 * half + 13 * part
+            r, v = 64 * part + 32 * y + 13 * half, 208 * half + 26 * (2 * t + y) + 13 * part
             out_ref[v : v + 13, :] = square[r : r + 13, :]
 
 

time: 87.6 us -> 87.6 us (level)
  no operation moved by 1% of the time
where the time goes in v7:
time: 87.6 us; the launch traced here: 87.3 us
  blocking collectives  80.8 us (92%)
  Pallas kernels  6.45 us (7%)
    all_to_all x6, blocking collectives, exchange(): return lax.all_to_all(block, axes, 0, 0).reshape(rows, 128)  80.8 us
    pallas_call x1, Pallas kernels, cycle_call(): pl.pallas_call(cycle_kernel, out_shape=FLAT, in_specs=[VMEM, VMEM, VMEM],...  3.83 us

profile of v7, /device:TPU:1, one launch (start us, length us, event | category | flops | bytes accessed | tf_op | source)
XLA Modules:
  0.0 87.3 jit_solution(12253466996820463356)
XLA Ops:
  0.0 1.1 %shard_map.37 = (f32[392,128]{1,0:T(8,128)S(1)}, f32[80,128]{1,0:T(8,128)S(1)}) custom-call(f32[7,14,512]{2,1,0:T(8,128)} %x_hbm.1, f32[1,73]{1,0:T(1,128)} %bitcast.25), custom_call_target="tpu_custom_call" | custom-call | tf_op jit(solution)/shard_map/pallas_call | solution.py:722
  1.1 11.6 %all_to_all.30 = f32[8,49,1,128]{3,2,1,0:T(1,128)S(1)} all-to-all(f32[8,49,1,128]{3,2,1,0:T(1,128)S(1)} %bitcast.24), channel_id=1, replica_groups=mesh['zh'=4,'z0'=2,'xh'=2,'core'=2,'xl'=2,'y'=4] {'xl','y'}, dimensions={0} | all-to-all | bytes 401408 | tf_op jit(solution)/shard_map/all_to_all | solution.py:692
  12.8 0.3 shard_map.38
  13.0 24.7 %all_to_all.31 = f32[32,13,1,128]{3,2,1,0:T(1,128)S(1)} all-to-all(f32[32,13,1,128]{3,2,1,0:T(1,128)S(1)} %bitcast.13), channel_id=1, replica_groups=mesh['zh'=4,'z0'=2,'xh'=2,'core'=2,'xl'=2,'y'=4] {'zh','z0','xh','core'}, dimensions={0} | all-to-all | bytes 425984 | tf_op jit(solution)/shard_map/all_to_all | solution.py:692
  37.7 0.0 copy-start
  37.7 0.1 shard_map.39
  37.8 10.2 %all_to_all.32 = f32[16,26,1,128]{3,2,1,0:T(1,128)S(1)} all-to-all(f32[16,26,1,128]{3,2,1,0:T(1,128)S(1)} %bitcast.18), channel_id=1, replica_groups=mesh['zh'=4,'z0'=2,'xh'=2,'core'=2,'xl'=2,'y'=4] {'core','xl','y'}, dimensions={0} | all-to-all | bytes 425984 | tf_op jit(solution)/shard_map/all_to_all | solution.py:692
  48.0 0.0 copy-done
  48.0 3.8 %shard_map.40 = f32[416,128]{1,0:T(8,128)S(1)} custom-call(f32[80,128]{1,0:T(8,128)S(1)} %get-tuple-element.7.h_ref, f32[728,128]{1,0:T(8,128)S(1)} %copy-done, f32[416,128]{1,0:T(8,128)S(1)} %bitcast.15), custom_call_target="tpu_custom_call" | custom-call | tf_op jit(solution)/shard_map/pallas_call | solution.py:699
  51.9 10.2 %all_to_all.33 = f32[16,26,1,128]{3,2,1,0:T(1,128)S(1)} all-to-all(f32[16,26,1,128]{3,2,1,0:T(1,128)S(1)} %bitcast.16), channel_id=1, replica_groups=mesh['zh'=4,'z0'=2,'xh'=2,'core'=2,'xl'=2,'y'=4] {'core','xl','y'}, dimensions={0} | all-to-all | bytes 425984 | tf_op jit(solution)/shard_map/all_to_all | solution.py:692
  62.0 0.1 shard_map.41
  62.1 15.7 %all_to_all.34 = f32[32,13,1,128]{3,2,1,0:T(1,128)S(1)} all-to-all(f32[32,13,1,128]{3,2,1,0:T(1,128)S(1)} %bitcast.20), channel_id=1, replica_groups=mesh['zh'=4,'z0'=2,'xh'=2,'core'=2,'xl'=2,'y'=4] {'zh','z0','xh','core'}, dimensions={0} | all-to-all | bytes 425984 | tf_op jit(solution)/shard_map/all_to_all | solution.py:692
  77.9 0.3 shard_map.42
  78.1 8.3 %all_to_all.35 = f32[8,49,1,128]{3,2,1,0:T(1,128)S(1)} all-to-all(f32[8,49,1,128]{3,2,1,0:T(1,128)S(1)} %bitcast.22), channel_id=1, replica_groups=mesh['zh'=4,'z0'=2,'xh'=2,'core'=2,'xl'=2,'y'=4] {'xl','y'}, dimensions={0} | all-to-all | bytes 401408 | tf_op jit(solution)/shard_map/all_to_all | solution.py:692
  86.5 0.8 shard_map.43
Async XLA Ops:
  37.7 10.3 %copy-start = (f32[728,128]{1,0:T(8,128)S(1)}, f32[728,128]{1,0:T(8,128)}, u32[]{:S(2)}) copy-start(f32[728,128]{1,0:T(8,128)} %constant.2.clone.mats_ref) | copy-start | bytes 1118212

commit v8 on v6

--- a/solution.py
+++ b/solution.py
@@ -466,8 +466,8 @@
     return pltpu.roll(v, 1, axis=0)
 
 
-def wall_apply(s, q, planes, g):
-    parts = [g * p for p in planes] + [g * roll_up(planes[0])]
+def element_products(s, q, planes):
+    parts = list(planes) + [roll_up(planes[0])]
     n = q + 1
     half = n // 2
     even = [parts[l] + parts[q - l] for l in range(half)]
@@ -483,8 +483,7 @@
             m = to if m is None else m + to
         out[k] = p + m
         out[q - k] = p - m
-    out[0] = out[0] + roll_down(out[q])
-    return out[:q]
+    return out
 
 
 def weighted_sum(coefs, planes):
@@ -498,9 +497,10 @@
     return total
 
 
-def restrict_wall(j, fine, coarse, planes):
-    out = [weighted_sum(j[:fine, c], planes) for c in range(coarse)]
-    out[0] = out[0] + roll_down(weighted_sum(j[:fine, coarse], planes))
+def restrict_wall(j, fine, coarse, planes, h, inv_pair):
+    out = [weighted_sum(j[1:fine, c], planes[1:]) for c in range(coarse)]
+    shared = h * out[0] + roll_down(h * weighted_sum(j[1:fine, coarse], planes[1:]))
+    out[0] = float(j[0, 0]) * planes[0] + inv_pair * shared
     return out
 
 
@@ -569,51 +569,60 @@
         w_ref[128 * t : 128 * t + 64, :] = jnp.where(outer, low, pltpu.roll(high, 32, axis=1)) * scale
         w_ref[128 * t + 64 : 128 * t + 128, :] = jnp.where(outer, pltpu.roll(low, 96, axis=1), high) * scale
     w_ref[512:, :] = jnp.zeros((w_ref.shape[0] - 512, 128), f32)
-    for k in range(7):
-        r7[k] = float(1.0 / FINE.weight[k]) * w_ref[pl.ds(k, ROWS, stride=7), :]
-
     h = h_ref[...]
     row = lax.broadcasted_iota(jnp.int32, (ROWS, 128), 0)
-    g = jnp.where(row < NY, 2.0 / jnp.where(row < NY, h, 1.0), 0.0)
+    inv = jnp.where(row < NY, 1.0 / jnp.where(row < NY, h, 1.0), 0.0)
+    g = 2.0 * inv
     h_pair = h + roll_down(h)
     g_pair = g + roll_down(g)
+    inv_pair = jnp.where(row <= NY, 1.0 / jnp.where(row <= NY, h_pair, 1.0), 0.0)
     geo_ref[0] = h
     geo_ref[1] = g
-    geo_ref[2] = h_pair
-
-    def height(k):
-        return geo_ref[0 if k else 2]
-
-    def inverse_diag(level, ratio, mask, k):
-        d = height(k) * ratio + float(level.stiff[k, k]) * (g if k else g_pair)
-        return jnp.where(d > 0.0, mask / jnp.where(d > 0.0, d, 1.0), 0.0)
+    geo_ref[2] = inv_pair
+    geo_ref[3] = g * inv
+
+    def inverse_diags(d, level, ratio, mask):
+        start, steps = cheb_steps(level.bound, SMOOTH_STEPS, smooth_floor)
+        for k in range(level.q):
+            wall = geo_ref[3] if k else g_pair * inv_pair
+            total = ratio + float(level.stiff[k, k]) * wall
+            used = (row < NY if k else row <= NY) & (mask > 0.0)
+            total = jnp.where(used, 1.0 / jnp.where(used, total, 1.0), 0.0)
+            for n, factor in enumerate([start] + [beta for _, beta in steps]):
+                d[n, k] = factor * total
+
+    inverse_diags(d7, FINE, ratio7, mask7)
+    inverse_diags(d3, MID, ratio3, mask3)
+    d1_mix = (4.0 + screen_shift) - 2.0 * cx - 2.0 * cz
+    d1 = h_pair * (4.0 + screen_shift) + g_pair
+    used = (row <= NY) & (mask1 > 0.0)
+    d1 = jnp.where(used, 1.0 / jnp.where(used, d1, 1.0), 0.0)
 
     for k in range(7):
-        d7[k] = inverse_diag(FINE, ratio7, mask7, k)
-    for k in range(3):
-        d3[k] = inverse_diag(MID, ratio3, mask3, k)
-    d1_mix = ((4.0 + screen_shift) - 2.0 * cx - 2.0 * cz) * mask1
-    d1 = inverse_diag(LOW, 4.0 + screen_shift, mask1, 0)
+        factor = float(1.0 / FINE.weight[k]) * (inv if k else inv_pair)
+        r7[k] = factor * w_ref[pl.ds(k, ROWS, stride=7), :]
 
     def apply(level, u, table):
         q = level.q
         m = table_product(u[...].reshape(q * ROWS, 128), table)
-        wall = wall_apply(level.stiff, q, [u[k] for k in range(q)], geo_ref[1])
-        return [height(k) * m[k * ROWS : (k + 1) * ROWS] + wall[k] for k in range(q)]
+        wall = element_products(level.stiff, q, [u[k] for k in range(q)])
+        shared = geo_ref[1] * wall[0] + roll_down(geo_ref[1] * wall[q])
+        out = [m[:ROWS] + geo_ref[2] * shared]
+        return out + [m[k * ROWS : (k + 1) * ROWS] + geo_ref[3] * wall[k] for k in range(1, q)]
 
     def smooth(level, u, r, x, d, table, fresh, keep_residual):
         q = level.q
-        start, steps = cheb_steps(level.bound, SMOOTH_STEPS, smooth_floor)
+        steps = cheb_steps(level.bound, SMOOTH_STEPS, smooth_floor)[1]
         for k in range(q):
-            t = start * (d[k] * r[k])
+            t = d[0, k] * r[k]
             u[k] = t
             x[k] = t if fresh else x[k] + t
-        for alpha, beta in steps:
+        for n, (alpha, _) in enumerate(steps):
             au = apply(level, u, table)
             for k in range(q):
                 t = r[k] - au[k]
                 r[k] = t
-                t = alpha * u[k] + beta * (d[k] * t)
+                t = alpha * u[k] + d[n + 1, k] * t
                 u[k] = t
                 x[k] = x[k] + t
         if keep_residual:
@@ -626,17 +635,17 @@
         return [m[k * ROWS : (k + 1) * ROWS] for k in range(len(planes))]
 
     smooth(FINE, u7, r7, x7, d7, g7_ref, True, True)
-    down = product(restrict_wall(R7, 7, 3, [r7[k] for k in range(7)]), r7_ref)
+    down = product(restrict_wall(R7, 7, 3, [r7[k] for k in range(7)], geo_ref[0], geo_ref[2]), r7_ref)
     for k in range(3):
         r3[k] = down[k]
 
     smooth(MID, u3, r3, x3, d3, g3_ref, True, True)
-    r1 = product(restrict_wall(R3, 3, 1, [r3[k] for k in range(3)]), r3_ref)[0]
+    r1 = product(restrict_wall(R3, 3, 1, [r3[k] for k in range(3)], geo_ref[0], geo_ref[2]), r3_ref)[0]
 
     start, steps = cheb_steps(LOW.bound, COARSE_STEPS, coarse_floor)
-    middle = d1 * (height(0) * d1_mix + g_pair)
+    middle = d1 * (h_pair * d1_mix + g_pair)
     after, before = d1 * g, d1 * roll_down(g)
-    r1 = d1 * r1
+    r1 = (d1 * h_pair) * r1
     u1 = start * r1
     x1 = u1
     for alpha, beta in steps:
@@ -700,8 +709,9 @@
         cycle_kernel, out_shape=FLAT,
         in_specs=[VMEM, VMEM, VMEM], out_specs=VMEM,
         scratch_shapes=[
-            pltpu.VMEM((7 * ROWS, 128), f32), mid,
-            fine, fine, fine, fine, mid, mid, mid, mid,
+            pltpu.VMEM((7 * ROWS, 128), f32), pltpu.VMEM((4, ROWS, 128), f32),
+            fine, fine, fine, pltpu.VMEM((SMOOTH_STEPS, 7, ROWS, 128), f32),
+            mid, mid, mid, pltpu.VMEM((SMOOTH_STEPS, 3, ROWS, 128), f32),
             pltpu.VMEM((128, 128), f32), table, table, table, table, table, table,
         ],
         compiler_params=PARAMS,

time: 87.6 us -> 87.5 us (level)
  no operation moved by 1% of the time
where the time goes in v8:
time: 87.5 us; the launch traced here: 87.1 us
  blocking collectives  80.8 us (92%)
  Pallas kernels  6.29 us (7%)
    all_to_all x6, blocking collectives, exchange(): return lax.all_to_all(block, axes, 0, 0).reshape(rows, 128)  80.8 us
    pallas_call x1, Pallas kernels, cycle_call(): pl.pallas_call(cycle_kernel, out_shape=FLAT, in_specs=[VMEM, VMEM, VMEM],...  3.67 us

profile of v8, /device:TPU:1, one launch (start us, length us, event | category | flops | bytes accessed | tf_op | source)
XLA Modules:
  0.0 87.1 jit_solution(13815836366487499209)
XLA Ops:
  0.0 1.1 %shard_map.37 = (f32[392,128]{1,0:T(8,128)S(1)}, f32[80,128]{1,0:T(8,128)S(1)}) custom-call(f32[7,14,512]{2,1,0:T(8,128)} %x_hbm.1, f32[1,73]{1,0:T(1,128)} %bitcast.25), custom_call_target="tpu_custom_call" | custom-call | tf_op jit(solution)/shard_map/pallas_call | solution.py:732
  1.1 11.6 %all_to_all.30 = f32[8,49,1,128]{3,2,1,0:T(1,128)S(1)} all-to-all(f32[8,49,1,128]{3,2,1,0:T(1,128)S(1)} %bitcast.24), channel_id=1, replica_groups=mesh['zh'=4,'z0'=2,'xh'=2,'core'=2,'xl'=2,'y'=4] {'xl','y'}, dimensions={0} | all-to-all | bytes 401408 | tf_op jit(solution)/shard_map/all_to_all | solution.py:701
  12.8 0.3 shard_map.38
  13.0 24.7 %all_to_all.31 = f32[32,13,1,128]{3,2,1,0:T(1,128)S(1)} all-to-all(f32[32,13,1,128]{3,2,1,0:T(1,128)S(1)} %bitcast.13), channel_id=1, replica_groups=mesh['zh'=4,'z0'=2,'xh'=2,'core'=2,'xl'=2,'y'=4] {'zh','z0','xh','core'}, dimensions={0} | all-to-all | bytes 425984 | tf_op jit(solution)/shard_map/all_to_all | solution.py:701
  37.7 0.0 copy-start
  37.7 0.1 shard_map.39
  37.8 9.8 %all_to_all.32 = f32[16,26,1,128]{3,2,1,0:T(1,128)S(1)} all-to-all(f32[16,26,1,128]{3,2,1,0:T(1,128)S(1)} %bitcast.18), channel_id=1, replica_groups=mesh['zh'=4,'z0'=2,'xh'=2,'core'=2,'xl'=2,'y'=4] {'xl','y','core'}, dimensions={0} | all-to-all | bytes 425984 | tf_op jit(solution)/shard_map/all_to_all | solution.py:701
  47.6 0.0 copy-done
  47.6 3.7 %shard_map.40 = f32[416,128]{1,0:T(8,128)S(1)} custom-call(f32[80,128]{1,0:T(8,128)S(1)} %get-tuple-element.7.h_ref, f32[728,128]{1,0:T(8,128)S(1)} %copy-done, f32[416,128]{1,0:T(8,128)S(1)} %bitcast.15), custom_call_target="tpu_custom_call" | custom-call | tf_op jit(solution)/shard_map/pallas_call | solution.py:708
  51.3 10.1 %all_to_all.33 = f32[16,26,1,128]{3,2,1,0:T(1,128)S(1)} all-to-all(f32[16,26,1,128]{3,2,1,0:T(1,128)S(1)} %bitcast.16), channel_id=1, replica_groups=mesh['zh'=4,'z0'=2,'xh'=2,'core'=2,'xl'=2,'y'=4] {'xl','y','core'}, dimensions={0} | all-to-all | bytes 425984 | tf_op jit(solution)/shard_map/all_to_all | solution.py:701
  61.4 0.1 shard_map.41
  61.5 16.3 %all_to_all.34 = f32[32,13,1,128]{3,2,1,0:T(1,128)S(1)} all-to-all(f32[32,13,1,128]{3,2,1,0:T(1,128)S(1)} %bitcast.20), channel_id=1, replica_groups=mesh['zh'=4,'z0'=2,'xh'=2,'core'=2,'xl'=2,'y'=4] {'zh','z0','xh','core'}, dimensions={0} | all-to-all | bytes 425984 | tf_op jit(solution)/shard_map/all_to_all | solution.py:701
  77.8 0.3 shard_map.42
  78.1 8.2 %all_to_all.35 = f32[8,49,1,128]{3,2,1,0:T(1,128)S(1)} all-to-all(f32[8,49,1,128]{3,2,1,0:T(1,128)S(1)} %bitcast.22), channel_id=1, replica_groups=mesh['zh'=4,'z0'=2,'xh'=2,'core'=2,'xl'=2,'y'=4] {'xl','y'}, dimensions={0} | all-to-all | bytes 401408 | tf_op jit(solution)/shard_map/all_to_all | solution.py:701
  86.3 0.8 shard_map.43
Async XLA Ops:
  37.7 9.9 %copy-start = (f32[728,128]{1,0:T(8,128)S(1)}, f32[728,128]{1,0:T(8,128)}, u32[]{:S(2)}) copy-start(f32[728,128]{1,0:T(8,128)} %constant.2.clone.mats_ref) | copy-start | bytes 1118212

commit v9 on v8

--- a/solution.py
+++ b/solution.py
@@ -214,7 +214,7 @@
 
 
 FLOW, SPAN = ("zh", "z0", "xh", "core"), ("xl", "y")
-LAST = ("xl", "y", "core")
+LAST = ("core", "xl", "y")
 USED = 8 * 49
 SLAB = 13
 FIELD = 32 * SLAB
@@ -562,7 +562,7 @@
     square[...] = jnp.zeros((128, 128), f32)
     for t in range(4):
         for y, half, part in PIECES:
-            r, v = 64 * part + 32 * y + 13 * half, 52 * (2 * t + y) + 26 * half + 13 * part
+            r, v = 64 * part + 32 * y + 13 * half, 208 * half + 26 * (2 * t + y) + 13 * part
             square[r : r + 13, :] = in_ref[v : v + 13, :]
         both = square[...].T
         low, high = both[:64], both[64:]
@@ -683,7 +683,7 @@
             axis=0,
         ).T
         for y, half, part in PIECES:
-            r, v = 64 * part + 32 * y + 13 * half, 52 * (2 * t + y) + 26 * half + 13 * part
+            r, v = 64 * part + 32 * y + 13 * half, 208 * half + 26 * (2 * t + y) + 13 * part
             out_ref[v : v + 13, :] = square[r : r + 13, :]
 
 

time: 87.5 us -> 87.4 us (level)
  no operation moved by 1% of the time
where the time goes in v9:
time: 87.4 us; the launch traced here: 87.1 us
  blocking collectives  80.8 us (92%)
  Pallas kernels  6.28 us (7%)
    all_to_all x6, blocking collectives, exchange(): return lax.all_to_all(block, axes, 0, 0).reshape(rows, 128)  80.8 us
    pallas_call x1, Pallas kernels, cycle_call(): pl.pallas_call(cycle_kernel, out_shape=FLAT, in_specs=[VMEM, VMEM, VMEM],...  3.67 us

profile of v9, /device:TPU:1, one launch (start us, length us, event | category | flops | bytes accessed | tf_op | source)
XLA Modules:
  0.0 87.1 jit_solution(13121093124268679294)
XLA Ops:
  0.0 1.1 %shard_map.37 = (f32[392,128]{1,0:T(8,128)S(1)}, f32[80,128]{1,0:T(8,128)S(1)}) custom-call(f32[7,14,512]{2,1,0:T(8,128)} %x_hbm.1, f32[1,73]{1,0:T(1,128)} %bitcast.25), custom_call_target="tpu_custom_call" | custom-call | tf_op jit(solution)/shard_map/pallas_call | solution.py:732
  1.1 11.6 %all_to_all.30 = f32[8,49,1,128]{3,2,1,0:T(1,128)S(1)} all-to-all(f32[8,49,1,128]{3,2,1,0:T(1,128)S(1)} %bitcast.24), channel_id=1, replica_groups=mesh['zh'=4,'z0'=2,'xh'=2,'core'=2,'xl'=2,'y'=4] {'xl','y'}, dimensions={0} | all-to-all | bytes 401408 | tf_op jit(solution)/shard_map/all_to_all | solution.py:701
  12.8 0.3 shard_map.38
  13.0 24.7 %all_to_all.31 = f32[32,13,1,128]{3,2,1,0:T(1,128)S(1)} all-to-all(f32[32,13,1,128]{3,2,1,0:T(1,128)S(1)} %bitcast.13), channel_id=1, replica_groups=mesh['zh'=4,'z0'=2,'xh'=2,'core'=2,'xl'=2,'y'=4] {'zh','z0','xh','core'}, dimensions={0} | all-to-all | bytes 425984 | tf_op jit(solution)/shard_map/all_to_all | solution.py:701
  37.7 0.0 copy-start
  37.7 0.1 shard_map.39
  37.8 10.2 %all_to_all.32 = f32[16,26,1,128]{3,2,1,0:T(1,128)S(1)} all-to-all(f32[16,26,1,128]{3,2,1,0:T(1,128)S(1)} %bitcast.18), channel_id=1, replica_groups=mesh['zh'=4,'z0'=2,'xh'=2,'core'=2,'xl'=2,'y'=4] {'core','xl','y'}, dimensions={0} | all-to-all | bytes 425984 | tf_op jit(solution)/shard_map/all_to_all | solution.py:701
  48.0 0.0 copy-done
  48.0 3.7 %shard_map.40 = f32[416,128]{1,0:T(8,128)S(1)} custom-call(f32[80,128]{1,0:T(8,128)S(1)} %get-tuple-element.7.h_ref, f32[728,128]{1,0:T(8,128)S(1)} %copy-done, f32[416,128]{1,0:T(8,128)S(1)} %bitcast.15), custom_call_target="tpu_custom_call" | custom-call | tf_op jit(solution)/shard_map/pallas_call | solution.py:708
  51.7 10.2 %all_to_all.33 = f32[16,26,1,128]{3,2,1,0:T(1,128)S(1)} all-to-all(f32[16,26,1,128]{3,2,1,0:T(1,128)S(1)} %bitcast.16), channel_id=1, replica_groups=mesh['zh'=4,'z0'=2,'xh'=2,'core'=2,'xl'=2,'y'=4] {'core','xl','y'}, dimensions={0} | all-to-all | bytes 425984 | tf_op jit(solution)/shard_map/all_to_all | solution.py:701
  61.9 0.1 shard_map.41
  62.0 15.7 %all_to_all.34 = f32[32,13,1,128]{3,2,1,0:T(1,128)S(1)} all-to-all(f32[32,13,1,128]{3,2,1,0:T(1,128)S(1)} %bitcast.20), channel_id=1, replica_groups=mesh['zh'=4,'z0'=2,'xh'=2,'core'=2,'xl'=2,'y'=4] {'zh','z0','xh','core'}, dimensions={0} | all-to-all | bytes 425984 | tf_op jit(solution)/shard_map/all_to_all | solution.py:701
  77.7 0.3 shard_map.42
  78.0 8.3 %all_to_all.35 = f32[8,49,1,128]{3,2,1,0:T(1,128)S(1)} all-to-all(f32[8,49,1,128]{3,2,1,0:T(1,128)S(1)} %bitcast.22), channel_id=1, replica_groups=mesh['zh'=4,'z0'=2,'xh'=2,'core'=2,'xl'=2,'y'=4] {'xl','y'}, dimensions={0} | all-to-all | bytes 401408 | tf_op jit(solution)/shard_map/all_to_all | solution.py:701
  86.3 0.8 shard_map.43
Async XLA Ops:
  37.7 10.3 %copy-start = (f32[728,128]{1,0:T(8,128)S(1)}, f32[728,128]{1,0:T(8,128)}, u32[]{:S(2)}) copy-start(f32[728,128]{1,0:T(8,128)} %constant.2.clone.mats_ref) | copy-start | bytes 1118212

commit v10 on v9

--- a/solution.py
+++ b/solution.py
@@ -339,8 +339,16 @@
     return [c[0]] + [c[j] - s[j] for j in (1, 2, 3)] + [c[4]] + [c[j] + s[j] for j in (3, 2, 1)]
 
 
-def mode_rows(k, part):
-    return 26 * (4 * (k // 2) + 2 * part + k % 2)
+ORDER = ("core", "zh", "z0", "xh")
+
+
+def flow_place(n):
+    return n % 2 * 16 + n // 2
+
+
+def mode_rows(k, part, half):
+    at = SLAB * (16 * half + 4 * (k // 2) + 2 * part + k % 2)
+    return slice(at, at + SLAB)
 
 
 def span_forward_kernel(x_ref, o_ref, v_ref):
@@ -360,20 +368,18 @@
             v_ref[k, 7 * (7 - b) : 7 * (7 - b) + 7] = differ[k]
     for k in range(8):
         re, im = mix(first, v_ref[k, 0:26], v_ref[k, 25:51])
-        o_ref[mode_rows(k, 0) : mode_rows(k, 0) + 26, :] = re
-        o_ref[mode_rows(k, 1) : mode_rows(k, 1) + 26, :] = im
+        for part, v in enumerate((re, im)):
+            o_ref[mode_rows(k, part, 0), :] = v[:SLAB]
+            o_ref[mode_rows(k, part, 1), :] = v[SLAB:]
 
 
 def span_backward_kernel(x_ref, o_ref, v_ref):
     first, sign = lane_tools()
     for k in range(8):
-        near, far = mix(
-            first,
-            x_ref[mode_rows(k, 0) : mode_rows(k, 0) + 26, :],
-            x_ref[mode_rows(k, 1) : mode_rows(k, 1) + 26, :],
-        )
-        v_ref[k, 0:25] = near[0:25]
-        v_ref[k, 25:49] = far[0:24]
+        for half, rows in ((0, 13), (1, 12)):
+            near, far = mix(first, x_ref[mode_rows(k, 0, half), :], x_ref[mode_rows(k, 1, half), :])
+            v_ref[k, 13 * half : 13 * half + rows] = near[:rows]
+            v_ref[k, 25 + 13 * half : 37 + 12 * half + (1 - half)] = far[: 13 - 2 * half]
 
     def store(b, planes):
         for j, v in enumerate(planes):
@@ -431,7 +437,7 @@
 
 
 def flow_forward_kernel(x_ref, o_ref):
-    modes = line_modes([slab(x_ref, n) for n in range(NX)])
+    modes = line_modes([slab(x_ref, flow_place(n)) for n in range(NX)])
     for n in range(16):
         re, im = modes[n][0], modes[n][1] if n else modes[16][0]
         o_ref[26 * n : 26 * n + 13, :] = re
@@ -442,7 +448,8 @@
     modes = [(slab(x_ref, 2 * n), slab(x_ref, 2 * n + 1)) for n in range(16)]
     modes = [(modes[0][0], None)] + modes[1:] + [(modes[0][1], None)]
     for n, v in enumerate(line_elements(modes, NX)):
-        o_ref[n * SLAB : n * SLAB + SLAB, :] = v
+        at = SLAB * flow_place(n)
+        o_ref[at : at + SLAB, :] = v
 
 
 def table_product(v, t_ref):
@@ -739,9 +746,9 @@
         compiler_params=PARAMS,
     )(stay(residual), stay(layer_heights.reshape(1, NY)))
     spans = transform(span_forward_kernel, exchange(packed, SPAN), scratch=LINES)
-    modes = exchange(transform(flow_forward_kernel, exchange(spans, FLOW)), LAST)
+    modes = exchange(transform(flow_forward_kernel, exchange(spans, ORDER)), LAST)
     solved = exchange(cycle_call(heights, modes), LAST)
-    flows = exchange(transform(flow_backward_kernel, solved), FLOW)
+    flows = exchange(transform(flow_backward_kernel, solved), ORDER)
     spread = exchange(transform(span_backward_kernel, flows, TIGHT, LINES), SPAN)
     return pl.pallas_call(
         unpack_kernel, out_shape=jax.ShapeDtypeStruct((7, 14, 512), f32),

time: 87.4 us -> 87.3 us (level); the launches traced: 87.1 us -> 86.1 us
  blocking collectives: 80.8 us -> 79.8 us
    all_to_all x6, blocking collectives: 80.8 us -> 79.8 us  [exchange(): return lax.all_to_all(block, axes, 0, 0).reshape(rows, 128)]
where the time goes in v10:
time: 87.3 us; the launch traced here: 86.1 us
  blocking collectives  79.8 us (91%)
  Pallas kernels  6.3 us (7%)
    all_to_all x6, blocking collectives, exchange(): return lax.all_to_all(block, axes, 0, 0).reshape(rows, 128)  79.8 us
    pallas_call x1, Pallas kernels, cycle_call(): pl.pallas_call(cycle_kernel, out_shape=FLAT, in_specs=[VMEM, VMEM, VMEM],...  3.67 us

profile of v10, /device:TPU:1, one launch (start us, length us, event | category | flops | bytes accessed | tf_op | source)
XLA Modules:
  0.0 86.1 jit_solution(9261475422699804993)
XLA Ops:
  0.0 1.1 %shard_map.37 = (f32[392,128]{1,0:T(8,128)S(1)}, f32[80,128]{1,0:T(8,128)S(1)}) custom-call(f32[7,14,512]{2,1,0:T(8,128)} %x_hbm.1, f32[1,73]{1,0:T(1,128)} %bitcast.25), custom_call_target="tpu_custom_call" | custom-call | tf_op jit(solution)/shard_map/pallas_call | solution.py:739
  1.1 11.6 %all_to_all.30 = f32[8,49,1,128]{3,2,1,0:T(1,128)S(1)} all-to-all(f32[8,49,1,128]{3,2,1,0:T(1,128)S(1)} %bitcast.24), channel_id=1, replica_groups=mesh['zh'=4,'z0'=2,'xh'=2,'core'=2,'xl'=2,'y'=4] {'xl','y'}, dimensions={0} | all-to-all | bytes 401408 | tf_op jit(solution)/shard_map/all_to_all | solution.py:708
  12.8 0.3 shard_map.38
  13.0 23.9 %all_to_all.31 = f32[32,13,1,128]{3,2,1,0:T(1,128)S(1)} all-to-all(f32[32,13,1,128]{3,2,1,0:T(1,128)S(1)} %bitcast.13), channel_id=1, replica_groups=mesh['zh'=4,'z0'=2,'xh'=2,'core'=2,'xl'=2,'y'=4] {'core','zh','z0','xh'}, dimensions={0} | all-to-all | bytes 425984 | tf_op jit(solution)/shard_map/all_to_all | solution.py:708
  36.9 0.0 copy-start
  36.9 0.1 shard_map.39
  37.0 11.3 %all_to_all.32 = f32[16,26,1,128]{3,2,1,0:T(1,128)S(1)} all-to-all(f32[16,26,1,128]{3,2,1,0:T(1,128)S(1)} %bitcast.18), channel_id=1, replica_groups=mesh['zh'=4,'z0'=2,'xh'=2,'core'=2,'xl'=2,'y'=4] {'core','xl','y'}, dimensions={0} | all-to-all | bytes 425984 | tf_op jit(solution)/shard_map/all_to_all | solution.py:708
  48.2 0.0 copy-done
  48.3 3.7 %shard_map.40 = f32[416,128]{1,0:T(8,128)S(1)} custom-call(f32[80,128]{1,0:T(8,128)S(1)} %get-tuple-element.7.h_ref, f32[728,128]{1,0:T(8,128)S(1)} %copy-done, f32[416,128]{1,0:T(8,128)S(1)} %bitcast.15), custom_call_target="tpu_custom_call" | custom-call | tf_op jit(solution)/shard_map/pallas_call | solution.py:715
  51.9 10.2 %all_to_all.33 = f32[16,26,1,128]{3,2,1,0:T(1,128)S(1)} all-to-all(f32[16,26,1,128]{3,2,1,0:T(1,128)S(1)} %bitcast.16), channel_id=1, replica_groups=mesh['zh'=4,'z0'=2,'xh'=2,'core'=2,'xl'=2,'y'=4] {'core','xl','y'}, dimensions={0} | all-to-all | bytes 425984 | tf_op jit(solution)/shard_map/all_to_all | solution.py:708
  62.1 0.1 shard_map.41
  62.2 14.7 %all_to_all.34 = f32[32,13,1,128]{3,2,1,0:T(1,128)S(1)} all-to-all(f32[32,13,1,128]{3,2,1,0:T(1,128)S(1)} %bitcast.20), channel_id=1, replica_groups=mesh['zh'=4,'z0'=2,'xh'=2,'core'=2,'xl'=2,'y'=4] {'core','zh','z0','xh'}, dimensions={0} | all-to-all | bytes 425984 | tf_op jit(solution)/shard_map/all_to_all | solution.py:708
  76.8 0.3 shard_map.42
  77.1 8.2 %all_to_all.35 = f32[8,49,1,128]{3,2,1,0:T(1,128)S(1)} all-to-all(f32[8,49,1,128]{3,2,1,0:T(1,128)S(1)} %bitcast.22), channel_id=1, replica_groups=mesh['zh'=4,'z0'=2,'xh'=2,'core'=2,'xl'=2,'y'=4] {'xl','y'}, dimensions={0} | all-to-all | bytes 401408 | tf_op jit(solution)/shard_map/all_to_all | solution.py:708
  85.3 0.8 shard_map.43
Async XLA Ops:
  36.9 11.4 %copy-start = (f32[728,128]{1,0:T(8,128)S(1)}, f32[728,128]{1,0:T(8,128)}, u32[]{:S(2)}) copy-start(f32[728,128]{1,0:T(8,128)} %constant.2.clone.mats_ref) | copy-start | bytes 1118212
